TPU v7x, 32 devices: a whole 2x2x4 slice. The times are simulated.
32 devices in a mesh: dp: 4 (over y, core), seq: 8 (over z, x).
Axes of the slice: x: 2, y: 2, z: 4, core: 2. Of those that a mesh axis runs over, the one named last changes fastest.
Arguments:
- stream_one: bfloat16 [8, 1024, 1024], P('dp', 'seq'), may hold values from -6 to 6
- stream_two: bfloat16 [8, 1024, 1024], P('dp', 'seq'), may hold values from -6 to 6
- slot_place: int32 [8, 4, 1024], P('dp', None, 'seq'), may hold values from 0 to 1535, as said below
- bucket_ids: int32 [8, 4, 1024], P('dp', None, 'seq'), may hold values from 0 to 23, as said below
- grad_one: bfloat16 [8, 1024, 1024], P('dp', 'seq'), may hold values from -6 to 6
- grad_two: bfloat16 [8, 1024, 1024], P('dp', 'seq'), may hold values from -6 to 6
- norm1_gain: bfloat16 [1024], P(('dp', 'seq')), may hold values from 0.5 to 1.5
- norm1_bias: bfloat16 [1024], P(('dp', 'seq')), may hold values from -1 to 1
- w_query_key: bfloat16 [1024, 1024], P(('dp', 'seq')), may hold values from -3 to 3
- w_value: bfloat16 [1024, 1024], P(('dp', 'seq')), may hold values from -0.1875 to 0.1875
- w_output: bfloat16 [1024, 1024], P(('dp', 'seq')), may hold values from -1.5 to 1.5
- norm2_gain: bfloat16 [1024], P(('dp', 'seq')), may hold values from 0.5 to 1.5
- norm2_bias: bfloat16 [1024], P(('dp', 'seq')), may hold values from -1 to 1
- w_inner: bfloat16 [1024, 4096], P(('dp', 'seq')), may hold values from -0.1875 to 0.1875
- inner_bias: bfloat16 [4096], P(('dp', 'seq')), may hold values from -3 to 3
- w_outer: bfloat16 [4096, 1024], P(('dp', 'seq')), may hold values from -0.1875 to 0.1875
- outer_bias: bfloat16 [1024], P(('dp', 'seq')), may hold values from -3 to 3
Outputs:
- out_one: float32 [8, 1024, 1024], P('dp', 'seq')
- out_two: float32 [8, 1024, 1024], P('dp', 'seq')
- back_one: float32 [8, 1024, 1024], P('dp', 'seq')
- back_two: float32 [8, 1024, 1024], P('dp', 'seq')
- grad_norm1_gain: float32 [1024], P(('dp', 'seq'))
- grad_norm1_bias: float32 [1024], P(('dp', 'seq'))
- grad_query_key: float32 [1024, 1024], P(('dp', 'seq'))
- grad_value: float32 [1024, 1024], P(('dp', 'seq'))
- grad_output: float32 [1024, 1024], P(('dp', 'seq'))
- grad_norm2_gain: float32 [1024], P(('dp', 'seq'))
- grad_norm2_bias: float32 [1024], P(('dp', 'seq'))
- grad_inner: float32 [1024, 4096], P(('dp', 'seq'))
- grad_inner_bias: float32 [4096], P(('dp', 'seq'))
- grad_outer: float32 [4096, 1024], P(('dp', 'seq'))
- grad_outer_bias: float32 [1024], P(('dp', 'seq'))
Inputs may be any that keep to these rules, and one draw needn't show every extreme that they name: `slot_place`: within a sequence and round, the places of the 1024 tokens are distinct. Of the tokens k * 128 to (k + 1) * 128 - 1 of a sequence, at most 32 have places in any one block m * 192 to (m + 1) * 192 - 1 of a round, and some reach 32. `bucket_ids`: along a round's order of places, bucket ids never fall; a bucket takes whole spans of 64 places, its unused places being empty.
All inputs are finite; a program needn't handle non-finite values.
Results may differ from a plain program's by a relative error of at most 0.015.
Values may be sent and summed in bfloat16 or wider, within the bound.
No kernel may reach another device: no remote copies, remote signals or barrier semaphores. Data moves between devices by JAX's collectives and lax.ppermute only.
A program may use at most 320 MiB of HBM per device.

v0:
```python
import jax
import jax.numpy as jnp
from jax import lax
from jax.sharding import PartitionSpec as P

HEADS = 8
HEAD_DIM = 128
SPAN = 64


def for_sending(x):

    def short(part):
        return part.astype(jnp.bfloat16) if part.dtype == jnp.float32 else part

    return jax.tree.map(short, x)


def shifted(block, axis, distance):
    devices = range(lax.axis_size(axis))
    route = [(i - distance, i) for i in devices if i - distance in devices]
    return lax.ppermute(block, axis, route)


def matmul(left, right):
    return jnp.dot(left, right, preferred_element_type=jnp.float32)


def matmul_left(left, right):
    return lax.dot_general(
        left, right, (((0,), (0,)), ((), ())), preferred_element_type=jnp.float32
    )


def matmul_right(left, right):
    return lax.dot_general(
        left, right, (((1,), (1,)), ((), ())), preferred_element_type=jnp.float32
    )


def norm_parts(value, gain, bias):
    row_mean = jnp.mean(value, -1, keepdims=True)
    centred = value - row_mean
    inv_scale = lax.rsqrt(jnp.mean(centred * centred, -1, keepdims=True) + 1e-05)
    normal = centred * inv_scale
    return (normal * gain + bias, normal, inv_scale)


def norm_back(cotangent, normal, inv_scale, gain):
    d_normal = cotangent * gain
    d_input = inv_scale * (
        d_normal
        - jnp.mean(d_normal, -1, keepdims=True)
        - normal * jnp.mean(d_normal * normal, -1, keepdims=True)
    )
    return (d_input, jnp.sum(cotangent * normal, 0), jnp.sum(cotangent, 0))


def unit_keys(query_rows):
    return query_rows * lax.rsqrt(jnp.mean(query_rows * query_rows, -1, keepdims=True) + 1e-06)


def routing(slot_place, slot_total, capacity, seq_devices):
    target = slot_place // slot_total
    local_place = slot_place % slot_total
    matched = (target[..., None] == jnp.arange(seq_devices)).astype(jnp.int32)
    rank = jnp.sum((jnp.cumsum(matched, 2) - 1) * matched, -1)
    return (target * capacity + rank, local_place)


def scatter_rows(values, position, length):
    out_shape = position.shape[:2] + (length,) + values.shape[3:]
    first_idx = jnp.arange(position.shape[0])[:, None, None]
    second_idx = jnp.arange(position.shape[1])[None, :, None]
    return (
        jnp.zeros(out_shape, values.dtype)
        .at[first_idx, second_idx, position]
        .set(values, mode="drop")
    )


def pick_rows(source, position):
    first_idx = jnp.arange(position.shape[0])[:, None, None]
    second_idx = jnp.arange(position.shape[1])[None, :, None]
    return source[first_idx, second_idx, jnp.clip(position, 0, source.shape[2] - 1)]


def blocked(array):
    return array.reshape(array.shape[:2] + (array.shape[2] // SPAN, SPAN) + array.shape[3:])


def window(own, before):
    blocks = blocked(own)
    earlier = jnp.concatenate([before[:, :, None], blocks[:, :, :-1]], 2)
    return jnp.concatenate([earlier, blocks], 3)


def fold_window(grads):
    earlier = grads[:, :, :, :SPAN]
    own_part = grads[:, :, :, SPAN:]
    own_part = own_part + jnp.concatenate([earlier[:, :, 1:], jnp.zeros_like(earlier[:, :, :1])], 2)
    return (own_part, earlier[:, :, 0])


def masked_scores(query_rows, key_rows, query_tag, key_tag):
    raw_scores = jnp.einsum(
        "rcqhd,rckhd->rchqk", query_rows, key_rows, preferred_element_type=jnp.float32
    ) * (1.0 / HEAD_DIM)
    allowed = (key_tag[:, :, None, None, :] > 0) & (
        query_tag[:, :, None, :, None] == key_tag[:, :, None, None, :]
    )
    raw_scores = jnp.where(allowed, raw_scores, -1000000000.0)
    own_place = jnp.arange(2 * SPAN)[None, :] == jnp.arange(SPAN)[:, None] + SPAN
    return jnp.where(own_place, raw_scores - 100000.0, raw_scores)


def attend(items):
    query_rows, key_rows, value_rows, query_tag, key_tag = items
    scores = masked_scores(query_rows, key_rows, query_tag, key_tag)
    row_max = jnp.max(scores, -1, keepdims=True)
    exponent = jnp.exp(scores - row_max)
    row_sum = jnp.sum(exponent, -1, keepdims=True)
    probability = (exponent / row_sum).astype(jnp.bfloat16)
    result = jnp.einsum(
        "rchqk,rckhd->rcqhd", probability, value_rows, preferred_element_type=jnp.float32
    )
    spread = jnp.swapaxes((row_max + jnp.log(row_sum))[..., 0], 2, 3)
    return (result.astype(jnp.bfloat16), spread)


def attend_back(items):
    query_rows, key_rows, value_rows, query_tag, key_tag, spread, grad_out, grad_spread = items
    scores = masked_scores(query_rows, key_rows, query_tag, key_tag)
    probability = jnp.exp(scores - jnp.swapaxes(spread, 2, 3)[..., None])
    d_probs = jnp.einsum(
        "rcqhd,rckhd->rchqk", grad_out, value_rows, preferred_element_type=jnp.float32
    )
    row_dot = jnp.sum(probability * d_probs, -1, keepdims=True)
    d_scores = (
        probability * (d_probs - row_dot + jnp.swapaxes(grad_spread, 2, 3)[..., None])
    ).astype(jnp.bfloat16)
    d_query = jnp.einsum(
        "rchqk,rckhd->rcqhd", d_scores, key_rows, preferred_element_type=jnp.float32
    ) * (1.0 / HEAD_DIM)
    d_keys = jnp.einsum(
        "rchqk,rcqhd->rckhd", d_scores, query_rows, preferred_element_type=jnp.float32
    ) * (1.0 / HEAD_DIM)
    d_values = jnp.einsum(
        "rchqk,rcqhd->rckhd",
        probability.astype(jnp.bfloat16),
        grad_out,
        preferred_element_type=jnp.float32,
    )
    return (d_query, d_keys, d_values)


def local(
    stream_one,
    stream_two,
    slot_place,
    bucket_ids,
    grad_one,
    grad_two,
    norm1_gain,
    norm1_bias,
    w_query_key,
    w_value,
    w_output,
    norm2_gain,
    norm2_bias,
    w_inner,
    inner_bias,
    w_outer,
    outer_bias,
):
    batch_seqs, tok_count, features = stream_one.shape
    round_count = slot_place.shape[1]
    seq_devices = lax.axis_size("seq")
    capacity = 2 * tok_count // seq_devices
    slot_total = 3 * tok_count // 2
    lane_total = seq_devices * capacity
    row_total = batch_seqs * tok_count
    head_shape = (batch_seqs, round_count, slot_total, HEADS, HEAD_DIM)
    gain_one, bias_one, full_query_key, full_value, full_output = (
        lax.all_gather(norm1_gain, ("dp", "seq"), axis=0, tiled=True),
        lax.all_gather(norm1_bias, ("dp", "seq"), axis=0, tiled=True),
        lax.all_gather(w_query_key, ("dp", "seq"), axis=0, tiled=True),
        lax.all_gather(w_value, ("dp", "seq"), axis=0, tiled=True),
        lax.all_gather(w_output, ("dp", "seq"), axis=0, tiled=True),
    )
    gain_two, bias_two, full_inner, full_inner_bias, full_outer, full_outer_bias = (
        lax.all_gather(norm2_gain, ("dp", "seq"), axis=0, tiled=True),
        lax.all_gather(norm2_bias, ("dp", "seq"), axis=0, tiled=True),
        lax.all_gather(w_inner, ("dp", "seq"), axis=0, tiled=True),
        lax.all_gather(inner_bias, ("dp", "seq"), axis=0, tiled=True),
        lax.all_gather(w_outer, ("dp", "seq"), axis=0, tiled=True),
        lax.all_gather(outer_bias, ("dp", "seq"), axis=0, tiled=True),
    )
    stream_a = stream_one.astype(jnp.float32).reshape(row_total, features)
    stream_b = stream_two.astype(jnp.float32).reshape(row_total, features)
    normed_one, unit_one, scale_one = norm_parts(
        stream_b, gain_one.astype(jnp.float32), bias_one.astype(jnp.float32)
    )
    hidden = normed_one.astype(jnp.bfloat16)
    joined = jnp.concatenate([full_query_key, full_value], 1)
    projected = (
        matmul(hidden, joined).astype(jnp.bfloat16).reshape(batch_seqs, tok_count, 2 * features)
    )
    position, local_place = routing(slot_place, slot_total, capacity, seq_devices)
    spread_rows = jnp.broadcast_to(
        projected[:, None], (batch_seqs, round_count, tok_count, 2 * features)
    )
    send_rows = scatter_rows(spread_rows, position, lane_total)
    send_meta = scatter_rows(jnp.stack([local_place, bucket_ids + 1], -1), position, lane_total)
    got_rows, got_meta = (
        lax.all_to_all(send_rows, "seq", split_axis=2, concat_axis=2, tiled=True),
        lax.all_to_all(send_meta, "seq", split_axis=2, concat_axis=2, tiled=True),
    )
    got_place = jnp.where(got_meta[..., 1] > 0, got_meta[..., 0], slot_total)
    placed = scatter_rows(got_rows, got_place, slot_total)
    place_tag = scatter_rows(got_meta[..., 1], got_place, slot_total)
    query_rows = placed[..., :features].reshape(head_shape)
    value_rows = placed[..., features:].reshape(head_shape)
    key_float, key_pull = jax.vjp(unit_keys, query_rows.astype(jnp.float32))
    key_rows = key_float.astype(jnp.bfloat16)
    prev_keys, prev_values, prev_tag = shifted(
        (key_rows[:, :, -SPAN:], value_rows[:, :, -SPAN:], for_sending(place_tag[:, :, -SPAN:])),
        "seq",
        1,
    )
    query_blocks = blocked(query_rows)
    tag_blocks = blocked(place_tag)
    key_window = window(key_rows, prev_keys)
    value_window = window(value_rows, prev_values)
    tag_window = window(place_tag, prev_tag)
    results, spreads = lax.map(
        attend, (query_blocks, key_window, value_window, tag_blocks, tag_window)
    )
    result_flat = lax.optimization_barrier(
        results.reshape(batch_seqs, round_count, slot_total, features)
    ).astype(jnp.float32)
    spread_flat = spreads.reshape(batch_seqs, round_count, slot_total, HEADS)
    ret_rows, ret_spread = (
        lax.all_to_all(
            pick_rows(result_flat, got_place), "seq", split_axis=2, concat_axis=2, tiled=True
        ),
        lax.all_to_all(
            pick_rows(spread_flat, got_place), "seq", split_axis=2, concat_axis=2, tiled=True
        ),
    )
    round_heads = pick_rows(ret_rows, position).reshape(
        batch_seqs, round_count, tok_count, HEADS, HEAD_DIM
    )
    round_spread = pick_rows(ret_spread, position)
    mix_weights = jax.nn.softmax(round_spread, axis=1)
    mixed = jnp.sum(mix_weights[..., None] * round_heads, 1).reshape(row_total, features)
    mixed_low = mixed.astype(jnp.bfloat16)
    out_one = stream_a + matmul(mixed_low, full_output)
    normed_two, unit_two, scale_two = norm_parts(
        out_one, gain_two.astype(jnp.float32), bias_two.astype(jnp.float32)
    )
    inner_low = normed_two.astype(jnp.bfloat16)
    pre_act = matmul(inner_low, full_inner) + full_inner_bias.astype(jnp.float32)
    activated, gelu_pull = jax.vjp(jax.nn.gelu, pre_act)
    act_low = activated.astype(jnp.bfloat16)
    out_two = stream_b + matmul(act_low, full_outer) + full_outer_bias.astype(jnp.float32)
    gain_two, bias_two, full_inner, full_inner_bias, full_outer, full_outer_bias = (
        lax.all_gather(norm2_gain, ("dp", "seq"), axis=0, tiled=True),
        lax.all_gather(norm2_bias, ("dp", "seq"), axis=0, tiled=True),
        lax.all_gather(w_inner, ("dp", "seq"), axis=0, tiled=True),
        lax.all_gather(inner_bias, ("dp", "seq"), axis=0, tiled=True),
        lax.all_gather(w_outer, ("dp", "seq"), axis=0, tiled=True),
        lax.all_gather(outer_bias, ("dp", "seq"), axis=0, tiled=True),
    )
    cot_two = grad_two.reshape(row_total, features)
    grad_outer = matmul_left(act_low, cot_two)
    grad_outer_bias = jnp.sum(cot_two.astype(jnp.float32), 0)
    d_act = matmul_right(cot_two, full_outer)
    d_pre = gelu_pull(d_act)[0].astype(jnp.bfloat16)
    grad_inner_bias = jnp.sum(d_pre.astype(jnp.float32), 0)
    grad_inner = matmul_left(inner_low, d_pre)
    d_normed_two = matmul_right(d_pre, full_inner)
    d_from_two, grad_gain_two, grad_bias_two = norm_back(
        d_normed_two, unit_two, scale_two, gain_two.astype(jnp.float32)
    )
    ffn_grads = (
        lax.psum_scatter(grad_gain_two, ("dp", "seq"), scatter_dimension=0, tiled=True),
        lax.psum_scatter(grad_bias_two, ("dp", "seq"), scatter_dimension=0, tiled=True),
        lax.psum_scatter(grad_inner, ("dp", "seq"), scatter_dimension=0, tiled=True),
        lax.psum_scatter(grad_inner_bias, ("dp", "seq"), scatter_dimension=0, tiled=True),
        lax.psum_scatter(grad_outer, ("dp", "seq"), scatter_dimension=0, tiled=True),
        lax.psum_scatter(grad_outer_bias, ("dp", "seq"), scatter_dimension=0, tiled=True),
    )
    back_one = grad_one.astype(jnp.float32).reshape(row_total, features) + d_from_two
    gain_one, bias_one, full_query_key, full_value, full_output = (
        lax.all_gather(norm1_gain, ("dp", "seq"), axis=0, tiled=True),
        lax.all_gather(norm1_bias, ("dp", "seq"), axis=0, tiled=True),
        lax.all_gather(w_query_key, ("dp", "seq"), axis=0, tiled=True),
        lax.all_gather(w_value, ("dp", "seq"), axis=0, tiled=True),
        lax.all_gather(w_output, ("dp", "seq"), axis=0, tiled=True),
    )
    joined = jnp.concatenate([full_query_key, full_value], 1)
    d_attended = back_one.astype(jnp.bfloat16)
    grad_output = matmul_left(mixed_low, d_attended)
    d_mixed = matmul_right(d_attended, full_output).reshape(
        batch_seqs, 1, tok_count, HEADS, HEAD_DIM
    )
    d_round = lax.optimization_barrier(
        (mix_weights[..., None] * d_mixed)
        .reshape(batch_seqs, round_count, tok_count, features)
        .astype(jnp.bfloat16)
    ).astype(jnp.float32)
    head_dot = jnp.sum(d_mixed * round_heads, -1)
    d_spread = mix_weights * (head_dot - jnp.sum(mix_weights * head_dot, 1, keepdims=True))
    got_grad, got_spread = (
        lax.all_to_all(
            scatter_rows(d_round, position, lane_total),
            "seq",
            split_axis=2,
            concat_axis=2,
            tiled=True,
        ),
        lax.all_to_all(
            scatter_rows(d_spread, position, lane_total),
            "seq",
            split_axis=2,
            concat_axis=2,
            tiled=True,
        ),
    )
    slot_grad = (
        scatter_rows(got_grad, got_place, slot_total).astype(jnp.bfloat16).reshape(head_shape)
    )
    slot_spread = scatter_rows(got_spread, got_place, slot_total).reshape(
        batch_seqs, round_count, slot_total, HEADS
    )
    d_query, d_keys, d_values = lax.map(
        attend_back,
        (
            query_blocks,
            key_window,
            value_window,
            tag_blocks,
            tag_window,
            spreads,
            blocked(slot_grad),
            blocked(slot_spread),
        ),
    )
    key_own, key_lead = fold_window(d_keys)
    value_own, value_lead = fold_window(d_values)
    key_next, value_next = (
        shifted(key_lead.astype(jnp.bfloat16), "seq", -1).astype(key_lead.dtype),
        shifted(value_lead.astype(jnp.bfloat16), "seq", -1).astype(value_lead.dtype),
    )
    key_own = key_own.at[:, :, -1].add(key_next)
    value_own = value_own.at[:, :, -1].add(value_next)
    d_from_keys = key_pull(key_own.reshape(head_shape))[0]
    d_query_total = (d_query.reshape(head_shape) + d_from_keys).reshape(
        batch_seqs, round_count, slot_total, features
    )
    d_place = jnp.concatenate(
        [d_query_total, value_own.reshape(batch_seqs, round_count, slot_total, features)], -1
    ).astype(jnp.bfloat16)
    returned = lax.all_to_all(
        pick_rows(d_place, got_place), "seq", split_axis=2, concat_axis=2, tiled=True
    )
    d_projected = (
        jnp.sum(pick_rows(returned, position).astype(jnp.float32), 1)
        .astype(jnp.bfloat16)
        .reshape(row_total, 2 * features)
    )
    grad_joined = matmul_left(hidden, d_projected)
    d_hidden = matmul_right(d_projected, joined)
    d_from_one, grad_gain_one, grad_bias_one = norm_back(
        d_hidden, unit_one, scale_one, gain_one.astype(jnp.float32)
    )
    back_two = cot_two.astype(jnp.float32) + d_from_one
    attn_grads = (
        lax.psum_scatter(grad_gain_one, ("dp", "seq"), scatter_dimension=0, tiled=True),
        lax.psum_scatter(grad_bias_one, ("dp", "seq"), scatter_dimension=0, tiled=True),
        lax.psum_scatter(grad_joined[:, :features], ("dp", "seq"), scatter_dimension=0, tiled=True),
        lax.psum_scatter(grad_joined[:, features:], ("dp", "seq"), scatter_dimension=0, tiled=True),
        lax.psum_scatter(grad_output, ("dp", "seq"), scatter_dimension=0, tiled=True),
    )
    out_shape = (batch_seqs, tok_count, features)
    return (
        out_one.reshape(out_shape),
        out_two.reshape(out_shape),
        back_one.reshape(out_shape),
        back_two.reshape(out_shape),
        attn_grads[0],
        attn_grads[1],
        attn_grads[2],
        attn_grads[3],
        attn_grads[4],
        ffn_grads[0],
        ffn_grads[1],
        ffn_grads[2],
        ffn_grads[3],
        ffn_grads[4],
        ffn_grads[5],
    )


def solution(mesh):
    return jax.shard_map(
        local,
        mesh=mesh,
        in_specs=(
            P("dp", "seq", None),
            P("dp", "seq", None),
            P("dp", None, "seq"),
            P("dp", None, "seq"),
            P("dp", "seq", None),
            P("dp", "seq", None),
            P(("dp", "seq")),
            P(("dp", "seq")),
            P(("dp", "seq"), None),
            P(("dp", "seq"), None),
            P(("dp", "seq"), None),
            P(("dp", "seq")),
            P(("dp", "seq")),
            P(("dp", "seq"), None),
            P(("dp", "seq")),
            P(("dp", "seq"), None),
            P(("dp", "seq")),
        ),
        out_specs=(
            P("dp", "seq", None),
            P("dp", "seq", None),
            P("dp", "seq", None),
            P("dp", "seq", None),
            P(("dp", "seq")),
            P(("dp", "seq")),
            P(("dp", "seq"), None),
            P(("dp", "seq"), None),
            P(("dp", "seq"), None),
            P(("dp", "seq")),
            P(("dp", "seq")),
            P(("dp", "seq"), None),
            P(("dp", "seq")),
            P(("dp", "seq"), None),
            P(("dp", "seq")),
        ),
        check_vma=False,
    )
```

profile of v0, /device:TPU:0, one launch (start us, length us, event | category | flops | bytes accessed | tf_op | source)
XLA Modules:
  0.0 2409.4 jit_solution(6583627973045844051)
XLA Ops:
  30.0 41.7 %all-reduce.14 = (bf16[1024]{0:T(1024)(128)(2,1)S(1)}, bf16[1024]{0:T(1024)(128)(2,1)S(1)}, bf16[1024]{0:T(1024)(128)(2,1)}, bf16[1024]{0:T(1024)(128)(2,1)S(1)}, bf16[1024]{0:T(1024)(128)(2,1)S(1)}) all-reduce(bf16[1024]{0:T(1024)(128)(2,1)S(1)} %dynamic-update-slice.7, ...), channel_id=1, replica_groups=mesh['dp'=4,'seq'=8] {'dp','seq'}, use_global_device_ids=true, to_apply=%add.3 | all-reduce | flops 5120 | bytes 20480
  76.3 52.8 %all-gather.9.cloned.1.call-done = bf16[1024,1024]{1,0:T(8,128)(2,1)} async-done(((bf16[32,1024]{1,0:T(8,128)(2,1)}), bf16[1024,1024]{1,0:T(8,128)(2,1)}) %all-gather.9.cloned.1.call-update) | async-done | bytes 2097168 | tf_op jit(solution)/shard_map/all_gather | solution.py:188
  172.0 206.6 %all-to-all-done.1 = bf16[2,4,256,2048]{3,1,0,2:T(4,128)(2,1)} async-done(((bf16[2,4,256,2048]{3,1,0,2:T(4,128)(2,1)}), bf16[2,4,256,2048]{3,1,0,2:T(4,128)(2,1)}, u32[]{:S(2)}, u32[]{:S(2)}) %all-to-all-start.1) | async-done | bytes 8388640 | tf_op jit(solution)/shard_map/all_to_all | solution.py:216
  389.8 17.1 scatter_custom_fusion.2
  442.9 32.8 %collective-permute-done.1 = s32[2,4,64]{2,1,0:T(4,128)S(1)} collective-permute-done((s32[2,4,64]{2,1,0:T(4,128)S(1)}, s32[2,4,64]{2,1,0:T(4,128)S(1)}, u32[]{:S(2)}, u32[]{:S(2)}) %collective-permute-start.1) | collective-permute-done | bytes 2080 | tf_op jit(solution)/shard_map/ppermute | solution.py:22
  502.8 24.4 %while.32 = (s32[]{:T(128)}, bf16[2,4,3,64,8,128]{5,4,3,2,1,0:T(8,128)(2,1)}, f32[2,4,3,64,8]{3,4,2,1,0:T(8,128)S(1)}, bf16[2,4,3,128,8,128]{5,3,4,2,1,0:T(8,128...) while((s32[]{:T(128)}, ...), condition=%wide.region_12.13_spmd, body=%wide.region_9.12_spmd.sunk | while | flops 411504192 | bytes 66625248 | solution.py:236
  571.0 74.6 %gather_fusion.2 = f32[2048,1024]{1,0:T(8,128)} fusion(f32[2,4,192,1024]{3,2,1,0:T(8,128)} %convert_element_type.147, s32[2048]{0:T(1024)S(1)} %bitcast.291), kind=kCustom, calls=%fused_computation.2 | custom fusion | bytes 16801792 | tf_op jit(solution)/shard_map/gather | solution.py:85
  664.3 232.2 %all-gather = bf16[32,1,128]{2,1,0:T(2,128)(2,1)S(1)} all-gather(bf16[1,1,128]{2,1,0:T(2,128)(2,1)S(1)} %bitcast.370), channel_id=1, replica_groups=mesh['dp'=4,'seq'=8] {'dp','seq'}, dimensions={0}, use_global_device_ids=true | all-gather | bytes 8448 | tf_op jit(solution)/shard_map/all_gather | solution.py:195
  927.5 21.6 gather_fusion.3
  1071.5 169.1 %all-to-all-done.4 = f32[2,4,256,1024]{3,1,0,2:T(4,128)} async-done(((f32[2,4,256,1024]{3,1,0,2:T(4,128)}), f32[2,4,256,1024]{3,1,0,2:T(4,128)}, u32[]{:S(2)}, u32[]{:S(2)}) %all-to-all-start.4) | async-done | bytes 8388640 | tf_op jit(solution)/shard_map/all_to_all | solution.py:316
  1271.4 166.8 %while.33 = (s32[]{:T(128)}, f32[2,4,3,64,8,128]{5,4,3,2,1,0:T(8,128)}, f32[2,4,3,128,8,128]{5,4,3,1,0,2:T(8,128)}, f32[2,4,3,128,8,128]{5,4,3,1,0,2:T(8,128)}, ...) while((s32[]{:T(128)}, ...), condition=%wide.region_28.29_spmd, body=%wide.region_26.28_spmd.sunk | while | flops 1021794112 | bytes 170286864 | solution.py:337
  1282.6 18.1 multiply_bitcast_fusion.4
  1306.4 19.7 multiply_bitcast_fusion.5
  1365.6 18.1 multiply_bitcast_fusion.4
  1389.6 19.6 multiply_bitcast_fusion.5
  1472.1 20.0 collective-permute-done.4
  1496.8 39.4 %collective-permute-done.3 = bf16[2,4,64,8,128]{4,3,2,1,0:T(8,128)(2,1)} collective-permute-done((bf16[2,4,64,8,128]{4,3,2,1,0:T(8,128)(2,1)}, bf16[2,4,64,8,128]{4,3,2,1,0:T(8,128)(2,1)}, u32[]{:S(2)}, u32[]{:S(2)}) %collective-permute-start.3) | collective-permute-done | bytes 1048608 | tf_op jit(solution)/shard_map/ppermute | solution.py:22
  1582.6 79.2 %gather_fusion.4 = bf16[2048,2048]{1,0:T(8,128)(2,1)} fusion(bf16[2,4,192,2048]{3,2,1,0:T(8,128)(2,1)} %pad_maximum_fusion.2, s32[2048]{0:T(1024)S(1)} %bitcast.292), kind=kCustom, calls=%fused_computation.4 | custom fusion | bytes 16801792 | tf_op jit(solution)/shard_map/gather | solution.py:85
  1671.9 277.7 %all_to_all.35 = bf16[2,4,256,2048]{3,1,0,2:T(4,128)(2,1)} all-to-all(bf16[2,4,256,2048]{3,1,0,2:T(4,128)(2,1)S(1)} %copy.375), channel_id=1, replica_groups=mesh['dp'=4,'seq'=8] {'seq'}, dimensions={2} | all-to-all | bytes 16777216 | tf_op jit(solution)/shard_map/all_to_all | solution.py:365
  1960.9 26.5 %gather_fusion.5 = bf16[1024,2048]{1,0:T(8,128)(2,1)} fusion(bf16[2,4,256,2048]{3,2,1,0:T(8,128)(2,1)} %copy.376, s32[1024]{0:T(1024)S(1)} %bitcast.295), kind=kCustom, calls=%fused_computation.5 | custom fusion | bytes 8400896 | tf_op jit(solution)/shard_map/gather | solution.py:85
  2007.6 47.5 %all-reduce.13 = (f32[1024]{0:T(1024)S(1)}, f32[1024]{0:T(1024)S(1)}, f32[1024]{0:T(1024)S(1)}, f32[1024]{0:T(1024)S(1)}, f32[4096]{0:T(1024)S(1)}, /*index=5*/f32[1024]{0:T(1024)S(1)}) all-reduce(f32[1024]{0:T(1024)S(1)} %get-tuple-element.479, ...), channel_id=2, replica_groups=mesh['dp'=4,'seq'=8] {'dp','seq'}, use_global_device_ids=true, to_apply=%region_34.35.clone | all-reduce | flops 9216 | bytes 73728
  2059.9 50.5 %reduce-scatter.14.cloned.1.call-done = f32[128,1024]{1,0:T(8,128)} async-done(((f32[4096,1024]{1,0:T(8,128)}), f32[128,1024]{1,0:T(8,128)}) %reduce-scatter.14.cloned.1.call-update) | async-done | bytes 524304 | tf_op jit(solution)/shard_map/reduce_scatter | solution.py:291
  2110.4 148.7 %reduce-scatter.6.cloned.1.call-done = f32[32,1024]{1,0:T(8,128)} async-done(((f32[1024,1024]{1,0:T(8,128)}), f32[32,1024]{1,0:T(8,128)}) %reduce-scatter.6.cloned.1.call-update) | async-done | bytes 131088 | tf_op jit(solution)/shard_map/reduce_scatter | solution.py:382
  2259.1 143.2 %reduce-scatter.8.cloned.1.call-done = f32[32,1024]{1,0:T(8,128)} async-done(((f32[1024,1024]{1,0:T(8,128)}), f32[32,1024]{1,0:T(8,128)}) %reduce-scatter.8.cloned.1.call-update) | async-done | bytes 131088 | tf_op jit(solution)/shard_map/reduce_scatter | solution.py:383
  (456 shorter events, 636.2 us)
Async XLA Ops:
  7.2 65.9 %all-gather.7.cloned.1.call-start = ((), (), s32[]{:S(2)}) async-start(), calls=%async_computation.12 | async-start | bytes 2162688 | tf_op jit(solution)/shard_map/all_gather | solution.py:187
  8.0 121.1 %all-gather.9.cloned.1.call-start = ((), (), s32[]{:S(2)}) async-start(), calls=%async_computation.13 | async-start | bytes 2162688 | tf_op jit(solution)/shard_map/all_gather | solution.py:188
  8.7 887.9 %all-gather.15.cloned.1.call-start = ((), (), s32[]{:S(2)}) async-start(), calls=%async_computation.16 | async-start | bytes 8650752 | tf_op jit(solution)/shard_map/all_gather | solution.py:196
  21.6 141.0 %all-to-all-start = ((s32[8,1,512]{2,1,0:T(1,128)}), s32[8,1,512]{2,1,0:T(1,128)S(1)}, u32[]{:S(2)}, u32[]{:S(2)}) async-start(s32[8,1,512]{2,1,0:T(1,128)} %reshape.608), calls=%async_computation | async-start | bytes 32768 | tf_op jit(solution)/shard_map/all_to_all | solution.py:217
  162.6 216.0 %all-to-all-start.1 = ((bf16[2,4,256,2048]{3,1,0,2:T(4,128)(2,1)}), bf16[2,4,256,2048]{3,1,0,2:T(4,128)(2,1)}, u32[]{:S(2)}, u32[]{:S(2)}) async-start(bf16[2,4,256,2048]{3,1,0,2:T(4,128)(2,1)} %copy.335), calls=%async_computation.1 | async-start | bytes 16777216 | tf_op jit(solution)/shard_map/all_to_all | solution.py:216
  167.7 788.3 %all-gather.11.cloned.1.call-start = ((), (), s32[]{:S(2)}) async-start(), calls=%async_computation.14 | async-start | bytes 2162688 | tf_op jit(solution)/shard_map/all_gather | solution.py:189
  168.3 790.6 %all-gather.13.cloned.1.call-start = ((), (), s32[]{:S(2)}) async-start(), calls=%async_computation.15 | async-start | bytes 8650752 | tf_op jit(solution)/shard_map/all_gather | solution.py:194
  172.0 261.3 %copy-start.55 = (s32[2,2,4,128]{3,1,2,0:T(2,128)}, s32[2,2,4,128]{3,1,2,0:T(2,128)S(1)}, u32[]{:S(2)}) copy-start(s32[2,2,4,128]{3,1,2,0:T(2,128)S(1)} %copy.423) | copy-start | bytes 24580
  423.8 62.9 %collective-permute-start.2 = (bf16[2,4,64,8,128]{4,3,2,1,0:T(8,128)(2,1)}, bf16[2,4,64,8,128]{4,3,2,1,0:T(8,128)(2,1)}, u32[]{:S(2)}, u32[]{:S(2)}) collective-permute-start(bf16[2,4,64,8,128]{4,3,2,1,0:T(8,128)(2,1)} %fusion.77), channel_id=1, source_target_pairs={{0,1},{1,2},{2,3},{3,4},{4,5},{5,6},{6,7},{8,9},{9,10},{10,11},{11... | collective-permute-start | bytes 3145736 | tf_op jit(solution)/shard_map/ppermute | solution.py:22
  431.1 66.4 %collective-permute-start = (bf16[2,4,64,8,128]{4,2,3,1,0:T(8,128)(2,1)}, bf16[2,4,64,8,128]{4,2,3,1,0:T(8,128)(2,1)}, u32[]{:S(2)}, u32[]{:S(2)}) collective-permute-start(bf16[2,4,64,8,128]{4,2,3,1,0:T(8,128)(2,1)} %copy.398), channel_id=1, source_target_pairs={{0,1},{1,2},{2,3},{3,4},{4,5},{5,6},{6,7},{8,9},{9,10},{10,11},{11... | collective-permute-start | bytes 3145736 | tf_op jit(solution)/shard_map/ppermute | solution.py:22
  441.5 34.3 %collective-permute-start.1 = (s32[2,4,64]{2,1,0:T(4,128)S(1)}, s32[2,4,64]{2,1,0:T(4,128)S(1)}, u32[]{:S(2)}, u32[]{:S(2)}) collective-permute-start(s32[2,4,64]{2,1,0:T(4,128)S(1)} %slice.180), channel_id=1, source_target_pairs={{0,1},{1,2},{2,3},{3,4},{4,5},{5,6},{6,7},{8,9},{9,10},{10,11},{11... | collective-permute-start | bytes 6152 | tf_op jit(solution)/shard_map/ppermute | solution.py:22
  442.9 128.1 %copy-start = (s32[2,2,4,128]{3,1,2,0:T(2,128)}, s32[2,2,4,128]{3,1,2,0:T(2,128)S(1)}, u32[]{:S(2)}) copy-start(s32[2,2,4,128]{3,1,2,0:T(2,128)S(1)} %copy.429) | copy-start | bytes 24580
  546.6 110.9 %all-to-all-start.2 = ((f32[8,1,2048]{2,1,0:T(1,128)}), f32[8,1,2048]{2,1,0:T(1,128)S(1)}, u32[]{:S(2)}, u32[]{:S(2)}) async-start(f32[8,1,2048]{2,1,0:T(1,128)} %reshape.610), calls=%async_computation.2 | async-start | bytes 131072 | tf_op jit(solution)/shard_map/all_to_all | solution.py:247
  657.6 239.1 %copy-start.22 = (bf16[2,128,1024]{2,1,0:T(8,128)(2,1)S(1)}, bf16[2,128,1024]{2,1,0:T(8,128)(2,1)}, u32[]{:S(2)}) copy-start(bf16[2,128,1024]{2,1,0:T(8,128)(2,1)} %param.30) | copy-start | bytes 1572868
  657.6 258.5 %all-to-all-start.3 = ((f32[2,4,256,1024]{3,1,0,2:T(4,128)}), f32[2,4,256,1024]{3,1,0,2:T(4,128)}, u32[]{:S(2)}, u32[]{:S(2)}) async-start(f32[2,4,256,1024]{3,1,0,2:T(4,128)} %copy.350), calls=%async_computation.3 | async-start | bytes 16777216 | tf_op jit(solution)/shard_map/all_to_all | solution.py:244
  664.3 1395.6 %reduce-scatter.10.cloned.1.call-start = ((), (), s32[]{:S(2)}) async-start(), calls=%async_computation.19 | async-start | bytes 4325376 | tf_op jit(solution)/shard_map/reduce_scatter | solution.py:384
  977.9 1082.0 %reduce-scatter.12.cloned.1.call-start = ((), (), s32[]{:S(2)}) async-start(), calls=%async_computation.20 | async-start | bytes 17301504 | tf_op jit(solution)/shard_map/reduce_scatter | solution.py:289
  1005.7 27.5 %all-to-all-start.5 = ((f32[8,1,2048]{2,1,0:T(1,128)}), f32[8,1,2048]{2,1,0:T(1,128)S(1)}, u32[]{:S(2)}, u32[]{:S(2)}) async-start(f32[8,1,2048]{2,1,0:T(1,128)} %reshape.612), calls=%async_computation.5 | async-start | bytes 131072 | tf_op jit(solution)/shard_map/all_to_all | solution.py:323
  1033.2 207.4 %all-to-all-start.4 = ((f32[2,4,256,1024]{3,1,0,2:T(4,128)}), f32[2,4,256,1024]{3,1,0,2:T(4,128)}, u32[]{:S(2)}, u32[]{:S(2)}) async-start(f32[2,4,256,1024]{3,1,0,2:T(4,128)} %copy.352), calls=%async_computation.4 | async-start | bytes 16777216 | tf_op jit(solution)/shard_map/all_to_all | solution.py:316
  1039.2 1071.2 %reduce-scatter.14.cloned.1.call-start = ((), (), s32[]{:S(2)}) async-start(), calls=%async_computation.21 | async-start | bytes 17301504 | tf_op jit(solution)/shard_map/reduce_scatter | solution.py:291
  1050.0 1209.1 %reduce-scatter.6.cloned.1.call-start = ((), (), s32[]{:S(2)}) async-start(), calls=%async_computation.17 | async-start | bytes 4325376 | tf_op jit(solution)/shard_map/reduce_scatter | solution.py:382
  1444.0 48.1 %collective-permute-start.4 = (bf16[2,4,64,8,128]{4,3,2,1,0:T(8,128)(2,1)}, bf16[2,4,64,8,128]{4,3,2,1,0:T(8,128)(2,1)S(1)}, u32[]{:S(2)}, u32[]{:S(2)}) collective-permute-start(bf16[2,4,64,8,128]{4,3,2,1,0:T(8,128)(2,1)} %fusion.80), channel_id=1, source_target_pairs={{1,0},{2,1},{3,2},{4,3},{5,4},{6,5},{7,6},{9,8},{10,9},{11,10},{12... | collective-permute-start | bytes 3145736 | tf_op jit(solution)/shard_map/ppermute | solution.py:22
  1448.2 87.9 %collective-permute-start.3 = (bf16[2,4,64,8,128]{4,3,2,1,0:T(8,128)(2,1)}, bf16[2,4,64,8,128]{4,3,2,1,0:T(8,128)(2,1)}, u32[]{:S(2)}, u32[]{:S(2)}) collective-permute-start(bf16[2,4,64,8,128]{4,3,2,1,0:T(8,128)(2,1)} %fusion.79), channel_id=1, source_target_pairs={{1,0},{2,1},{3,2},{4,3},{5,4},{6,5},{7,6},{9,8},{10,9},{11,10},{12... | collective-permute-start | bytes 3145736 | tf_op jit(solution)/shard_map/ppermute | solution.py:22
  1996.1 406.2 %reduce-scatter.8.cloned.1.call-start = ((), (), s32[]{:S(2)}) async-start(), calls=%async_computation.18 | async-start | bytes 4325376 | tf_op jit(solution)/shard_map/reduce_scatter | solution.py:383
  (81 other events, 923.6 us)
Sparse Core Ops, SparseCore 0:
  11.1 59.4 all-gather.6
  73.6 55.4 all-gather.8
  132.1 161.3 all-gather.14
  296.2 117.8 all-gather.10
  442.9 83.1 all-gather.12
  978.0 275.5 reduce-scatter.9
  1256.5 400.9 reduce-scatter.11
  1660.3 450.0 reduce-scatter.13
  2113.3 145.8 reduce-scatter.5
  2261.8 140.4 reduce-scatter.7
where the time goes:
time: 2420 us; the launch traced here: 2410 us
  waiting for transfers between devices  866 us (36%)
  blocking collectives  599 us (25%)
  local copies, waits for them, and re-layouts  588 us (24%)
  matrix products  185 us (8%)
  other arithmetic  98.9 us (4%)
  starting transfers between devices  55.5 us (2%)
    all_to_all x1, blocking collectives, local(): lax.all_to_all(pick_rows(d_place, got_place), 'seq', split_axis=2, concat...  278 us
    gather x9, local copies, waits for them, and re-layouts, pick_rows(): source[first_idx, second_idx, jnp.clip(position, 0, source.shape[2] - 1)]  250 us
    all_gather x1, blocking collectives, local(): lax.all_gather(inner_bias, ('dp', 'seq'), axis=0, tiled=True)  232 us
    all_to_all x1, waiting for transfers between devices, local(): lax.all_to_all(send_rows, 'seq', split_axis=2, concat_axis=2, tiled=True)  207 us
    all_to_all x1, waiting for transfers between devices, local(): lax.all_to_all(scatter_rows(d_round, position, lane_total), 'seq', split_...  169 us
    reduce_scatter x1, waiting for transfers between devices, local(): lax.psum_scatter(grad_joined[:, :features], ('dp', 'seq'), scatter_dimens...  149 us
    reduce_scatter x1, waiting for transfers between devices, local(): lax.psum_scatter(grad_joined[:, features:], ('dp', 'seq'), scatter_dimens...  143 us
    unnamed x179, local copies, waits for them, and re-layouts  102 us
  transfers between devices with their start and end apart: 21, of which 9 were waited for; matrix products, arithmetic and copies ran while one was open for 35% of the time, Pallas kernels for 0%

commit v1 on v0

v1 whole, which is shorter than its diff:
```python
import functools

import jax
import jax.numpy as jnp
from jax import lax
from jax.experimental import pallas as pl
from jax.experimental.pallas import tpu as pltpu
from jax.sharding import Mesh, PartitionSpec as P

HEADS = 8
HEAD_DIM = 128
SPAN = 64
GROUP = 3 * SPAN
WINDOW = GROUP + SPAN
F32 = jnp.float32
BF16 = jnp.bfloat16
CORE_SWAP = [(0, 1), (1, 0)]


def matmul(left, right):
    return jnp.dot(left, right, preferred_element_type=F32)


def matmul_left(left, right):
    return lax.dot_general(left, right, (((0,), (0,)), ((), ())), preferred_element_type=F32)


def matmul_right(left, right):
    return lax.dot_general(left, right, (((1,), (1,)), ((), ())), preferred_element_type=F32)


def norm_parts(value, gain, bias):
    row_mean = jnp.mean(value, -1, keepdims=True)
    centred = value - row_mean
    inv_scale = lax.rsqrt(jnp.mean(centred * centred, -1, keepdims=True) + 1e-05)
    normal = centred * inv_scale
    return (normal * gain + bias, normal, inv_scale)


def norm_back(cotangent, normal, inv_scale, gain):
    d_normal = cotangent * gain
    d_input = inv_scale * (
        d_normal
        - jnp.mean(d_normal, -1, keepdims=True)
        - normal * jnp.mean(d_normal * normal, -1, keepdims=True)
    )
    return (d_input, jnp.sum(cotangent * normal, 0), jnp.sum(cotangent, 0))


def swap(block):
    return lax.ppermute(block, "core", CORE_SWAP)


def pick(block, position, axis):
    return lax.dynamic_index_in_dim(block, position, axis, keepdims=False)


def exchange(block, axis, bit):
    size = lax.axis_size(axis)
    return lax.ppermute(block, axis, [(i, i ^ bit) for i in range(size)])


def half_steps(axes):
    steps = []
    for axis in axes:
        bit = lax.axis_size(axis) // 2
        while bit:
            steps.append((axis, bit))
            bit //= 2
    return steps


def gather_steps(block, axes):
    out = block[None]
    for axis, bit in reversed(half_steps(axes)):
        other = exchange(out, axis, bit)
        upper = (lax.axis_index(axis) // bit) % 2 == 1
        out = jnp.where(upper, jnp.concatenate([other, out], 0), jnp.concatenate([out, other], 0))
    return out


def scatter_steps(total, axes, sent_as):
    for axis, bit in half_steps(axes):
        half = total.reshape((2, total.shape[0] // 2) + total.shape[1:])
        mine = (lax.axis_index(axis) // bit) % 2
        sent = exchange(pick(half, 1 - mine, 0).astype(sent_as), axis, bit)
        total = pick(half, mine, 0) + sent.astype(F32)
    return total[0]


def all_to_all(block):
    return lax.all_to_all(block, "seq", split_axis=0, concat_axis=0, tiled=True)


def group_routes(count):
    size = lax.axis_size("seq")
    return [
        [(i, i // count * count + (i % count + step) % count) for i in range(size)]
        for step in range(1, count)
    ]


def group_sum(value, count):
    total = value
    for route in group_routes(count):
        total = total + lax.ppermute(value, "seq", route)
    return total


def group_max(value, count):
    total = value
    for route in group_routes(count):
        total = jnp.maximum(total, lax.ppermute(value, "seq", route))
    return total


def span_bias():
    query = jnp.arange(GROUP)[:, None]
    key = jnp.arange(WINDOW)[None, :]
    reach = key // SPAN - query // SPAN
    bias = jnp.where((reach == 0) | (reach == 1), 0.0, -1e9)
    return jnp.where(key == query + SPAN, -1e5, bias).astype(F32)


def split_three(value):
    high = value.astype(BF16).astype(F32)
    rest = value - high
    middle = rest.astype(BF16).astype(F32)
    return high, middle, rest - middle


def in_lanes(columns, rows):
    lane = lax.broadcasted_iota(jnp.int32, (rows, 128), 1)
    out = jnp.zeros((rows, 128), F32)
    for k, column in enumerate(columns):
        out = jnp.where(lane == k, column, out)
    return out


def one_hot_rows(place_row, base, rows, tokens):
    slot = lax.broadcasted_iota(jnp.int32, (rows, tokens), 0) + base
    return jnp.where(slot == place_row, 1.0, 0.0).astype(BF16)


def one_hot_columns(place_column, rows, slots):
    slot = lax.broadcasted_iota(jnp.int32, (rows, slots), 1)
    return jnp.where(slot == place_column, 1.0, 0.0).astype(BF16)


def tile_rows(tokens):
    if tokens <= 1024:
        return 3 * tokens // 2 // 2, tokens // 2
    return GROUP, 128


def head_scores(query, keys, bias, same):
    raw = matmul_right(query, keys) * (1.0 / HEAD_DIM)
    return jnp.where(same, raw + bias, -1e9)


def forward_kernel(
    heads, qv_ref, row_ref, column_ref, key_tag_ref, query_tag_ref, bias_ref,
    out_ref, spread_ref, placed_ref, slot_spread_ref, result_ref
):
    tokens = qv_ref.shape[0]
    slots = placed_ref.shape[1] - SPAN
    width = heads * HEAD_DIM
    place_rows, token_rows = tile_rows(tokens)
    placed_ref[0, 0:SPAN] = jnp.zeros((SPAN, 3 * width), BF16)

    def place(step, carry):
        base = pl.multiple_of(step * place_rows, place_rows)
        hot = one_hot_rows(row_ref[0], base, place_rows, tokens)
        rows = matmul(hot, qv_ref[...])
        where = pl.ds(pl.multiple_of(base + SPAN, SPAN), place_rows)
        placed_ref[0, where, 0 : 2 * width] = rows.astype(BF16)
        for head in range(heads):
            query = rows[:, head * HEAD_DIM : (head + 1) * HEAD_DIM]
            scale = lax.rsqrt(jnp.mean(query * query, -1, keepdims=True) + 1e-06)
            first = 2 * width + head * HEAD_DIM
            placed_ref[0, where, first : first + HEAD_DIM] = (query * scale).astype(BF16)
        return carry

    lax.fori_loop(0, slots // place_rows, place, 0)

    def attend(group, carry):
        base = pl.multiple_of(group * GROUP, GROUP)
        own = pl.ds(pl.multiple_of(base + SPAN, SPAN), GROUP)
        window = pl.ds(base, WINDOW)
        same = query_tag_ref[0, pl.ds(base, GROUP), :] == key_tag_ref[0, group]
        bias = bias_ref[...]
        spreads = []
        for head in range(heads):
            lanes = slice(head * HEAD_DIM, (head + 1) * HEAD_DIM)
            query = placed_ref[0, own, lanes]
            keys = placed_ref[0, window, 2 * width + head * HEAD_DIM : 2 * width + (head + 1) * HEAD_DIM]
            values = placed_ref[0, window, width + head * HEAD_DIM : width + (head + 1) * HEAD_DIM]
            scores = head_scores(query, keys, bias, same)
            row_max = jnp.max(scores, -1, keepdims=True)
            exponent = jnp.exp(scores - row_max)
            row_sum = jnp.sum(exponent, -1, keepdims=True)
            probability = (exponent * (1.0 / row_sum)).astype(BF16)
            result_ref[pl.ds(base, GROUP), lanes] = matmul(probability, values).astype(BF16)
            spreads.append(row_max + jnp.log(row_sum))
        query_tag = query_tag_ref[0, pl.ds(base, GROUP), :]
        slot_spread_ref[0, pl.ds(base, GROUP), :] = in_lanes(spreads + [query_tag], GROUP)
        pieces = [split_three(spread) for spread in spreads]
        packed = in_lanes([piece[k] for k in range(3) for piece in pieces], GROUP)
        result_ref[pl.ds(base, GROUP), width : width + 128] = packed.astype(BF16)
        return carry

    lax.fori_loop(0, slots // GROUP, attend, 0)

    def read_back(step, carry):
        where = pl.ds(pl.multiple_of(step * token_rows, token_rows), token_rows)
        hot = one_hot_columns(column_ref[0, where, :], token_rows, slots)
        rows = matmul(hot, result_ref[...])
        out_ref[0, where, :] = rows[:, :width].astype(BF16)
        packed = rows[:, width:]
        spread_ref[0, where, :] = (
            packed[:, 0:heads] + packed[:, heads : 2 * heads] + packed[:, 2 * heads : 3 * heads]
        )
        return carry

    lax.fori_loop(0, tokens // token_rows, read_back, 0)


def backward_kernel(
    heads, grad_ref, placed_ref, slot_spread_ref, row_ref, column_ref, key_tag_ref,
    bias_ref, total_ref, slot_grad_ref, d_query_ref, d_key_ref, d_value_ref, d_place_ref
):
    tokens = grad_ref.shape[1]
    slots = placed_ref.shape[1] - SPAN
    width = heads * HEAD_DIM
    place_rows, token_rows = tile_rows(tokens)

    @pl.when(pl.program_id(0) == 0)
    def _():
        total_ref[...] = jnp.zeros(total_ref.shape, F32)

    d_key_ref[...] = jnp.zeros(d_key_ref.shape, F32)
    d_value_ref[...] = jnp.zeros(d_value_ref.shape, F32)

    def place(step, carry):
        base = pl.multiple_of(step * place_rows, place_rows)
        hot = one_hot_rows(row_ref[0], base, place_rows, tokens)
        slot_grad_ref[pl.ds(base, place_rows), :] = matmul(hot, grad_ref[0]).astype(BF16)
        return carry

    lax.fori_loop(0, slots // place_rows, place, 0)

    def attend(group, carry):
        base = pl.multiple_of(group * GROUP, GROUP)
        here = pl.ds(base, GROUP)
        own = pl.ds(pl.multiple_of(base + SPAN, SPAN), GROUP)
        window = pl.ds(base, WINDOW)
        same = slot_spread_ref[0, here, heads : heads + 1] == key_tag_ref[0, group]
        bias = bias_ref[...]
        packed = slot_grad_ref[here, width : width + 128].astype(F32)
        for head in range(heads):
            lanes = slice(head * HEAD_DIM, (head + 1) * HEAD_DIM)
            query = placed_ref[0, own, lanes]
            keys = placed_ref[0, window, 2 * width + head * HEAD_DIM : 2 * width + (head + 1) * HEAD_DIM]
            values = placed_ref[0, window, width + head * HEAD_DIM : width + (head + 1) * HEAD_DIM]
            d_out = slot_grad_ref[here, lanes]
            d_spread = (
                packed[:, head : head + 1]
                + packed[:, heads + head : heads + head + 1]
                + packed[:, 2 * heads + head : 2 * heads + head + 1]
            )
            scores = head_scores(query, keys, bias, same)
            probability = jnp.exp(scores - slot_spread_ref[0, here, head : head + 1])
            d_probs = matmul_right(d_out, values)
            row_dot = jnp.sum(probability * d_probs, -1, keepdims=True)
            d_scores = (probability * (d_probs + (d_spread - row_dot))).astype(BF16)
            d_query_ref[here, lanes] = matmul(d_scores, keys) * (1.0 / HEAD_DIM)
            d_key_ref[window, lanes] += matmul_left(d_scores, query)
            d_value_ref[window, lanes] += matmul_left(probability.astype(BF16), d_out)
        return carry

    lax.fori_loop(0, slots // GROUP, attend, 0)

    def finish(group, carry):
        base = pl.multiple_of(group * GROUP, GROUP)
        here = pl.ds(base, GROUP)
        own = pl.ds(pl.multiple_of(base + SPAN, SPAN), GROUP)
        for head in range(heads):
            lanes = slice(head * HEAD_DIM, (head + 1) * HEAD_DIM)
            query = placed_ref[0, own, lanes].astype(F32)
            d_unit = d_key_ref[own, lanes] * (1.0 / HEAD_DIM)
            scale = lax.rsqrt(jnp.mean(query * query, -1, keepdims=True) + 1e-06)
            inner = jnp.mean(d_unit * query, -1, keepdims=True)
            d_query = d_query_ref[here, lanes] + scale * d_unit - query * (scale * scale * scale * inner)
            d_place_ref[here, lanes] = d_query.astype(BF16)
        d_place_ref[here, width : 2 * width] = d_value_ref[own, :].astype(BF16)
        return carry

    lax.fori_loop(0, slots // GROUP, finish, 0)

    def read_back(step, carry):
        where = pl.ds(pl.multiple_of(step * token_rows, token_rows), token_rows)
        hot = one_hot_columns(column_ref[0, where, :], token_rows, slots)
        total_ref[where, :] += matmul(hot, d_place_ref[...])
        return carry

    lax.fori_loop(0, tokens // token_rows, read_back, 0)


def per_round(shape, buffers):
    rest = (0,) * (len(shape) - 1)
    return pl.BlockSpec((1,) + shape[1:], lambda r: (r,) + rest, pipeline_mode=pl.Buffered(buffers))


def whole(shape):
    return pl.BlockSpec(shape, lambda r: (0,) * len(shape), pipeline_mode=pl.Buffered(1))


def attention_forward(qv, places, tags):
    row, column, key_tag, query_tag = places[0], places[1], tags[0], tags[1]
    rounds, _, tokens = row.shape
    slots = query_tag.shape[1]
    width = qv.shape[1] // 2
    heads = width // HEAD_DIM
    buffers = min(2, rounds)
    bias = span_bias()
    outs = [
        jax.ShapeDtypeStruct((rounds, tokens, width), BF16),
        jax.ShapeDtypeStruct((rounds, tokens, heads), F32),
        jax.ShapeDtypeStruct((rounds, slots + SPAN, 3 * width), BF16),
        jax.ShapeDtypeStruct((rounds, slots, 128), F32),
    ]
    flops = rounds * slots * (2 * tokens * (3 * width + 128) + 4 * width * WINDOW)
    return pl.pallas_call(
        functools.partial(forward_kernel, heads),
        grid=(rounds,),
        in_specs=[whole(qv.shape)]
        + [per_round(x.shape, buffers) for x in (row, column, key_tag, query_tag)]
        + [whole(bias.shape)],
        out_specs=[per_round(x.shape, buffers) for x in outs],
        out_shape=outs,
        scratch_shapes=[pltpu.VMEM((slots, width + 128), BF16)],
        compiler_params=pltpu.CompilerParams(vmem_limit_bytes=56 * 1024 * 1024),
        cost_estimate=pl.CostEstimate(flops=flops, bytes_accessed=20 << 20, transcendentals=0),
    )(qv, row, column, key_tag, query_tag, bias)


def attention_backward(grads, placed, slot_spread, places, tags):
    row, column, key_tag = places[0], places[1], tags
    rounds, _, tokens = row.shape
    slots = placed.shape[1] - SPAN
    width = placed.shape[2] // 3
    heads = width // HEAD_DIM
    buffers = min(2, rounds)
    bias = span_bias()
    flops = rounds * slots * (2 * tokens * (3 * width + 128) + 10 * width * WINDOW)
    return pl.pallas_call(
        functools.partial(backward_kernel, heads),
        grid=(rounds,),
        in_specs=[
            per_round(x.shape, buffers)
            for x in (grads, placed, slot_spread, row, column, key_tag)
        ]
        + [whole(bias.shape)],
        out_specs=whole((tokens, 2 * width)),
        out_shape=jax.ShapeDtypeStruct((tokens, 2 * width), F32),
        scratch_shapes=[
            pltpu.VMEM((slots, width + 128), BF16),
            pltpu.VMEM((slots, width), F32),
            pltpu.VMEM((slots + SPAN, width), F32),
            pltpu.VMEM((slots + SPAN, width), F32),
            pltpu.VMEM((slots, 2 * width), BF16),
        ],
        compiler_params=pltpu.CompilerParams(vmem_limit_bytes=56 * 1024 * 1024),
        cost_estimate=pl.CostEstimate(flops=flops, bytes_accessed=20 << 20, transcendentals=0),
    )(grads, placed, slot_spread, row, column, key_tag, bias)


def local(
    stream_one,
    stream_two,
    slot_place,
    bucket_ids,
    grad_one,
    grad_two,
    norm1_gain,
    norm1_bias,
    w_query_key,
    w_value,
    w_output,
    norm2_gain,
    norm2_bias,
    w_inner,
    inner_bias,
    w_outer,
    outer_bias,
):
    chips, devices = lax.axis_size("chip"), lax.axis_size("seq")
    batch, tok, features = stream_one.shape
    rounds = slot_place.shape[1]
    sequences = 2 * batch
    tokens = devices * tok
    slots = 3 * tokens // 2
    own_rows = batch * tok
    rows = sequences * tok
    width = features // (2 * chips)
    heads = width // HEAD_DIM
    hidden_units = w_inner.shape[1]
    units = sequences * chips
    sharing = devices // units
    own_rounds = rounds // sharing
    shard = w_query_key.shape[0]
    core = lax.axis_index("core")
    place = ("chip", "seq")
    every = ("chip", "core", "seq")

    def by_core(own, other):
        return jnp.where(core == 0, jnp.stack([own, other]), jnp.stack([other, own]))

    small = jnp.stack([norm1_gain, norm1_bias, norm2_gain, norm2_bias, outer_bias])
    small = jnp.swapaxes(gather_steps(small, every), 0, 1).reshape(5, features).astype(F32)
    gain_one, bias_one, gain_two, bias_two, full_outer_bias = [small[k] for k in range(5)]
    half_inner_bias = gather_steps(inner_bias, place).reshape(-1).astype(F32)

    def column_halves(weight, outer):
        split = weight.reshape(weight.shape[0], outer, 2, -1)
        return pick(split, core, 2), pick(split, 1 - core, 2)

    key_own, key_other = column_halves(w_query_key, chips)
    value_own, value_other = column_halves(w_value, chips)
    joined_own = jnp.concatenate([key_own, value_own], 2).reshape(shard, -1)
    joined_other = jnp.concatenate([key_other, value_other], 2).reshape(shard, -1)
    joined = gather_steps(by_core(joined_own, swap(joined_other)), place)
    joined = jnp.swapaxes(joined.reshape(chips, devices, 2, shard, -1), 1, 2).reshape(features, -1)

    inner_own, inner_other = column_halves(w_inner, chips)
    inner_both = by_core(inner_own.reshape(shard, -1), swap(inner_other.reshape(shard, -1)))
    full_inner = lax.all_gather(inner_both, place, axis=0, tiled=False)
    full_inner = jnp.swapaxes(
        full_inner.reshape(chips, devices, 2, shard, -1), 1, 2
    ).reshape(features, -1)
    full_output = lax.all_gather(w_output, place, axis=0, tiled=True)
    full_outer = lax.all_gather(w_outer, place, axis=0, tiled=True)

    meta = jnp.stack([slot_place, bucket_ids + 1], 1)
    meta = jnp.concatenate([meta, swap(meta)], 0)
    meta = meta.reshape(sequences, 1, 2, sharing, own_rounds, tok)
    meta = jnp.swapaxes(jnp.broadcast_to(meta, (sequences, chips) + meta.shape[2:]), 2, 3)
    meta = all_to_all(meta.reshape(devices, 2, own_rounds, tok))
    meta = jnp.moveaxis(meta, 0, 2).reshape(2, own_rounds, tokens)
    token_place, token_tag = meta[0], meta[1]
    found = token_place[:, :, None] == jnp.arange(slots)[None, None, :]
    slot_tag = jnp.sum(jnp.where(found, token_tag[:, :, None], 0), 1).astype(F32)
    before = jnp.concatenate([jnp.zeros((own_rounds, SPAN), F32), slot_tag], 1)
    key_tag = jnp.stack(
        [before[:, first : first + WINDOW] for first in range(0, slots, GROUP)], 1
    )[:, :, None, :]
    places = (token_place[:, None, :], token_place[:, :, None])
    tags = (key_tag, slot_tag[:, :, None])

    stream_a = stream_one.astype(F32).reshape(own_rows, features)
    stream_b = stream_two.astype(F32).reshape(own_rows, features)
    normed_one, unit_one, scale_one = norm_parts(stream_b, gain_one, bias_one)
    hidden = normed_one.astype(BF16)
    hidden = jnp.concatenate([hidden, swap(hidden)], 0)
    projected = matmul(hidden, joined).astype(BF16)

    def to_attention(value):
        value = jnp.swapaxes(value.reshape(sequences, tok, chips, -1), 1, 2)
        value = jnp.broadcast_to(value[:, :, None], value.shape[:2] + (sharing,) + value.shape[2:])
        return all_to_all(value.reshape(devices, tok, -1)).reshape(tokens, -1)

    def from_attention(value):
        value = all_to_all(value.reshape(devices, tok, -1))
        value = value.reshape(sequences, chips, sharing, tok, -1)[:, :, 0]
        return jnp.swapaxes(value, 1, 2).reshape(rows, -1)

    round_heads, round_spread, placed, slot_spread = attention_forward(
        to_attention(projected), places, tags
    )
    top = group_max(jnp.max(round_spread, 0), sharing)
    weight = jnp.exp(round_spread - top)
    mix_weights = weight / group_sum(jnp.sum(weight, 0), sharing)
    round_heads = round_heads.reshape(own_rounds, tokens, heads, HEAD_DIM)
    mixed = group_sum(jnp.sum(mix_weights[..., None] * round_heads, 0), sharing)
    mixed = from_attention(mixed.reshape(tokens, width).astype(BF16))

    def core_sum(value):
        return value[:own_rows] + swap(value[own_rows:])

    out_one = stream_a + core_sum(matmul(mixed, full_output))
    normed_two, unit_two, scale_two = norm_parts(out_one, gain_two, bias_two)
    inner_low = normed_two.astype(BF16)
    inner_low = jnp.concatenate([inner_low, swap(inner_low)], 0)
    pre_act = matmul(inner_low, full_inner) + half_inner_bias
    activated, gelu_pull = jax.vjp(jax.nn.gelu, pre_act)
    act_low = activated.astype(BF16)
    out_two = stream_b + core_sum(matmul(act_low, full_outer)) + full_outer_bias

    cot_own = grad_two.reshape(own_rows, features)
    cot_two = jnp.concatenate([cot_own, swap(cot_own)], 0)
    grad_outer = matmul_left(act_low, cot_two)
    d_act = matmul_right(cot_two, full_outer)
    d_pre = gelu_pull(d_act)[0].astype(BF16)
    grad_inner = matmul_left(inner_low, d_pre)
    d_normed_two = core_sum(matmul_right(d_pre, full_inner))
    d_from_two, grad_gain_two, grad_bias_two = norm_back(
        d_normed_two, unit_two, scale_two, gain_two
    )
    back_one = grad_one.astype(F32).reshape(own_rows, features) + d_from_two
    grad_outer = lax.psum_scatter(grad_outer.astype(BF16), place, scatter_dimension=0, tiled=True)
    grad_inner = jnp.swapaxes(
        grad_inner.astype(BF16).reshape(chips, 2, devices, shard, -1), 1, 2
    ).reshape(chips * devices, 2 * shard, -1)
    grad_inner = lax.psum_scatter(grad_inner, place, scatter_dimension=0, tiled=True)
    grad_inner = grad_inner.reshape(2, shard, -1).astype(F32)
    grad_inner_bias = scatter_steps(
        jnp.sum(d_pre.astype(F32), 0).reshape(chips * devices, -1), place, F32
    )

    def join_columns(pieces, outer):
        own, other = pick(pieces, core, 0), swap(pick(pieces, 1 - core, 0))
        both = by_core(own.reshape(shard, outer, -1), other.reshape(shard, outer, -1))
        return jnp.moveaxis(both, 0, 2)

    grad_inner = join_columns(grad_inner, chips).reshape(shard, hidden_units)

    d_attended = back_one.astype(BF16)
    d_attended = jnp.concatenate([d_attended, swap(d_attended)], 0)
    grad_output = matmul_left(mixed, d_attended).astype(BF16)
    grad_output = lax.psum_scatter(grad_output, place, scatter_dimension=0, tiled=True)
    d_mixed = to_attention(matmul_right(d_attended, full_output).astype(BF16))
    d_mixed = d_mixed.reshape(1, tokens, heads, HEAD_DIM).astype(F32)
    head_dot = jnp.sum(d_mixed * round_heads, -1)
    all_dot = group_sum(jnp.sum(mix_weights * head_dot, 0), sharing)
    d_spread = mix_weights * (head_dot - all_dot)
    d_round = (mix_weights[..., None] * d_mixed).astype(BF16).reshape(own_rounds, tokens, width)
    pieces = [piece.astype(BF16) for piece in split_three(d_spread)]
    blank = jnp.zeros((own_rounds, tokens, 128 - 3 * heads), BF16)
    grads = jnp.concatenate([d_round] + pieces + [blank], 2)
    d_total = attention_backward(grads, placed, slot_spread, places, tags[0])
    d_projected = from_attention(group_sum(d_total, sharing).astype(BF16))

    d_hidden = core_sum(matmul_right(d_projected, joined))
    d_from_one, grad_gain_one, grad_bias_one = norm_back(d_hidden, unit_one, scale_one, gain_one)
    back_two = cot_own.astype(F32) + d_from_one
    grad_joined = matmul_left(hidden, d_projected)
    grad_joined = jnp.swapaxes(
        grad_joined.reshape(chips, 2, devices, shard, -1), 1, 2
    ).reshape(chips * devices, 2 * shard, -1)
    grad_joined = scatter_steps(grad_joined, place, BF16).reshape(2, shard, -1)
    grad_joined = join_columns(grad_joined, chips).reshape(shard, chips, 2, 2, width)
    grad_query_key = grad_joined[:, :, :, 0].reshape(shard, features)
    grad_value = grad_joined[:, :, :, 1].reshape(shard, features)
    small_grads = jnp.stack(
        [grad_gain_one, grad_bias_one, grad_gain_two, grad_bias_two, jnp.sum(cot_own.astype(F32), 0)]
    )
    small_grads = jnp.swapaxes(small_grads.reshape(5, 2 * chips * devices, shard), 0, 1)
    small_grads = scatter_steps(small_grads, every, F32)
    out_shape = (batch, tok, features)
    return (
        out_one.reshape(out_shape),
        out_two.reshape(out_shape),
        back_one.reshape(out_shape),
        back_two.reshape(out_shape),
        small_grads[0],
        small_grads[1],
        grad_query_key,
        grad_value,
        grad_output.astype(F32),
        small_grads[2],
        small_grads[3],
        grad_inner,
        grad_inner_bias,
        grad_outer.astype(F32),
        small_grads[4],
    )


def solution(mesh):
    split = Mesh(
        mesh.devices.reshape(mesh.shape["dp"] // 2, 2, mesh.shape["seq"]), ("chip", "core", "seq")
    )
    dp = ("chip", "core")
    every = ("chip", "core", "seq")
    stream, meta, vector, matrix = (
        P(dp, "seq", None), P(dp, None, "seq"), P(every), P(every, None)
    )
    return jax.shard_map(
        local,
        mesh=split,
        in_specs=(
            stream, stream, meta, meta, stream, stream,
            vector, vector, matrix, matrix, matrix, vector, vector, matrix, vector, matrix, vector,
        ),
        out_specs=(
            stream, stream, stream, stream,
            vector, vector, matrix, matrix, matrix, vector, vector, matrix, vector, matrix, vector,
        ),
        check_vma=False,
    )
```

time: 2420 us -> 615 us (0.25)
  waiting for transfers between devices: 866 us -> 220 us
  blocking collectives: 599 us -> 31.5 us
  local copies, waits for them, and re-layouts: 588 us -> 70.6 us
  matrix products: 185 us -> 42.7 us
  Pallas kernels: 0 us -> 118 us
  other arithmetic: 98.9 us -> 47.5 us
    reduce_scatter x5 -> x3, waiting for transfers between devices: 342 us -> 0.06 us  [the longest x1 0.02 us: local(): lax.psum_scatter(grad_output, place, scatter_dimension=0, tiled=True)]
    all_to_all x6 -> x4, waiting for transfers between devices: 376 us -> 43.1 us  [all_to_all(): return lax.all_to_all(block, 'seq', split_axis=0, concat_axis=0, tiled=True)]
    gather x9 -> x0, local copies, waits for them, and re-layouts: 250 us -> none  [pick_rows(): source[first_idx, second_idx, jnp.clip(position, 0, source.shape[2] - 1)]]
    all_to_all x1, blocking collectives: 278 us -> 31.5 us  [all_to_all(): return lax.all_to_all(block, 'seq', split_axis=0, concat_axis=0, tiled=True)]
    all_gather x1 -> x0, blocking collectives: 232 us -> none  [local(): lax.all_gather(inner_bias, ('dp', 'seq'), axis=0, tiled=True)]
    dot_general x18 -> x4, matrix products: 145 us -> 12.6 us  [matmul(): return jnp.dot(left, right, preferred_element_type=F32)]
    pallas_call x0 -> x2, Pallas kernels: none -> 118 us  [the longest x1 68.4 us: attention_backward(): pl.pallas_call(functools.partial(backward_kernel, heads), grid=(rounds,),...]
    unnamed x179 -> x92, local copies, waits for them, and re-layouts: 102 us -> 9.98 us
  transfers between devices with their start and end apart: 21 -> 49, of which waited for: 9 -> 26; matrix products, arithmetic and copies ran while one was open for 35% -> 22% of each run, Pallas kernels for 0% -> 19%
where the time goes in v1:
time: 615 us; the launch traced here: 608 us
  waiting for transfers between devices  220 us (36%)
  Pallas kernels  118 us (19%)
  local copies, waits for them, and re-layouts  70.6 us (11%)
  starting transfers between devices  62 us (10%)
  other arithmetic  47.5 us (8%)
  matrix products  42.7 us (7%)
  blocking collectives  31.5 us (5%)
  between operations  15.9 us (3%)
    ppermute x26, waiting for transfers between devices, exchange(): return lax.ppermute(block, axis, [(i, i ^ bit) for i in range(size)])  167 us
    pallas_call x1, Pallas kernels, attention_backward(): pl.pallas_call(functools.partial(backward_kernel, heads), grid=(rounds,),...  68.4 us
    pallas_call x1, Pallas kernels, attention_forward(): pl.pallas_call(functools.partial(forward_kernel, heads), grid=(rounds,),...  49.7 us
    ppermute x26, starting transfers between devices, exchange(): return lax.ppermute(block, axis, [(i, i ^ bit) for i in range(size)])  44.3 us
    all_to_all x4, waiting for transfers between devices, all_to_all(): return lax.all_to_all(block, 'seq', split_axis=0, concat_axis=0, tiled=True)  43.1 us
    all_to_all x1, blocking collectives, all_to_all(): return lax.all_to_all(block, 'seq', split_axis=0, concat_axis=0, tiled=True)  31.5 us
    all_to_all x4, starting transfers between devices, all_to_all(): return lax.all_to_all(block, 'seq', split_axis=0, concat_axis=0, tiled=True)  15.2 us
    dot_general x4, matrix products, matmul_right(): lax.dot_general(left, right, (((1,), (1,)), ((), ())), preferred_element_...  15.1 us
  transfers between devices with their start and end apart: 49, of which 26 were waited for; matrix products, arithmetic and copies ran while one was open for 22% of the time, Pallas kernels for 19%

profile of v1, /device:TPU:0, one launch (start us, length us, event | category | flops | bytes accessed | tf_op | source)
XLA Modules:
  0.0 607.8 jit_solution(3027625322614376157)
XLA Ops:
  18.2 5.1 collective-permute-done.7
  25.3 6.9 %collective-permute-done.8 = bf16[2,2,32,1024]{3,2,1,0:T(8,128)(2,1)S(1)} collective-permute-done((bf16[2,2,32,1024]{3,2,1,0:T(8,128)(2,1)S(1)}, bf16[2,2,32,1024]{3,2,1,0:T(8,128)(2,1)S(1)}, u32[]{:S(2)}, u32[]{:S(2)}) %collective-permute-start.8) | collective-permute-done | bytes 262176 | tf_op jit(solution)/shard_map/ppermute | solution.py:60
  36.5 9.8 %collective-permute-done.1 = bf16[2,5,32]{2,1,0:T(8,128)(2,1)S(1)} collective-permute-done((bf16[2,5,32]{2,1,0:T(8,128)(2,1)S(1)}, bf16[2,5,32]{2,1,0:T(8,128)(2,1)S(1)}, u32[]{:S(2)}, u32[]{:S(2)}) %collective-permute-start.1) | collective-permute-done | bytes 672 | tf_op jit(solution)/shard_map/ppermute | solution.py:60
  48.7 11.7 %collective-permute-done.2 = bf16[4,5,32]{2,1,0:T(8,128)(2,1)S(1)} collective-permute-done((bf16[4,5,32]{2,1,0:T(8,128)(2,1)S(1)}, bf16[4,5,32]{2,1,0:T(8,128)(2,1)S(1)}, u32[]{:S(2)}, u32[]{:S(2)}) %collective-permute-start.2) | collective-permute-done | bytes 1312 | tf_op jit(solution)/shard_map/ppermute | solution.py:60
  63.2 27.4 %collective-permute-done.4 = bf16[16,5,32]{2,1,0:T(8,128)(2,1)S(1)} collective-permute-done((bf16[16,5,32]{2,1,0:T(8,128)(2,1)S(1)}, bf16[16,5,32]{2,1,0:T(8,128)(2,1)S(1)}, u32[]{:S(2)}, u32[]{:S(2)}) %collective-permute-start.4) | collective-permute-done | bytes 5152 | tf_op jit(solution)/shard_map/ppermute | solution.py:60
  97.4 5.9 all-to-all-done.1
  121.4 27.1 %all-to-all-done = bf16[8,128,512]{2,1,0:T(8,128)(2,1)S(1)} async-done(((bf16[8,128,512]{2,1,0:T(8,128)(2,1)}), bf16[8,128,512]{2,1,0:T(8,128)(2,1)S(1)}, u32[]{:S(2)}, u32[]{:S(2)}) %all-to-all-start) | async-done | bytes 1048608 | tf_op jit(solution)/shard_map/all_to_all | solution.py:92
  149.5 49.7 %shard_map.280 = (bf16[4,1024,256]{2,1,0:T(8,128)(2,1)}, f32[4,1024,2]{2,1,0:T(8,128)}, bf16[4,1600,768]{2,1,0:T(8,128)(2,1)}, f32[4,1536,128]{2,1,0:T(8,128)}) custom-call(bf16[1024,512]{1,0:T(8,128)(2,1)} %bitcast.286, s32[4,1,1024]{2,1,0:T(1,128)} %bitcast.308, s32[4,1024,1]{2,1,0:T(8,128)} %copy.175.column_ref, ...), custom_call_target="tpu_custom_call" | custom-call | flops 12884901888 | bytes 20971520 | tf_op jit(solution)/shard_map/pallas_call | solution.py:333
  202.5 6.5 %mul.182 = f32[4,1024,2,128]{3,2,1,0:T(2,128)} broadcast(f32[4,1024,2]{2,1,0:T(8,128)S(1)} %fusion.7), dimensions={0,1,2} | broadcast | bytes 4227072 | tf_op jit(solution)/shard_map/mul | solution.py:484
  209.0 6.4 %mul.183 = f32[4,1024,256]{2,1,0:T(8,128)} reshape(f32[4,1024,2,128]{3,2,1,0:T(2,128)} %mul.182) | data formatting | bytes 8388608 | tf_op jit(solution)/shard_map/mul | solution.py:484
  218.8 31.5 %all_to_all.25 = bf16[8,128,256]{2,1,0:T(8,128)(2,1)S(1)} all-to-all(bf16[8,128,256]{2,1,0:T(8,128)(2,1)S(1)} %bitcast.285), channel_id=1, replica_groups=mesh['chip'=2,'core'=2,'seq'=8] {'seq'}, dimensions={0} | all-to-all | bytes 1048576 | tf_op jit(solution)/shard_map/all_to_all | solution.py:92
  279.7 6.4 %fusion.30 = f32[512,2048]{1,0:T(8,128)} fusion(bf16[1024,2048]{1,0:T(8,128)(2,1)S(1)} %bitcast.271, bf16[256,1024]{1,0:T(8,128)(2,1)} %collective-permute-done.13, bf16[256,1024]{1,0:T(8,128)(2,1)} %add_convert_fusion), kind=kOutput, calls=%fused_computation.76 | convolution fusion | flops 2149580800 | bytes 9437184 | tf_op jit(solution)/shard_map/dot_general | solution.py:21
  286.2 8.7 %convert_reduce_fusion = (f32[2048]{0:T(1024)S(1)}, bf16[512,2048]{1,0:T(8,128)(2,1)S(1)}) fusion(f32[512,2048]{1,0:T(8,128)} %fusion.30, f32[2048]{0:T(1024)S(1)} %fusion.46, bf16[2048,1024]{1,0:T(8,128)(2,1)} %all-gather.8.cloned.1.call-done, bf16[256,1024]{1,0:T(8,128)(2,1)} %collective-permute-done.20, bf16[256,1024]{1,0:T(8,128)(2,1)} %bitcast.48), kind=kOutput, calls=%fused_computation.11 | convolution fusion | flops 2173696000 | bytes 11550720 | tf_op jit(solution)/shard_map/dot_general | solution.py:29
  328.8 10.1 %all-to-all-done.3 = bf16[8,128,256]{2,1,0:T(8,128)(2,1)S(1)} async-done(((bf16[8,128,256]{2,1,0:T(8,128)(2,1)}), bf16[8,128,256]{2,1,0:T(8,128)(2,1)S(1)}, u32[]{:S(2)}, u32[]{:S(2)}) %all-to-all-start.3) | async-done | bytes 524320 | tf_op jit(solution)/shard_map/all_to_all | solution.py:92
  341.4 7.1 %multiply_reduce_fusion = f32[4,1024,2]{2,1,0:T(8,128)S(1)} fusion(f32[4,1024,2,128]{3,2,1,0:T(2,128)} %reshape.573, f32[1024,2,128]{2,1,0:T(2,128)} %reshape.572), kind=kLoop, calls=%fused_computation.12 | loop fusion | flops 2088960 | bytes 5275648 | tf_op jit(solution)/shard_map/reduce_sum | solution.py:533
  354.6 8.3 %concatenate.168.grad_ref = bf16[4,1024,384]{2,1,0:T(8,128)(2,1)} concatenate(bf16[4,1024,256]{2,1,0:T(8,128)(2,1)S(1)} %multiply_convert_fusion, bf16[4,1024,2]{2,1,0:T(8,128)(2,1)} %get-tuple-element.47, bf16[4,1024,2]{2,1,0:T(8,128)(2,1)} %get-tuple-element.46, bf16[4,1024,2]{2,1,0:T(8,128)(2,1)S(1)} %get-tuple-element.39, bf16[4,1024,122]{2,1,0:T(8,128)(2,1)} %broadcast_in_dim.81), dimensions={2} | concatenate | bytes 6291456 | tf_op jit(solution)/shard_map/concatenate | solution.py:539
  362.9 68.4 %shard_map.281 = f32[1024,512]{1,0:T(8,128)} custom-call(bf16[4,1024,384]{2,1,0:T(8,128)(2,1)} %concatenate.168.grad_ref, bf16[4,1600,768]{2,1,0:T(8,128)(2,1)} %get-tuple-element.21.placed_ref, f32[4,1536,128]{2,1,0:T(8,128)} %get-tuple-element.22.slot_spread_ref, s32[4,1,1024]{2,1,0:T(1,128)} %bitcast.309, s32[4,1024,1]{2,1,0:T(8,128)} %copy.175.column_ref, ...), custom_call_target="tpu_custom_call" | custom-call | flops 15300820992 | bytes 20971520 | tf_op jit(solution)/shard_map/pallas_call | solution.py:356
  437.8 7.7 %convolution_convert_fusion = bf16[2048,1024]{1,0:T(8,128)(2,1)} fusion(bf16[256,1024]{1,0:T(8,128)(2,1)} %collective-permute-done.20, bf16[256,1024]{1,0:T(8,128)(2,1)} %bitcast.48, f32[512,2048]{1,0:T(8,128)} %fusion.30, f32[2048]{0:T(1024)S(1)} %fusion.46), kind=kOutput, calls=%fused_computation.16 | convolution fusion | flops 2162163712 | bytes 9445376 | tf_op jit(solution)/shard_map/dot_general | solution.py:25
  449.9 21.5 %collective-permute-done.36 = f32[4,128]{1,0:T(4,128)S(1)} collective-permute-done((f32[4,128]{1,0:T(4,128)S(1)}, f32[4,128]{1,0:T(4,128)S(1)}, u32[]{:S(2)}, u32[]{:S(2)}) %collective-permute-start.36) | collective-permute-done | bytes 2080 | tf_op jit(solution)/shard_map/ppermute | solution.py:60
  496.4 22.3 %collective-permute-done.29 = bf16[8,64,1024]{2,1,0:T(8,128)(2,1)} collective-permute-done((bf16[8,64,1024]{2,1,0:T(8,128)(2,1)S(1)}, bf16[8,64,1024]{2,1,0:T(8,128)(2,1)}, u32[]{:S(2)}, u32[]{:S(2)}) %collective-permute-start.29) | collective-permute-done | bytes 1048608 | tf_op jit(solution)/shard_map/ppermute | solution.py:60
  533.6 26.6 %collective-permute-done.26 = f32[4,5,32]{2,1,0:T(8,128)S(1)} collective-permute-done((f32[4,5,32]{2,1,0:T(8,128)S(1)}, f32[4,5,32]{2,1,0:T(8,128)S(1)}, u32[]{:S(2)}, u32[]{:S(2)}) %collective-permute-start.26) | collective-permute-done | bytes 2592 | tf_op jit(solution)/shard_map/ppermute | solution.py:60
  560.3 5.5 collective-permute-start.27
  571.6 7.5 %collective-permute-done.31 = bf16[2,64,1024]{2,1,0:T(8,128)(2,1)S(1)} collective-permute-done((bf16[2,64,1024]{2,1,0:T(8,128)(2,1)S(1)}, bf16[2,64,1024]{2,1,0:T(8,128)(2,1)S(1)}, u32[]{:S(2)}, u32[]{:S(2)}) %collective-permute-start.31) | collective-permute-done | bytes 262176 | tf_op jit(solution)/shard_map/ppermute | solution.py:60
  582.7 8.1 %collective-permute-done.32 = bf16[1,64,1024]{2,1,0:T(8,128)(2,1)S(1)} collective-permute-done((bf16[1,64,1024]{2,1,0:T(8,128)(2,1)S(1)}, bf16[1,64,1024]{2,1,0:T(8,128)(2,1)S(1)}, u32[]{:S(2)}, u32[]{:S(2)}) %collective-permute-start.32) | collective-permute-done | bytes 131104 | tf_op jit(solution)/shard_map/ppermute | solution.py:60
  (353 shorter events, 195.6 us)
Async XLA Ops:
  7.3 243.7 %all-gather.4.cloned.1.call-start = ((), (), s32[]{:S(2)}) async-start(), calls=%async_computation.8 | async-start | bytes 1114112 | tf_op jit(solution)/shard_map/all_gather | solution.py:441
  8.0 269.2 %all-gather.6.cloned.1.call-start = ((), (), s32[]{:S(2)}) async-start(), calls=%async_computation.9 | async-start | bytes 4456448 | tf_op jit(solution)/shard_map/all_gather | solution.py:437
  13.3 272.8 %all-gather.8.cloned.1.call-start = ((), (), s32[]{:S(2)}) async-start(), calls=%async_computation.10 | async-start | bytes 4456448 | tf_op jit(solution)/shard_map/all_gather | solution.py:442
  14.3 20.6 %collective-permute-start = (bf16[1,5,32]{2,1,0:T(8,128)(2,1)S(1)}, bf16[1,5,32]{2,1,0:T(8,128)(2,1)S(1)}, u32[]{:S(2)}, u32[]{:S(2)}) collective-permute-start(bf16[1,5,32]{2,1,0:T(8,128)(2,1)S(1)} %bitcast.320), channel_id=1, source_target_pairs={{0,1},{1,0},{2,3},{3,2},{4,5},{5,4},{6,7},{7,6},{8,9},{9,8},{10,11... | collective-permute-start | bytes 968 | tf_op jit(solution)/shard_map/ppermute | solution.py:60
  17.0 74.4 %collective-permute-start.11 = (s32[2,2,4,128]{3,2,0,1:T(4,128)S(1)}, s32[2,2,4,128]{3,2,0,1:T(4,128)S(1)}, u32[]{:S(2)}, u32[]{:S(2)}) collective-permute-start(s32[2,2,4,128]{3,2,0,1:T(4,128)S(1)} %pad_add_fusion.1), channel_id=1, source_target_pairs={{0,8},{8,0},{1,9},{9,1},{2,10},{10,2},{3,11},{11,3},{4,12},{12,4},... | collective-permute-start | bytes 24584 | tf_op jit(solution)/shard_map/ppermute | solution.py:51
  32.3 28.1 %collective-permute-start.9 = (bf16[4,2,32,1024]{3,2,1,0:T(8,128)(2,1)S(1)}, bf16[4,2,32,1024]{3,2,1,0:T(8,128)(2,1)S(1)}, u32[]{:S(2)}, u32[]{:S(2)}) collective-permute-start(bf16[4,2,32,1024]{3,2,1,0:T(8,128)(2,1)S(1)} %maximum_select_fusion.2), channel_id=1, source_target_pairs={{0,4},{1,5},{2,6},{3,7},{4,0},{5,1},{6,2},{7,3},{8,12},{9,13},{10,... | collective-permute-start | bytes 1572872 | tf_op jit(solution)/shard_map/ppermute | solution.py:60
  60.6 42.7 %collective-permute-start.10 = (bf16[8,2,32,1024]{3,2,1,0:T(8,128)(2,1)S(1)}, bf16[8,2,32,1024]{3,2,1,0:T(8,128)(2,1)S(1)}, u32[]{:S(2)}, u32[]{:S(2)}) collective-permute-start(bf16[8,2,32,1024]{3,2,1,0:T(8,128)(2,1)S(1)} %maximum_select_fusion.1), channel_id=1, source_target_pairs={{0,16},{16,0},{1,17},{17,1},{2,18},{18,2},{3,19},{19,3},{4,20},{20... | collective-permute-start | bytes 3145736 | tf_op jit(solution)/shard_map/ppermute | solution.py:60
  62.2 28.4 %collective-permute-start.4 = (bf16[16,5,32]{2,1,0:T(8,128)(2,1)S(1)}, bf16[16,5,32]{2,1,0:T(8,128)(2,1)S(1)}, u32[]{:S(2)}, u32[]{:S(2)}) collective-permute-start(bf16[16,5,32]{2,1,0:T(8,128)(2,1)S(1)} %maximum_select_fusion.9), channel_id=1, source_target_pairs={{0,16},{16,0},{1,17},{17,1},{2,18},{18,2},{3,19},{19,3},{4,20},{20... | collective-permute-start | bytes 15368 | tf_op jit(solution)/shard_map/ppermute | solution.py:60
  108.5 40.0 %all-to-all-start = ((bf16[8,128,512]{2,1,0:T(8,128)(2,1)}), bf16[8,128,512]{2,1,0:T(8,128)(2,1)S(1)}, u32[]{:S(2)}, u32[]{:S(2)}) async-start(bf16[8,128,512]{2,1,0:T(8,128)(2,1)} %bitcast.20), calls=%async_computation | async-start | bytes 2097152 | tf_op jit(solution)/shard_map/all_to_all | solution.py:92
  112.1 380.4 %reduce-scatter.4.cloned.1.call-start = ((), (), s32[]{:S(2)}) async-start(), calls=%async_computation.11 | async-start | bytes 1114112 | tf_op jit(solution)/shard_map/reduce_scatter | solution.py:530
  261.7 18.0 %collective-permute-start.13 = (bf16[256,1024]{1,0:T(8,128)(2,1)}, bf16[256,1024]{1,0:T(8,128)(2,1)}, u32[]{:S(2)}, u32[]{:S(2)}) collective-permute-start(bf16[256,1024]{1,0:T(8,128)(2,1)} %add_convert_fusion), channel_id=1, source_target_pairs={{0,8},{8,0},{1,9},{9,1},{2,10},{10,2},{3,11},{11,3},{4,12},{12,4},... | collective-permute-start | bytes 1572872 | tf_op jit(solution)/shard_map/ppermute | solution.py:51
  306.0 286.4 %reduce-scatter.6.cloned.1.call-start = ((), (), s32[]{:S(2)}) async-start(), calls=%async_computation.12 | async-start | bytes 4456448 | tf_op jit(solution)/shard_map/reduce_scatter | solution.py:514
  318.6 20.2 %all-to-all-start.3 = ((bf16[8,128,256]{2,1,0:T(8,128)(2,1)}), bf16[8,128,256]{2,1,0:T(8,128)(2,1)S(1)}, u32[]{:S(2)}, u32[]{:S(2)}) async-start(bf16[8,128,256]{2,1,0:T(8,128)(2,1)} %bitcast.51), calls=%async_computation.3 | async-start | bytes 1048576 | tf_op jit(solution)/shard_map/all_to_all | solution.py:92
  327.3 118.3 %collective-permute-start.35 = (f32[8,128]{1,0:T(8,128)S(1)}, f32[8,128]{1,0:T(8,128)S(1)}, u32[]{:S(2)}, u32[]{:S(2)}) collective-permute-start(f32[8,128]{1,0:T(8,128)S(1)} %fusion.43), channel_id=1, source_target_pairs={{0,16},{16,0},{1,17},{17,1},{2,18},{18,2},{3,19},{19,3},{4,20},{20... | collective-permute-start | bytes 12296 | tf_op jit(solution)/shard_map/ppermute | solution.py:60
  434.0 41.4 %all-to-all-start.4 = ((bf16[8,128,512]{2,1,0:T(8,128)(2,1)}), bf16[8,128,512]{2,1,0:T(8,128)(2,1)S(1)}, u32[]{:S(2)}, u32[]{:S(2)}) async-start(bf16[8,128,512]{2,1,0:T(8,128)(2,1)} %bitcast.53), calls=%async_computation.4 | async-start | bytes 2097152 | tf_op jit(solution)/shard_map/all_to_all | solution.py:92
  437.5 158.8 %reduce-scatter.8.cloned.1.call-start = ((), (), s32[]{:S(2)}) async-start(), calls=%async_computation.13 | async-start | bytes 4456448 | tf_op jit(solution)/shard_map/reduce_scatter | solution.py:510
  445.6 25.7 %collective-permute-start.36 = (f32[4,128]{1,0:T(4,128)S(1)}, f32[4,128]{1,0:T(4,128)S(1)}, u32[]{:S(2)}, u32[]{:S(2)}) collective-permute-start(f32[4,128]{1,0:T(4,128)S(1)} %fusion.49), channel_id=1, source_target_pairs={{0,4},{1,5},{2,6},{3,7},{4,0},{5,1},{6,2},{7,3},{8,12},{9,13},{10,... | collective-permute-start | bytes 6152 | tf_op jit(solution)/shard_map/ppermute | solution.py:60
  475.0 16.8 %collective-permute-start.38 = (f32[1,128]{1,0:T(1,128)S(1)}, f32[1,128]{1,0:T(1,128)S(1)}, u32[]{:S(2)}, u32[]{:S(2)}) collective-permute-start(f32[1,128]{1,0:T(1,128)S(1)} %constant_dynamic-slice_fusion), channel_id=1, source_target_pairs={{0,1},{1,0},{2,3},{3,2},{4,5},{5,4},{6,7},{7,6},{8,9},{9,8},{10,11... | collective-permute-start | bytes 1544 | tf_op jit(solution)/shard_map/ppermute | solution.py:60
  479.4 14.5 %collective-permute-start.23 = (f32[256,1024]{1,0:T(8,128)}, f32[256,1024]{1,0:T(8,128)}, u32[]{:S(2)}, u32[]{:S(2)}) collective-permute-start(f32[256,1024]{1,0:T(8,128)} %slice.153), channel_id=1, source_target_pairs={{0,8},{8,0},{1,9},{9,1},{2,10},{10,2},{3,11},{11,3},{4,12},{12,4},... | collective-permute-start | bytes 3145736 | tf_op jit(solution)/shard_map/ppermute | solution.py:51
  483.0 35.7 %collective-permute-start.29 = (bf16[8,64,1024]{2,1,0:T(8,128)(2,1)S(1)}, bf16[8,64,1024]{2,1,0:T(8,128)(2,1)}, u32[]{:S(2)}, u32[]{:S(2)}) collective-permute-start(bf16[8,64,1024]{2,1,0:T(8,128)(2,1)S(1)} %fusion.10), channel_id=1, source_target_pairs={{0,16},{16,0},{1,17},{17,1},{2,18},{18,2},{3,19},{19,3},{4,20},{20... | collective-permute-start | bytes 3145736 | tf_op jit(solution)/shard_map/ppermute | solution.py:60
  491.7 38.7 %collective-permute-start.19 = (f32[256,1024]{1,0:T(8,128)}, f32[256,1024]{1,0:T(8,128)}, u32[]{:S(2)}, u32[]{:S(2)}) collective-permute-start(f32[256,1024]{1,0:T(8,128)} %slice.148), channel_id=1, source_target_pairs={{0,8},{8,0},{1,9},{9,1},{2,10},{10,2},{3,11},{11,3},{4,12},{12,4},... | collective-permute-start | bytes 3145736 | tf_op jit(solution)/shard_map/ppermute | solution.py:51
  527.4 38.4 %collective-permute-start.30 = (bf16[4,64,1024]{2,1,0:T(8,128)(2,1)S(1)}, bf16[4,64,1024]{2,1,0:T(8,128)(2,1)S(1)}, u32[]{:S(2)}, u32[]{:S(2)}) collective-permute-start(bf16[4,64,1024]{2,1,0:T(8,128)(2,1)S(1)} %fusion.32), channel_id=1, source_target_pairs={{0,4},{1,5},{2,6},{3,7},{4,0},{5,1},{6,2},{7,3},{8,12},{9,13},{10,... | collective-permute-start | bytes 1572872 | tf_op jit(solution)/shard_map/ppermute | solution.py:60
  528.5 31.8 %collective-permute-start.26 = (f32[4,5,32]{2,1,0:T(8,128)S(1)}, f32[4,5,32]{2,1,0:T(8,128)S(1)}, u32[]{:S(2)}, u32[]{:S(2)}) collective-permute-start(f32[4,5,32]{2,1,0:T(8,128)S(1)} %dynamic-slice_bitcast_fusion.4), channel_id=1, source_target_pairs={{0,4},{1,5},{2,6},{3,7},{4,0},{5,1},{6,2},{7,3},{8,12},{9,13},{10,... | collective-permute-start | bytes 7688 | tf_op jit(solution)/shard_map/ppermute | solution.py:60
  567.4 15.3 %collective-permute-start.28 = (f32[1,5,32]{2,1,0:T(8,128)S(1)}, f32[1,5,32]{2,1,0:T(8,128)S(1)}, u32[]{:S(2)}, u32[]{:S(2)}) collective-permute-start(f32[1,5,32]{2,1,0:T(8,128)S(1)} %constant_dynamic-slice_fusion.10), channel_id=1, source_target_pairs={{0,1},{1,0},{2,3},{3,2},{4,5},{5,4},{6,7},{7,6},{8,9},{9,8},{10,11... | collective-permute-start | bytes 1928 | tf_op jit(solution)/shard_map/ppermute | solution.py:60
  (69 other events, 445.3 us)
Sparse Core Ops, SparseCore 0:
  10.9 71.9 all-gather.3
  86.3 90.2 all-gather.5
  179.4 81.2 all-gather.7
  306.1 77.1 reduce-scatter.3
  385.5 107.4 reduce-scatter.5
  495.3 100.2 reduce-scatter.7

commit v2 on v1

v2 whole, which is shorter than its diff:
```python
import functools

import jax
import jax.numpy as jnp
from jax import lax
from jax.experimental import pallas as pl
from jax.experimental.pallas import tpu as pltpu
from jax.sharding import Mesh, PartitionSpec as P

HEADS = 8
HEAD_DIM = 128
SPAN = 64
PAIR = 2 * SPAN
WINDOW = PAIR + SPAN
FORWARD_PAIRS = 4
BACKWARD_PAIRS = 4
F32 = jnp.float32
BF16 = jnp.bfloat16
CORE_SWAP = [(0, 1), (1, 0)]


def matmul(left, right):
    return jnp.dot(left, right, preferred_element_type=F32)


def matmul_left(left, right):
    return lax.dot_general(left, right, (((0,), (0,)), ((), ())), preferred_element_type=F32)


def matmul_right(left, right):
    return lax.dot_general(left, right, (((1,), (1,)), ((), ())), preferred_element_type=F32)


def norm_parts(value, gain, bias):
    row_mean = jnp.mean(value, -1, keepdims=True)
    centred = value - row_mean
    inv_scale = lax.rsqrt(jnp.mean(centred * centred, -1, keepdims=True) + 1e-05)
    normal = centred * inv_scale
    return (normal * gain + bias, normal, inv_scale)


def norm_back(cotangent, normal, inv_scale, gain):
    d_normal = cotangent * gain
    d_input = inv_scale * (
        d_normal
        - jnp.mean(d_normal, -1, keepdims=True)
        - normal * jnp.mean(d_normal * normal, -1, keepdims=True)
    )
    return (d_input, jnp.sum(cotangent * normal, 0), jnp.sum(cotangent, 0))


def swap(block):
    return lax.ppermute(block, "core", CORE_SWAP)


def pick(block, position, axis):
    return lax.dynamic_index_in_dim(block, position, axis, keepdims=False)


def exchange(block, axis, bit):
    size = lax.axis_size(axis)
    return lax.ppermute(block, axis, [(i, i ^ bit) for i in range(size)])


def half_steps(axis):
    steps = []
    bit = lax.axis_size(axis) // 2
    while bit:
        steps.append((axis, bit))
        bit //= 2
    return steps


def side(axis, bit):
    return (lax.axis_index(axis) // bit) % 2


def ordered(own, other, axis, bit):
    upper = side(axis, bit) == 1
    return jnp.where(upper, jnp.stack([other, own]), jnp.stack([own, other]))


class Gather:
    def __init__(self, block):
        self.dims = half_steps("chip") + [None] + half_steps("seq")
        self.tail = list(block.shape[1:])
        self.sizes = [2 if dim is None else 1 for dim in self.dims] + self.tail
        self.starts = [0 if dim is None else side(*dim) for dim in self.dims] + [0] * len(self.tail)
        buffer = jnp.zeros([2] * len(self.dims) + self.tail, block.dtype)
        self.held = lax.dynamic_update_slice(buffer, block.reshape(self.sizes), self.starts)

    def step(self, step):
        dim = self.dims.index(step)
        piece = exchange(lax.dynamic_slice(self.held, self.starts, self.sizes), *step)
        opposite = list(self.starts)
        opposite[dim] = 1 - self.starts[dim]
        self.held = lax.dynamic_update_slice(self.held, piece, opposite)
        self.starts[dim], self.sizes[dim] = 0, 2


class Stack:
    def __init__(self, block):
        self.held = block

    def step(self, step):
        self.held = ordered(self.held, exchange(self.held, *step), *step)


class Scatter:
    def __init__(self, total):
        self.dims = half_steps("chip") + [None] + half_steps("seq")
        self.held = total.reshape([2] * len(self.dims) + list(total.shape[3:]))

    def step(self, step):
        dim = self.dims.index(step)
        mine = side(*step)
        sent = exchange(pick(self.held, 1 - mine, dim).astype(BF16), *step)
        self.held = pick(self.held, mine, dim) + sent.astype(F32)
        self.dims.pop(dim)


class Halve:
    def __init__(self, total):
        self.held = total

    def step(self, step):
        half = self.held.reshape((2, self.held.shape[0] // 2) + self.held.shape[1:])
        mine = side(*step)
        self.held = pick(half, mine, 0) + exchange(pick(half, 1 - mine, 0), *step)


def together(chains):
    for chain, held in zip(chains, lax.optimization_barrier([chain.held for chain in chains])):
        chain.held = held


def all_to_all(block):
    return lax.all_to_all(block, "seq", split_axis=0, concat_axis=0, tiled=True)


def group_routes(count):
    size = lax.axis_size("seq")
    return [
        [(i, i // count * count + (i % count + step) % count) for i in range(size)]
        for step in range(1, count)
    ]


def group_sum(value, count):
    total = value
    for route in group_routes(count):
        total = total + lax.ppermute(value, "seq", route)
    return total


def group_max(value, count):
    total = value
    for route in group_routes(count):
        total = jnp.maximum(total, lax.ppermute(value, "seq", route))
    return total


def own_bias():
    own = jnp.arange(WINDOW)[:, None] == jnp.arange(PAIR)[None, :] + SPAN
    return jnp.where(own, -1e5, 0.0).astype(F32)


def pair_rows():
    return (jnp.arange(HEAD_DIM)[:, None] == jnp.arange(PAIR)[None, :] // SPAN).astype(BF16)


def flipped(value):
    return jnp.transpose(value.astype(F32)).astype(BF16)


def split_three(value):
    high = value.astype(BF16).astype(F32)
    rest = value - high
    middle = rest.astype(BF16).astype(F32)
    return high, middle, rest - middle


def in_lanes(columns, rows):
    lane = lax.broadcasted_iota(jnp.int32, (rows, 128), 1)
    out = jnp.zeros((rows, 128), F32)
    for k, column in enumerate(columns):
        out = jnp.where(lane == k, column, out)
    return out


def stacked_rows(rows):
    blank = jnp.zeros((128 - len(rows), 128), F32)
    return jnp.transpose(jnp.concatenate(rows + [blank], 0))


def pack_three(value, count):
    high, middle, low = split_three(value)
    return (high + pltpu.roll(middle, count, 1) + pltpu.roll(low, 2 * count, 1)).astype(BF16)


def sum_three(packed, count):
    return packed + pltpu.roll(packed, 128 - count, 1) + pltpu.roll(packed, 128 - 2 * count, 1)


def one_hot_rows(place_row, base, rows, tokens):
    slot = lax.broadcasted_iota(jnp.int32, (rows, tokens), 0) + base
    return jnp.where(slot == place_row, 1.0, 0.0).astype(BF16)


def one_hot_columns(place_column, rows, slots):
    slot = lax.broadcasted_iota(jnp.int32, (rows, slots), 1)
    return jnp.where(slot == place_column, 1.0, 0.0).astype(BF16)


def tile_rows(tokens):
    if tokens <= 1024:
        return 3 * tokens // 4, tokens // 2
    return 3 * SPAN, 128


def at_once(pairs, most):
    return most if pairs % most == 0 else 1


def aligned(start, rows):
    return pl.ds(pl.multiple_of(start, SPAN), rows)


def forward_kernel(
    heads, mixing, qv_ref, row_ref, column_ref, key_bias_ref, own_bias_ref, pair_row_ref,
    out_ref, spread_ref, mixed_ref, placed_ref, slot_spread_ref, result_ref
):
    this_round, rounds = pl.program_id(0), out_ref.shape[0]
    tokens = qv_ref.shape[0]
    slots = placed_ref.shape[1] - SPAN
    width = heads * HEAD_DIM
    place_rows, token_rows = tile_rows(tokens)
    placed_ref[0, 0:SPAN] = jnp.zeros((SPAN, 3 * width), BF16)

    def place(step, carry):
        base = pl.multiple_of(step * place_rows, place_rows)
        hot = one_hot_rows(row_ref[0], base, place_rows, tokens)
        rows = matmul(hot, qv_ref[...])
        where = pl.ds(pl.multiple_of(base + SPAN, SPAN), place_rows)
        placed_ref[0, where, 0 : 2 * width] = rows.astype(BF16)
        for head in range(heads):
            query = rows[:, head * HEAD_DIM : (head + 1) * HEAD_DIM]
            scale = lax.rsqrt(jnp.mean(query * query, -1, keepdims=True) + 1e-06)
            first = 2 * width + head * HEAD_DIM
            placed_ref[0, where, first : first + HEAD_DIM] = (query * (scale * (1.0 / HEAD_DIM))).astype(BF16)
        return carry

    lax.fori_loop(0, slots // place_rows, place, 0)

    pairs = slots // PAIR
    batch = at_once(pairs, FORWARD_PAIRS)
    lanes_of = [slice(head * HEAD_DIM, (head + 1) * HEAD_DIM) for head in range(heads)]

    def attend(step, carry):
        chains = [(step * batch + part, head) for part in range(batch) for head in range(heads)]
        bias, pair_row = own_bias_ref[...], pair_row_ref[...]
        scores = []
        for pair, head in chains:
            query = placed_ref[0, aligned(pair * PAIR + SPAN, PAIR), lanes_of[head]]
            keys = placed_ref[0, aligned(pair * PAIR, WINDOW), 2 * width + head * HEAD_DIM : 2 * width + (head + 1) * HEAD_DIM]
            left = jnp.concatenate([keys, key_bias_ref[0, pair]], 1)
            right = jnp.concatenate([flipped(query), pair_row], 0)
            scores.append(matmul(left, right) + bias)
        tops = [jnp.max(score, 0, keepdims=True) for score in scores]
        exponents = [jnp.exp(score - top) for score, top in zip(scores, tops)]
        sums = [jnp.sum(exponent, 0, keepdims=True) for exponent in exponents]
        spreads = [top + jnp.log(total) for top, total in zip(tops, sums)]
        for (pair, head), exponent, total in zip(chains, exponents, sums):
            values = placed_ref[0, aligned(pair * PAIR, WINDOW), width + head * HEAD_DIM : width + (head + 1) * HEAD_DIM]
            probability = jnp.transpose(exponent * (1.0 / total)).astype(BF16)
            result_ref[aligned(pair * PAIR, PAIR), lanes_of[head]] = matmul(probability, values).astype(BF16)
        for part in range(batch):
            pair, rows = step * batch + part, spreads[part * heads : (part + 1) * heads]
            slot_spread_ref[0, pair] = jnp.concatenate(rows + [jnp.zeros((8 - heads, 128), F32)], 0)
            terms = [split_three(row) for row in rows]
            packed = stacked_rows([term[k] for k in range(3) for term in terms])
            result_ref[aligned(pair * PAIR, PAIR), width : width + 128] = packed.astype(BF16)
        return carry

    lax.fori_loop(0, pairs // batch, attend, 0)

    def read_back(step, carry):
        where = pl.ds(pl.multiple_of(step * token_rows, token_rows), token_rows)
        hot = one_hot_columns(column_ref[0, where, :], token_rows, slots)
        rows = matmul(hot, result_ref[...])
        out_ref[this_round, where, :] = rows[:, :width].astype(BF16)
        spread_ref[this_round, where, :] = sum_three(rows[:, width:], heads)
        return carry

    lax.fori_loop(0, tokens // token_rows, read_back, 0)

    if mixing:

        @pl.when(this_round == rounds - 1)
        def _():
            def mix(step, carry):
                where = pl.ds(pl.multiple_of(step * 128, 128), 128)
                spreads = [spread_ref[r, where, :] for r in range(rounds)]
                top = functools.reduce(jnp.maximum, spreads)
                weights = [jnp.exp(spread - top) for spread in spreads]
                share = 1.0 / functools.reduce(jnp.add, weights)
                weights = [weight * share for weight in weights]
                for r in range(rounds):
                    spread_ref[r, where, :] = weights[r]
                for head in range(heads):
                    lanes = slice(head * HEAD_DIM, (head + 1) * HEAD_DIM)
                    total = functools.reduce(
                        jnp.add,
                        [
                            weights[r][:, head : head + 1] * out_ref[r, where, lanes].astype(F32)
                            for r in range(rounds)
                        ],
                    )
                    mixed_ref[where, lanes] = total.astype(BF16)
                return carry

            lax.fori_loop(0, tokens // 128, mix, 0)


def backward_kernel(
    heads, mixing, d_mixed_ref, out_ref, weight_ref, dot_ref, placed_ref, slot_spread_ref, row_ref,
    column_ref, key_bias_ref, own_bias_ref, pair_row_ref, total_ref, d_spread_ref, token_grad_ref, slot_grad_ref,
    d_place_ref, sum_ref
):
    if not mixing:
        sum_ref = total_ref
    this_round, rounds = pl.program_id(0), out_ref.shape[0]
    tokens = d_mixed_ref.shape[0]
    slots = placed_ref.shape[1] - SPAN
    width = heads * HEAD_DIM
    place_rows, token_rows = tile_rows(tokens)
    head_lanes = [slice(head * HEAD_DIM, (head + 1) * HEAD_DIM) for head in range(heads)]

    @pl.when(this_round == 0)
    def _():
        sum_ref[...] = jnp.zeros(sum_ref.shape, F32)

        def dots(step, carry):
            where = pl.ds(pl.multiple_of(step * 128, 128), 128)
            inner = []
            for r in range(rounds):
                columns = [
                    jnp.sum(
                        d_mixed_ref[where, lanes].astype(F32) * out_ref[r, where, lanes].astype(F32),
                        -1,
                        keepdims=True,
                    )
                    for lanes in head_lanes
                ]
                inner.append(in_lanes(columns, 128))
            if mixing:
                every = functools.reduce(
                    jnp.add, [weight_ref[r, where, :] * inner[r] for r in range(rounds)]
                )
            else:
                every = dot_ref[where, :]
            for r in range(rounds):
                d_spread_ref[r, where, :] = weight_ref[r, where, :] * (inner[r] - every)
            return carry

        lax.fori_loop(0, tokens // 128, dots, 0)


    def weigh(step, carry):
        where = pl.ds(pl.multiple_of(step * 128, 128), 128)
        for head, lanes in enumerate(head_lanes):
            share = weight_ref[this_round, where, head : head + 1]
            token_grad_ref[where, lanes] = (share * d_mixed_ref[where, lanes].astype(F32)).astype(BF16)
        token_grad_ref[where, width : width + 128] = pack_three(
            d_spread_ref[this_round, where, :], heads
        )
        return carry

    lax.fori_loop(0, tokens // 128, weigh, 0)

    def place(step, carry):
        base = pl.multiple_of(step * place_rows, place_rows)
        hot = one_hot_rows(row_ref[0], base, place_rows, tokens)
        slot_grad_ref[pl.ds(base, place_rows), :] = matmul(
            hot, token_grad_ref[...]
        ).astype(BF16)
        return carry

    lax.fori_loop(0, slots // place_rows, place, 0)

    pairs = slots // PAIR
    batch = at_once(pairs, BACKWARD_PAIRS)

    def finish(start, rows, head, d_query, d_unit, d_value):
        here = aligned(start + SPAN, rows)
        query = placed_ref[0, here, head_lanes[head]].astype(F32)
        scale = lax.rsqrt(jnp.mean(query * query, -1, keepdims=True) + 1e-06)
        inner = jnp.mean(d_unit * query, -1, keepdims=True)
        factor = scale * (1.0 / HEAD_DIM)
        d_query = d_query + factor * d_unit - query * (factor * scale * scale * inner)
        d_place_ref[here, head_lanes[head]] = d_query.astype(BF16)
        d_place_ref[here, width + head * HEAD_DIM : width + (head + 1) * HEAD_DIM] = d_value.astype(BF16)

    def attend(step, carry):
        chains = [(step * batch + part, head) for part in range(batch) for head in range(heads)]
        bias, pair_row = own_bias_ref[...], pair_row_ref[...]
        d_spread_rows = []
        for part in range(batch):
            packed = slot_grad_ref[aligned((step * batch + part) * PAIR, PAIR), width : width + 128]
            rows = jnp.transpose(packed.astype(F32))
            d_spread_rows += [
                rows[head : head + 1]
                + rows[heads + head : heads + head + 1]
                + rows[2 * heads + head : 2 * heads + head + 1]
                for head in range(heads)
            ]
        scores, d_probs = [], []
        for pair, head in chains:
            query = placed_ref[0, aligned(pair * PAIR + SPAN, PAIR), head_lanes[head]]
            keys = placed_ref[0, aligned(pair * PAIR, WINDOW), 2 * width + head * HEAD_DIM : 2 * width + (head + 1) * HEAD_DIM]
            values = placed_ref[0, aligned(pair * PAIR, WINDOW), width + head * HEAD_DIM : width + (head + 1) * HEAD_DIM]
            left = jnp.concatenate([keys, key_bias_ref[0, pair]], 1)
            right = jnp.concatenate([flipped(query), pair_row], 0)
            scores.append(matmul(left, right) + bias)
            d_out = slot_grad_ref[aligned(pair * PAIR, PAIR), head_lanes[head]]
            d_probs.append(matmul(values, flipped(d_out)))
        probs = [
            jnp.exp(score - slot_spread_ref[0, pair, head : head + 1, :])
            for (pair, head), score in zip(chains, scores)
        ]
        dots = [jnp.sum(p * d, 0, keepdims=True) for p, d in zip(probs, d_probs)]
        d_scores = [
            p * (d + (row - dot)) for p, d, row, dot in zip(probs, d_probs, d_spread_rows, dots)
        ]
        last = list(carry)
        for (pair, head), p, d in zip(chains, probs, d_scores):
            query = placed_ref[0, aligned(pair * PAIR + SPAN, PAIR), head_lanes[head]]
            keys = placed_ref[0, aligned(pair * PAIR, WINDOW), 2 * width + head * HEAD_DIM : 2 * width + (head + 1) * HEAD_DIM]
            d_out = slot_grad_ref[aligned(pair * PAIR, PAIR), head_lanes[head]]
            d_query = matmul(jnp.transpose(d).astype(BF16), keys)
            d_keys = matmul(d.astype(BF16), query)
            d_values = matmul(p.astype(BF16), d_out)
            last_query, last_key, last_value = last[head]

            before = pair * PAIR - SPAN
            finish(before, SPAN, head, last_query, last_key + d_keys[:SPAN], last_value + d_values[:SPAN])
            finish(pair * PAIR, SPAN, head, d_query[:SPAN], d_keys[SPAN:PAIR], d_values[SPAN:PAIR])
            last[head] = (d_query[SPAN:], d_keys[PAIR:], d_values[PAIR:])
        return tuple(last)

    blank = jnp.zeros((SPAN, HEAD_DIM), F32)
    carry = lax.fori_loop(
        0, pairs // batch, attend, tuple((blank, blank, blank) for _ in range(heads))
    )
    for head in range(heads):
        finish(slots - SPAN, SPAN, head, *carry[head])

    def read_back(step, carry):
        where = pl.ds(pl.multiple_of(step * token_rows, token_rows), token_rows)
        hot = one_hot_columns(column_ref[0, where, :], token_rows, slots)
        sum_ref[where, :] += matmul(hot, d_place_ref[SPAN:, :])
        return carry

    lax.fori_loop(0, tokens // token_rows, read_back, 0)

    if mixing:

        @pl.when(this_round == rounds - 1)
        def _():
            total_ref[...] = sum_ref[...].astype(BF16)


def per_round(shape, buffers):
    rest = (0,) * (len(shape) - 1)
    return pl.BlockSpec((1,) + shape[1:], lambda r: (r,) + rest, pipeline_mode=pl.Buffered(buffers))


def whole(shape):
    return pl.BlockSpec(shape, lambda r: (0,) * len(shape), pipeline_mode=pl.Buffered(1))


def attention_forward(qv, places, key_bias, mixing):
    row, column = places
    rounds, _, tokens = row.shape
    slots = key_bias.shape[1] * PAIR
    width = qv.shape[1] // 2
    heads = width // HEAD_DIM
    buffers = min(2, rounds)
    bias, pair_row = own_bias(), pair_rows()
    kept = [
        jax.ShapeDtypeStruct((rounds, tokens, width), BF16),
        jax.ShapeDtypeStruct((rounds, tokens, 128), F32),
        jax.ShapeDtypeStruct((tokens if mixing else 8, width), BF16),
    ]
    outs = [
        jax.ShapeDtypeStruct((rounds, slots + SPAN, 3 * width), BF16),
        jax.ShapeDtypeStruct((rounds, slots // PAIR, 8, PAIR), F32),
    ]
    flops = rounds * slots * (2 * tokens * (3 * width + 128) + 4 * width * WINDOW)
    return pl.pallas_call(
        functools.partial(forward_kernel, heads, mixing),
        grid=(rounds,),
        in_specs=[whole(qv.shape)]
        + [per_round(x.shape, buffers) for x in (row, column, key_bias)]
        + [whole(bias.shape), whole(pair_row.shape)],
        out_specs=[whole(x.shape) for x in kept] + [per_round(x.shape, buffers) for x in outs],
        out_shape=kept + outs,
        scratch_shapes=[pltpu.VMEM((slots, width + 128), BF16)],
        compiler_params=pltpu.CompilerParams(vmem_limit_bytes=56 * 1024 * 1024),
        cost_estimate=pl.CostEstimate(flops=flops, bytes_accessed=20 << 20, transcendentals=0),
    )(qv, row, column, key_bias, bias, pair_row)


def attention_backward(d_mixed, round_out, weights, all_dot, placed, slot_spread, places, key_bias):
    row, column = places
    rounds, _, tokens = row.shape
    slots = placed.shape[1] - SPAN
    width = placed.shape[2] // 3
    heads = width // HEAD_DIM
    buffers = min(2, rounds)
    bias, pair_row = own_bias(), pair_rows()
    mixing = all_dot is None
    if mixing:
        all_dot = jnp.zeros((8, 128), F32)
    flops = rounds * slots * (2 * tokens * (3 * width + 128) + 10 * width * WINDOW)
    return pl.pallas_call(
        functools.partial(backward_kernel, heads, mixing),
        grid=(rounds,),
        in_specs=[whole(x.shape) for x in (d_mixed, round_out, weights, all_dot)]
        + [per_round(x.shape, buffers) for x in (placed, slot_spread, row, column, key_bias)]
        + [whole(bias.shape), whole(pair_row.shape)],
        out_specs=whole((tokens, 2 * width)),
        out_shape=jax.ShapeDtypeStruct((tokens, 2 * width), BF16 if mixing else F32),
        scratch_shapes=[
            pltpu.VMEM((rounds, tokens, 128), F32),
            pltpu.VMEM((tokens, width + 128), BF16),
            pltpu.VMEM((slots, width + 128), BF16),
            pltpu.VMEM((slots + SPAN, 2 * width), BF16),
            pltpu.VMEM((tokens if mixing else 8, 2 * width), F32),
        ],
        compiler_params=pltpu.CompilerParams(vmem_limit_bytes=60 * 1024 * 1024),
        cost_estimate=pl.CostEstimate(flops=flops, bytes_accessed=20 << 20, transcendentals=0),
    )(d_mixed, round_out, weights, all_dot, placed, slot_spread, row, column, key_bias, bias, pair_row)


def local(
    stream_one,
    stream_two,
    slot_place,
    bucket_ids,
    grad_one,
    grad_two,
    norm1_gain,
    norm1_bias,
    w_query_key,
    w_value,
    w_output,
    norm2_gain,
    norm2_bias,
    w_inner,
    inner_bias,
    w_outer,
    outer_bias,
):
    chips, devices = lax.axis_size("chip"), lax.axis_size("seq")
    batch, tok, features = stream_one.shape
    rounds = slot_place.shape[1]
    sequences = 2 * batch
    tokens = devices * tok
    slots = 3 * tokens // 2
    own_rows = batch * tok
    width = features // (2 * chips)
    heads = width // HEAD_DIM
    hidden_units = w_inner.shape[1]
    quarter = hidden_units // (2 * chips)
    units = sequences * chips
    sharing = devices // units
    mixing = sharing == 1
    own_rounds = rounds // sharing
    shard = w_query_key.shape[0]
    core, chip = lax.axis_index("core"), lax.axis_index("chip")

    def by_core(own, other):
        return jnp.where(core == 0, jnp.stack([own, other]), jnp.stack([other, own]))

    def flip(block):
        return exchange(block, "chip", 1)

    def both_chips(block):
        return ordered(block, flip(block), "chip", 1) if chips == 2 else block[None]

    def trade_quarters(pieces):
        if chips == 2:
            kept, sent = pick(pieces, chip, 0), pick(pieces, 1 - chip, 0)
            pieces = ordered(kept, flip(sent), "chip", 1)
        return jnp.swapaxes(by_core(pick(pieces, core, 1), swap(pick(pieces, 1 - core, 1))), 0, 1)

    seq_steps, chip_steps = half_steps("seq"), half_steps("chip")
    mid_steps = seq_steps[1:-1]
    gather_orders = [
        seq_steps[:1] + seq_steps[-1:] + mid_steps + chip_steps,
        chip_steps + seq_steps[:1] + seq_steps[-1:] + mid_steps,
    ]
    scatter_orders = [
        chip_steps + seq_steps[-1:] + mid_steps + seq_steps[:1],
        mid_steps + chip_steps + seq_steps[-1:] + seq_steps[:1],
    ]

    base = 64
    meta = jnp.stack([slot_place // base, slot_place % base, bucket_ids + 1], 1).astype(BF16)
    small = [norm1_gain, norm1_bias, norm2_gain, norm2_bias, outer_bias]
    small = jnp.concatenate([jnp.concatenate(small), inner_bias, meta.reshape(-1)])

    key_split = w_query_key.reshape(shard, chips, 2, width)
    value_split = w_value.reshape(shard, chips, 2, width)
    joined_split = jnp.concatenate([key_split, value_split], 3)
    joined_own, joined_sent = pick(joined_split, core, 2), pick(joined_split, 1 - core, 2)
    streams, joined_got, small_other = lax.optimization_barrier(
        (stream_two.reshape(own_rows, features), swap(joined_sent), swap(small))
    )
    joined_both = by_core(joined_own, joined_got)
    chains = [Gather(joined_both[:, :, pair]) for pair in range(chips)]
    small = Stack(by_core(small, small_other))
    small_steps = mid_steps + seq_steps[:1] + seq_steps[-1:]
    for k in range(len(seq_steps) + len(chip_steps)):
        for pair, chain in enumerate(chains):
            chain.step(gather_orders[pair % 2][k])
        if k < len(small_steps):
            small.step(small_steps[k])
            together(chains + [small])
            if k == len(small_steps) - 1:
                split = small.held.reshape([2] * len(small_steps) + list(small.held.shape[-2:]))
                taken = small_steps[::-1]
                split = jnp.transpose(
                    split,
                    [taken.index(step) for step in seq_steps] + [split.ndim - 2, split.ndim - 1],
                ).reshape(devices, 2, -1)
                vectors = Stack(jnp.swapaxes(split[:, :, : 5 * shard], 0, 1))
                cut = 5 * shard + inner_bias.shape[0]
                quarter_bias = pick(split[:, :, 5 * shard : cut], core, 1).reshape(-1).astype(F32)
                meta = split[:, :, cut:].reshape(devices, 2, batch, 3, rounds, tok)
                for step in chip_steps:
                    vectors.step(step)
    joined = [chain.held.reshape(features, 2 * width) for chain in chains]
    vectors = jnp.moveaxis(vectors.held.reshape(-1, 5, shard), 1, 0).reshape(5, features).astype(F32)
    gain_one, bias_one, gain_two, bias_two, full_outer_bias = [vectors[k] for k in range(5)]

    inner_pieces = jnp.moveaxis(w_inner.reshape(shard, chips, 2, quarter), 0, 2)
    inner_pieces = trade_quarters(inner_pieces).reshape(-1, features)
    output_pieces = both_chips(w_output).reshape(-1, features)
    bundle = jnp.concatenate([w_outer, inner_pieces, output_pieces], 0)
    bundle, *joined = lax.optimization_barrier([bundle] + joined)
    cuts = [w_outer.shape[0], w_outer.shape[0] + inner_pieces.shape[0]]
    gathered = lax.all_gather(bundle, "seq", axis=0, tiled=False)
    full_outer = gathered[:, : cuts[0]].reshape(quarter, features)
    full_inner = gathered[:, cuts[0] : cuts[1]].reshape(devices, 2 * chips, shard, quarter)
    full_inner = jnp.swapaxes(full_inner, 0, 1).reshape(features, quarter)
    full_output = gathered[:, cuts[1] :].reshape(devices, chips, shard, features)
    full_output = jnp.swapaxes(full_output, 0, 1).reshape(chips * width, features)

    unit = lax.axis_index("seq") // sharing
    sequence = unit // chips
    owner = jnp.where(sequence < batch, core, 1 - core)
    meta = lax.dynamic_slice(
        meta,
        (0, owner, sequence % batch, 0, lax.axis_index("seq") % sharing * own_rounds, 0),
        (devices, 1, 1, 3, own_rounds, tok),
    )
    meta = jnp.moveaxis(meta.reshape(devices, 3, own_rounds, tok), 0, 2)
    meta = meta.reshape(3, own_rounds, tokens).astype(jnp.int32)
    token_place, token_tag = meta[0] * base + meta[1], meta[2]
    found = token_place[:, :, None] == jnp.arange(slots)[None, None, :]
    slot_tag = jnp.sum(jnp.where(found, token_tag[:, :, None], 0), 1)
    slot_tag = jnp.pad(slot_tag.reshape(own_rounds, slots // SPAN, SPAN), ((0, 0), (1, 0), (0, 0)))
    span_tag = jnp.max(slot_tag, 2, keepdims=True)
    first, second, third = slot_tag[:, :-2:2], slot_tag[:, 1:-1:2], slot_tag[:, 2::2]
    unmet = jnp.full(first.shape, False)
    met = jnp.stack(
        [
            jnp.concatenate([first == span_tag[:, 1:-1:2], second == span_tag[:, 1:-1:2], unmet], 2),
            jnp.concatenate([unmet, second == span_tag[:, 2::2], third == span_tag[:, 2::2]], 2),
        ],
        3,
    )
    key_bias = jnp.where(met, 0.0, -1e9).astype(BF16)
    key_bias = jnp.pad(key_bias, ((0, 0), (0, 0), (0, 0), (0, HEAD_DIM - 2)))
    places = (token_place[:, None, :], token_place[:, :, None])

    def near(value):
        return jnp.concatenate([value, swap(value)], 0)

    def far(value):
        return near(flip(value))

    def everywhere(value):
        return jnp.concatenate([near(value), far(value)], 0) if chips == 2 else near(value)

    stream_a = stream_one.astype(F32).reshape(own_rows, features)
    stream_b = streams.astype(F32)
    normed_one, unit_one, scale_one = norm_parts(near(streams).astype(F32), gain_one, bias_one)
    hidden = normed_one.astype(BF16)
    unit_one, scale_one = unit_one[:own_rows], scale_one[:own_rows]
    projected = [matmul(hidden, weight).astype(BF16) for weight in joined]

    def to_attention(pairs):
        value = jnp.stack([pair.reshape(sequences, tok, -1) for pair in pairs], 1)
        value = jnp.broadcast_to(value[:, :, None], value.shape[:2] + (sharing,) + value.shape[2:])
        return all_to_all(value.reshape(devices, tok, -1)).reshape(tokens, -1)

    def from_attention(value):
        value = all_to_all(value.reshape(devices, tok, -1))
        value = value.reshape(sequences, chips, sharing, tok, -1)
        return [value[:, pair, 0].reshape(sequences * tok, -1) for pair in range(chips)]

    round_out, weights, mixed, placed, slot_spread = attention_forward(
        to_attention(projected), places, key_bias, mixing
    )
    if not mixing:
        top = group_max(jnp.max(weights, 0), sharing)
        weights = jnp.exp(weights - top)
        weights = weights / group_sum(jnp.sum(weights, 0), sharing)
        by_head = round_out.reshape(own_rounds, tokens, heads, HEAD_DIM)
        mixed = group_sum(jnp.sum(weights[:, :, :heads, None] * by_head, 0), sharing)
        mixed = mixed.reshape(tokens, width).astype(BF16)
    mixed = jnp.concatenate(from_attention(mixed), 1)

    def core_sum(value):
        return value[:own_rows] + swap(value[own_rows:])

    out_one = stream_a + core_sum(matmul(mixed, full_output))
    normed_two, unit_two, scale_two = norm_parts(out_one, gain_two, bias_two)
    inner_low = normed_two.astype(BF16)
    cot_own = grad_two.reshape(own_rows, features)

    def feed_forward(value, cotangent):
        pre_act = matmul(value, full_inner) + quarter_bias
        activated, gelu_pull = jax.vjp(jax.nn.gelu, pre_act)
        act_low = activated.astype(BF16)
        d_act = matmul_right(cotangent, full_outer)
        d_pre = gelu_pull(d_act)[0].astype(BF16)
        return act_low, d_pre, matmul(act_low, full_outer), matmul_right(d_pre, full_inner)

    parts = [(near(inner_low), near(cot_own))]
    if chips == 2:
        parts.append((far(inner_low), far(cot_own)))
    done = [feed_forward(*part) for part in parts]
    rows_in, rows_cot = [jnp.concatenate([part[k] for part in parts], 0) for k in range(2)]
    act_low, d_pre = [jnp.concatenate([part[k] for part in done], 0) for k in range(2)]

    def quarter_sum(values):
        total = core_sum(values[0])
        if chips == 2:
            total = total + flip(core_sum(values[1]).astype(BF16)).astype(F32)
        return total

    d_normed_two = quarter_sum([part[3] for part in done])
    d_from_two, grad_gain_two, grad_bias_two = norm_back(
        d_normed_two, unit_two, scale_two, gain_two
    )
    back_one = grad_one.astype(F32).reshape(own_rows, features) + d_from_two
    out_two = stream_b + quarter_sum([part[2] for part in done]) + full_outer_bias

    d_attended = near(back_one.astype(BF16))
    d_mixed = matmul_right(d_attended, full_output).astype(BF16)
    d_mixed = to_attention([d_mixed[:, p * width : (p + 1) * width] for p in range(chips)])

    grad_outer = matmul_left(act_low, rows_cot).astype(BF16)
    grad_inner = matmul_left(rows_in, d_pre).astype(BF16)
    grad_output = matmul_left(mixed, d_attended).astype(BF16)
    grad_inner = jnp.swapaxes(grad_inner.reshape(2 * chips, devices, shard, quarter), 0, 1)
    grad_output = jnp.swapaxes(grad_output.reshape(chips, devices, shard, features), 0, 1)
    summed = jnp.concatenate(
        [
            grad_outer.reshape(devices, -1, features),
            grad_inner.reshape(devices, -1, features),
            grad_output.reshape(devices, -1, features),
        ],
        1,
    )
    summed, d_mixed = lax.optimization_barrier((summed, d_mixed))
    summed = lax.psum_scatter(summed, "seq", scatter_dimension=0, tiled=True)[0]
    quarter_bias_grad = jnp.sum(d_pre.astype(F32), 0).reshape(devices, -1)

    all_dot = None
    if not mixing:
        inner = d_mixed.reshape(1, tokens, heads, HEAD_DIM).astype(F32) * by_head
        inner = jnp.sum(weights[:, :, :heads] * jnp.sum(inner, -1), 0)
        all_dot = jnp.pad(group_sum(inner, sharing), ((0, 0), (0, 128 - heads)))
    d_total = attention_backward(
        d_mixed, round_out, weights, all_dot, placed, slot_spread, places, key_bias
    )
    if not mixing:
        d_total = group_sum(d_total, sharing).astype(BF16)
    d_projected = from_attention(d_total)

    chains = []
    for pair in range(chips):
        grad = matmul_left(hidden, d_projected[pair])
        chains.append(Scatter(grad.reshape(chips, 2, devices, shard, 2 * width)))
    orders = list(zip(*[scatter_orders[pair % 2] for pair in range(chips)]))
    for chain, step in zip(chains, orders[0]):
        chain.step(step)
    d_hidden = core_sum(
        functools.reduce(jnp.add, [matmul_right(d, w) for d, w in zip(d_projected, joined)])
    )
    d_from_one, grad_gain_one, grad_bias_one = norm_back(d_hidden, unit_one, scale_one, gain_one)
    back_two = cot_own.astype(F32) + d_from_one
    small_grads = jnp.stack(
        [grad_gain_one, grad_bias_one, grad_gain_two, grad_bias_two, jnp.sum(cot_own.astype(F32), 0)]
    )
    small_grads = jnp.swapaxes(small_grads.reshape(5, 2 * chips * devices, shard), 0, 1)
    small_grads = Halve(small_grads.reshape(-1, 5 * shard))
    small_steps = chip_steps + [("core", 1)] + seq_steps
    reduced = Stack(summed)
    for k in range(max(len(orders) - 1, len(small_steps))):
        together(chains + [small_grads] + [reduced] * (k == 0))
        if k + 1 < len(orders):
            for chain, step in zip(chains, orders[k + 1]):
                chain.step(step)
        elif k + 1 == len(orders):
            grad_joined = jnp.stack([chain.held for chain in chains], 1)
            grad_joined = by_core(pick(grad_joined, core, 0), swap(pick(grad_joined, 1 - core, 0)))
        if small_steps[k][0] == "seq" and small_grads.held.shape[1] == 5 * shard:
            small_grads.held = jnp.concatenate([small_grads.held, quarter_bias_grad], 1)
        small_grads.step(small_steps[k])
    summed = reduced.held
    grad_outer = summed[: cuts[0]].astype(F32)
    grad_inner = trade_quarters(summed[cuts[0] : cuts[1]].reshape(chips, 2, shard, quarter))
    grad_inner = jnp.moveaxis(grad_inner, 2, 0).reshape(shard, hidden_units).astype(F32)
    grad_output = summed[cuts[1] :].reshape(chips, shard, features)
    if chips == 2:
        other = flip(pick(grad_output, 1 - chip, 0)).astype(F32)
        grad_output = pick(grad_output, chip, 0).astype(F32) + other
    else:
        grad_output = grad_output[0].astype(F32)
    small_grads, grad_inner_bias = (
        small_grads.held[0, : 5 * shard].reshape(5, shard), small_grads.held[0, 5 * shard :]
    )
    grad_joined = grad_joined.reshape(2, chips, shard, 2, width)
    grad_joined = jnp.transpose(grad_joined, (3, 2, 1, 0, 4)).reshape(2, shard, features)
    out_shape = (batch, tok, features)
    return (
        out_one.reshape(out_shape),
        out_two.reshape(out_shape),
        back_one.reshape(out_shape),
        back_two.reshape(out_shape),
        small_grads[0],
        small_grads[1],
        grad_joined[0],
        grad_joined[1],
        grad_output,
        small_grads[2],
        small_grads[3],
        grad_inner,
        grad_inner_bias,
        grad_outer,
        small_grads[4],
    )


def solution(mesh):
    split = Mesh(
        mesh.devices.reshape(mesh.shape["dp"] // 2, 2, mesh.shape["seq"]), ("chip", "core", "seq")
    )
    dp = ("chip", "core")
    every = ("chip", "core", "seq")
    stream, meta, vector, matrix = (
        P(dp, "seq", None), P(dp, None, "seq"), P(every), P(every, None)
    )
    return jax.shard_map(
        local,
        mesh=split,
        in_specs=(
            stream, stream, meta, meta, stream, stream,
            vector, vector, matrix, matrix, matrix, vector, vector, matrix, vector, matrix, vector,
        ),
        out_specs=(
            stream, stream, stream, stream,
            vector, vector, matrix, matrix, matrix, vector, vector, matrix, vector, matrix, vector,
        ),
        check_vma=False,
    )
```

time: 615 us -> 438 us (0.71)
  waiting for transfers between devices: 220 us -> 145 us
  Pallas kernels: 118 us -> 76.8 us
  local copies, waits for them, and re-layouts: 70.6 us -> 47.5 us
  other arithmetic: 47.5 us -> 33.5 us
  starting transfers between devices: 62 us -> 53.1 us
  matrix products: 42.7 us -> 34.4 us
  blocking collectives: 31.5 us -> 24.8 us
    ppermute x26 -> x33, waiting for transfers between devices: 167 us -> 87.9 us  [exchange(): return lax.ppermute(block, axis, [(i, i ^ bit) for i in range(size)])]
    pallas_call x2, Pallas kernels: 118 us -> 76.8 us  [the longest x1 41.9 us: attention_backward(): pl.pallas_call(functools.partial(backward_kernel, heads, mixing), grid=(r...]
    mul x2 -> x0, local copies, waits for them, and re-layouts: 12.9 us -> none  [local(): mixed = group_sum(jnp.sum(mix_weights[..., None] * round_heads, 0), sharing)]
    reduce_scatter x3 -> x1, waiting for transfers between devices: 0.06 us -> 11.9 us  [local(): summed = lax.psum_scatter(summed, 'seq', scatter_dimension=0, tiled=True)[0]]
    reduce_sum x5 -> x2, other arithmetic: 15.2 us -> 4.21 us  [the longest x1 3.86 us: local(): slot_tag = jnp.sum(jnp.where(found, token_tag[:, :, None], 0), 1)]
    slice x5 -> x20, local copies, waits for them, and re-layouts: 0.72 us -> 8.72 us  [the longest x1 2.7 us: local(): full_outer = gathered[:, :cuts[0]].reshape(quarter, features)]
    ppermute x26 -> x33, starting transfers between devices: 44.3 us -> 37.2 us  [exchange(): return lax.ppermute(block, axis, [(i, i ^ bit) for i in range(size)])]
    ppermute x13 -> x17, waiting for transfers between devices: 8.9 us -> 2.12 us  [swap(): return lax.ppermute(block, 'core', CORE_SWAP)]
  transfers between devices with their start and end apart: 49 -> 55, of which waited for: 26 -> 29; matrix products, arithmetic and copies ran while one was open for 22% -> 22% of each run, Pallas kernels for 19% -> 18%
where the time goes in v2:
time: 438 us; the launch traced here: 431 us
  waiting for transfers between devices  145 us (33%)
  Pallas kernels  76.8 us (18%)
  starting transfers between devices  53.1 us (12%)
  local copies, waits for them, and re-layouts  47.5 us (11%)
  matrix products  34.4 us (8%)
  other arithmetic  33.5 us (8%)
  blocking collectives  24.8 us (6%)
  between operations  15.8 us (4%)
    ppermute x33, waiting for transfers between devices, exchange(): return lax.ppermute(block, axis, [(i, i ^ bit) for i in range(size)])  87.9 us
    all_to_all x3, waiting for transfers between devices, all_to_all(): return lax.all_to_all(block, 'seq', split_axis=0, concat_axis=0, tiled=True)  43 us
    pallas_call x1, Pallas kernels, attention_backward(): pl.pallas_call(functools.partial(backward_kernel, heads, mixing), grid=(r...  41.9 us
    ppermute x33, starting transfers between devices, exchange(): return lax.ppermute(block, axis, [(i, i ^ bit) for i in range(size)])  37.2 us
    pallas_call x1, Pallas kernels, attention_forward(): pl.pallas_call(functools.partial(forward_kernel, heads, mixing), grid=(ro...  34.9 us
    all_to_all x1, blocking collectives, all_to_all(): return lax.all_to_all(block, 'seq', split_axis=0, concat_axis=0, tiled=True)  24.8 us
    all_to_all x3, starting transfers between devices, all_to_all(): return lax.all_to_all(block, 'seq', split_axis=0, concat_axis=0, tiled=True)  13.2 us
    dot_general x7, matrix products, matmul(): return jnp.dot(left, right, preferred_element_type=F32)  12.6 us
  transfers between devices with their start and end apart: 55, of which 29 were waited for; matrix products, arithmetic and copies ran while one was open for 22% of the time, Pallas kernels for 18%

profile of v2, /device:TPU:0, one launch (start us, length us, event | category | flops | bytes accessed | tf_op | source)
XLA Modules:
  0.0 431.1 jit_solution(11181088949645527198)
XLA Ops:
  10.7 4.1 concatenate.79
  42.2 3.8 collective-permute-done.10
  54.2 5.2 %collective-permute-done.17 = bf16[2,2,2,1,2,32,512]{6,5,4,3,2,1,0:T(8,128)(2,1)} collective-permute-done((bf16[2,2,2,1,2,32,512]{6,5,4,3,2,1,0:T(8,128)(2,1)}, bf16[2,2,2,1,2,32,512]{6,5,4,3,2,1,0:T(8,128)(2,1)}, u32[]{:S(2)}, u32[]{:S(2)}) %collective-permute-start.17) | collective-permute-done | bytes 524320 | tf_op jit(solution)/shard_map/ppermute | solution.py:62
  61.7 3.6 collective-permute-done.12
  71.4 4.7 %all-to-all-start = ((bf16[8,128,512]{2,1,0:T(8,128)(2,1)}), bf16[8,128,512]{2,1,0:T(8,128)(2,1)}, u32[]{:S(2)}, u32[]{:S(2)}) async-start(bf16[8,128,512]{2,1,0:T(8,128)(2,1)} %bitcast.41), calls=%async_computation | async-start | bytes 2097152 | tf_op jit(solution)/shard_map/all_to_all | solution.py:138
  77.1 3.9 select_reduce_fusion
  88.9 26.5 %all-to-all-done = bf16[8,128,512]{2,1,0:T(8,128)(2,1)} async-done(((bf16[8,128,512]{2,1,0:T(8,128)(2,1)}), bf16[8,128,512]{2,1,0:T(8,128)(2,1)}, u32[]{:S(2)}, u32[]{:S(2)}) %all-to-all-start) | async-done | bytes 1048608 | tf_op jit(solution)/shard_map/all_to_all | solution.py:138
  115.4 34.9 %shard_map.280 = (bf16[4,1024,256]{2,1,0:T(8,128)(2,1)}, f32[4,1024,128]{2,1,0:T(8,128)}, bf16[1024,256]{1,0:T(8,128)(2,1)}, bf16[4,1600,768]{2,1,0:T(8,128)(2,1)}, f32[4,12,8,128]{3,2,1,0:T(8,128)}) custom-call(bf16[1024,512]{1,0:T(8,128)(2,1)} %bitcast.42.qv_ref, s32[4,1,1024]{2,1,0:T(1,128)} %bitcast.379, s32[4,1024,1]{2,1,0:T(8,128)} %copy.248.column_ref, ...), custom_call_target="tpu_custom_call" | custom-call | flops 12482248704 | bytes 20971520 | tf_op jit(solution)/shard_map/pallas_call | solution.py:500
  150.3 24.8 %all_to_all.20 = bf16[8,128,256]{2,1,0:T(8,128)(2,1)S(1)} all-to-all(bf16[8,128,256]{2,1,0:T(8,128)(2,1)} %bitcast.335), channel_id=1, replica_groups=mesh['chip'=2,'core'=2,'seq'=8] {'seq'}, dimensions={0} | all-to-all | bytes 1048576 | tf_op jit(solution)/shard_map/all_to_all | solution.py:138
  186.4 7.7 %collective-permute-done.27 = bf16[256,1024]{1,0:T(8,128)(2,1)} collective-permute-done((bf16[256,1024]{1,0:T(8,128)(2,1)}, bf16[256,1024]{1,0:T(8,128)(2,1)}, u32[]{:S(2)}, u32[]{:S(2)}) %collective-permute-start.27) | collective-permute-done | bytes 524320 | tf_op jit(solution)/shard_map/ppermute | solution.py:62
  194.1 10.7 %collective-permute-done.21 = bf16[256,1024]{1,0:T(8,128)(2,1)S(1)} collective-permute-done((bf16[256,1024]{1,0:T(8,128)(2,1)S(1)}, bf16[256,1024]{1,0:T(8,128)(2,1)S(1)}, u32[]{:S(2)}, u32[]{:S(2)}) %collective-permute-start.21) | collective-permute-done | bytes 524320 | tf_op jit(solution)/shard_map/ppermute | solution.py:62
  212.5 3.7 fusion.16
  218.1 3.7 fusion.9
  226.4 11.9 %collective-permute-done.30 = bf16[256,1024]{1,0:T(8,128)(2,1)S(1)} collective-permute-done((bf16[256,1024]{1,0:T(8,128)(2,1)S(1)}, bf16[256,1024]{1,0:T(8,128)(2,1)S(1)}, u32[]{:S(2)}, u32[]{:S(2)}) %collective-permute-start.30) | collective-permute-done | bytes 524320 | tf_op jit(solution)/shard_map/ppermute | solution.py:62
  245.8 4.1 all-to-all-start.2
  250.1 4.6 %fusion.39 = bf16[1024,1024]{1,0:T(8,128)(2,1)S(1)} fusion(bf16[256,1024]{1,0:T(8,128)(2,1)} %copy-done.34, bf16[256,1024]{1,0:T(8,128)(2,1)} %collective-permute-done.27, bf16[256,1024]{1,0:T(8,128)(2,1)} %copy-done.33, bf16[256,1024]{1,0:T(8,128)(2,1)} %bitcast.71, bf16[512,1024]{1,0:T(8,128)(2,1)} %get-tuple-element.142, ...), kind=kOutput, calls=%fused_computation.51 | convolution fusion | flops 2161115136 | bytes 6291456 | tf_op jit(solution)/shard_map/dot_general | solution.py:27
  258.7 6.7 %all-to-all-done.2 = bf16[8,128,256]{2,1,0:T(8,128)(2,1)} async-done(((bf16[8,128,256]{2,1,0:T(8,128)(2,1)}), bf16[8,128,256]{2,1,0:T(8,128)(2,1)}, u32[]{:S(2)}, u32[]{:S(2)}) %all-to-all-start.2) | async-done | bytes 524320 | tf_op jit(solution)/shard_map/all_to_all | solution.py:138
  266.1 41.9 %shard_map.281 = bf16[1024,512]{1,0:T(8,128)(2,1)} custom-call(bf16[1024,256]{1,0:T(8,128)(2,1)} %bitcast.83.d_mixed_ref, bf16[4,1024,256]{2,1,0:T(8,128)(2,1)} %get-tuple-element.68.out_ref, f32[4,1024,128]{2,1,0:T(8,128)} %get-tuple-element.69.weight_ref, f32[8,128]{1,0:T(8,128)} %broadcast_in_dim.72.dot_ref, ...), custom_call_target="tpu_custom_call" | custom-call | flops 14294188032 | bytes 20971520 | tf_op jit(solution)/shard_map/pallas_call | solution.py:526
  308.0 4.4 %all-to-all-start.3 = ((bf16[8,128,512]{2,1,0:T(8,128)(2,1)}), bf16[8,128,512]{2,1,0:T(8,128)(2,1)}, u32[]{:S(2)}, u32[]{:S(2)}) async-start(bf16[8,128,512]{2,1,0:T(8,128)(2,1)} %bitcast.326), calls=%async_computation.3 | async-start | bytes 2097152 | tf_op jit(solution)/shard_map/all_to_all | solution.py:138
  329.9 9.8 %all-to-all-done.3 = bf16[8,128,512]{2,1,0:T(8,128)(2,1)} async-done(((bf16[8,128,512]{2,1,0:T(8,128)(2,1)}), bf16[8,128,512]{2,1,0:T(8,128)(2,1)}, u32[]{:S(2)}, u32[]{:S(2)}) %all-to-all-start.3) | async-done | bytes 1048608 | tf_op jit(solution)/shard_map/all_to_all | solution.py:138
  348.6 14.5 %collective-permute-done.34 = bf16[2,2,2,2,32,512]{5,4,1,2,3,0:T(8,128)(2,1)S(1)} collective-permute-done((bf16[2,2,2,2,32,512]{5,4,1,2,3,0:T(8,128)(2,1)S(1)}, bf16[2,2,2,2,32,512]{5,4,1,2,3,0:T(8,128)(2,1)S(1)}, u32[]{:S(2)}, u32[]{:S(2)}) %collective-permute-start.34) | collective-permute-done | bytes 524320 | tf_op jit(solution)/shard_map/ppermute | solution.py:62
  368.6 11.9 %reduce-scatter.2.cloned.1.call-done = bf16[1,320,1024]{2,1,0:T(8,128)(2,1)} async-done(((bf16[8,320,1024]{2,1,0:T(8,128)(2,1)}), bf16[1,320,1024]{2,1,0:T(8,128)(2,1)}) %reduce-scatter.2.cloned.1.call-update) | async-done | bytes 655376 | tf_op jit(solution)/shard_map/reduce_scatter | solution.py:781
  398.5 4.2 collective-permute-done.39
  409.0 3.6 collective-permute-done.42
  (387 shorter events, 160.2 us)
Async XLA Ops:
  7.2 168.6 %all-gather.3.cloned.1.call-start = ((), (), s32[]{:S(2)}) async-start(), calls=%async_computation.6 | async-start | bytes 5898240 | tf_op jit(solution)/shard_map/all_gather | solution.py:654
  9.4 10.1 %collective-permute-start = (bf16[32,2,512]{2,0,1:T(8,128)(2,1)S(1)}, bf16[32,2,512]{2,0,1:T(8,128)(2,1)S(1)}, u32[]{:S(2)}, u32[]{:S(2)}) collective-permute-start(bf16[32,2,512]{2,0,1:T(8,128)(2,1)S(1)} %bitcast.364), channel_id=1, source_target_pairs={{0,8},{8,0},{1,9},{9,1},{2,10},{10,2},{3,11},{11,3},{4,12},{12,4},... | collective-permute-start | bytes 196616 | tf_op jit(solution)/shard_map/ppermute | solution.py:53
  16.3 17.0 %collective-permute-start.13 = (bf16[2,32,1024]{2,0,1:T(2,128)(2,1)S(1)}, bf16[2,32,1024]{2,0,1:T(2,128)(2,1)S(1)}, u32[]{:S(2)}, u32[]{:S(2)}) collective-permute-start(bf16[2,32,1024]{2,0,1:T(2,128)(2,1)S(1)} %get-tuple-element.128), channel_id=1, source_target_pairs={{0,16},{16,0},{1,17},{17,1},{2,18},{18,2},{3,19},{19,3},{4,20},{20... | collective-permute-start | bytes 393224 | tf_op jit(solution)/shard_map/ppermute | solution.py:62
  19.3 32.7 %collective-permute-start.15 = (bf16[32,1024]{1,0:T(8,128)(2,1)S(1)}, bf16[32,1024]{1,0:T(8,128)(2,1)S(1)}, u32[]{:S(2)}, u32[]{:S(2)}) collective-permute-start(bf16[32,1024]{1,0:T(8,128)(2,1)S(1)} %copy-done.29), channel_id=1, source_target_pairs={{0,16},{16,0},{1,17},{17,1},{2,18},{18,2},{3,19},{19,3},{4,20},{20... | collective-permute-start | bytes 196616 | tf_op jit(solution)/shard_map/ppermute | solution.py:62
  40.0 9.0 %collective-permute-start.9 = (bf16[1,2,2,1,2,32,512]{6,5,4,3,2,1,0:T(8,128)(2,1)S(1)}, bf16[1,2,2,1,2,32,512]{6,5,4,3,2,1,0:T(8,128)(2,1)S(1)}, u32[]{:S(2)}, u32[]{:S(2)}) collective-permute-start(bf16[1,2,2,1,2,32,512]{6,5,4,3,2,1,0:T(8,128)(2,1)S(1)} %constant_dynamic-slice_fusion.22), channel_id=1, source_target_pairs={{0,2},{1,3},{2,0},{3,1},{4,6},{5,7},{6,4},{7,5},{8,10},{9,11},{10,... | collective-permute-start | bytes 786440 | tf_op jit(solution)/shard_map/ppermute | solution.py:62
  49.9 9.5 %collective-permute-start.17 = (bf16[2,2,2,1,2,32,512]{6,5,4,3,2,1,0:T(8,128)(2,1)}, bf16[2,2,2,1,2,32,512]{6,5,4,3,2,1,0:T(8,128)(2,1)}, u32[]{:S(2)}, u32[]{:S(2)}) collective-permute-start(bf16[2,2,2,1,2,32,512]{6,5,4,3,2,1,0:T(8,128)(2,1)} %constant_dynamic-slice_fusion.17), channel_id=1, source_target_pairs={{0,2},{1,3},{2,0},{3,1},{4,6},{5,7},{6,4},{7,5},{8,10},{9,11},{10,... | collective-permute-start | bytes 1572872 | tf_op jit(solution)/shard_map/ppermute | solution.py:62
  51.2 9.4 %collective-permute-start.16 = (bf16[1,2,2,2,2,32,512]{6,5,4,3,2,1,0:T(8,128)(2,1)}, bf16[1,2,2,2,2,32,512]{6,5,4,3,2,1,0:T(8,128)(2,1)S(1)}, u32[]{:S(2)}, u32[]{:S(2)}) collective-permute-start(bf16[1,2,2,2,2,32,512]{6,5,4,3,2,1,0:T(8,128)(2,1)} %constant_dynamic-slice_fusion.18), channel_id=1, source_target_pairs={{0,16},{16,0},{1,17},{17,1},{2,18},{18,2},{3,19},{19,3},{4,20},{20... | collective-permute-start | bytes 1572872 | tf_op jit(solution)/shard_map/ppermute | solution.py:62
  71.4 44.0 %all-to-all-start = ((bf16[8,128,512]{2,1,0:T(8,128)(2,1)}), bf16[8,128,512]{2,1,0:T(8,128)(2,1)}, u32[]{:S(2)}, u32[]{:S(2)}) async-start(bf16[8,128,512]{2,1,0:T(8,128)(2,1)} %bitcast.41), calls=%async_computation | async-start | bytes 2097152 | tf_op jit(solution)/shard_map/all_to_all | solution.py:138
  179.1 15.0 %collective-permute-start.27 = (bf16[256,1024]{1,0:T(8,128)(2,1)}, bf16[256,1024]{1,0:T(8,128)(2,1)}, u32[]{:S(2)}, u32[]{:S(2)}) collective-permute-start(bf16[256,1024]{1,0:T(8,128)(2,1)} %bitcast.71), channel_id=1, source_target_pairs={{0,16},{16,0},{1,17},{17,1},{2,18},{18,2},{3,19},{19,3},{4,20},{20... | collective-permute-start | bytes 1572872 | tf_op jit(solution)/shard_map/ppermute | solution.py:62
  184.8 20.1 %collective-permute-start.21 = (bf16[256,1024]{1,0:T(8,128)(2,1)S(1)}, bf16[256,1024]{1,0:T(8,128)(2,1)S(1)}, u32[]{:S(2)}, u32[]{:S(2)}) collective-permute-start(bf16[256,1024]{1,0:T(8,128)(2,1)S(1)} %add_convert_fusion.1), channel_id=1, source_target_pairs={{0,16},{16,0},{1,17},{17,1},{2,18},{18,2},{3,19},{19,3},{4,20},{20... | collective-permute-start | bytes 1572872 | tf_op jit(solution)/shard_map/ppermute | solution.py:62
  185.8 22.0 %collective-permute-start.19 = (bf16[256,1024]{1,0:T(8,128)(2,1)S(1)}, bf16[256,1024]{1,0:T(8,128)(2,1)S(1)}, u32[]{:S(2)}, u32[]{:S(2)}) collective-permute-start(bf16[256,1024]{1,0:T(8,128)(2,1)S(1)} %add_convert_fusion.1), channel_id=1, source_target_pairs={{0,8},{8,0},{1,9},{9,1},{2,10},{10,2},{3,11},{11,3},{4,12},{12,4},... | collective-permute-start | bytes 1572872 | tf_op jit(solution)/shard_map/ppermute | solution.py:53
  185.8 32.4 %collective-permute-start.25 = (bf16[256,1024]{1,0:T(8,128)(2,1)}, bf16[256,1024]{1,0:T(8,128)(2,1)S(1)}, u32[]{:S(2)}, u32[]{:S(2)}) collective-permute-start(bf16[256,1024]{1,0:T(8,128)(2,1)} %bitcast.71), channel_id=1, source_target_pairs={{0,8},{8,0},{1,9},{9,1},{2,10},{10,2},{3,11},{11,3},{4,12},{12,4},... | collective-permute-start | bytes 1572872 | tf_op jit(solution)/shard_map/ppermute | solution.py:53
  194.1 18.4 %collective-permute-start.28 = (bf16[256,1024]{1,0:T(8,128)(2,1)}, bf16[256,1024]{1,0:T(8,128)(2,1)S(1)}, u32[]{:S(2)}, u32[]{:S(2)}) collective-permute-start(bf16[256,1024]{1,0:T(8,128)(2,1)} %collective-permute-done.27), channel_id=1, source_target_pairs={{0,8},{8,0},{1,9},{9,1},{2,10},{10,2},{3,11},{11,3},{4,12},{12,4},... | collective-permute-start | bytes 1572872 | tf_op jit(solution)/shard_map/ppermute | solution.py:53
  224.0 14.4 %collective-permute-start.30 = (bf16[256,1024]{1,0:T(8,128)(2,1)S(1)}, bf16[256,1024]{1,0:T(8,128)(2,1)S(1)}, u32[]{:S(2)}, u32[]{:S(2)}) collective-permute-start(bf16[256,1024]{1,0:T(8,128)(2,1)S(1)} %fusion.44), channel_id=1, source_target_pairs={{0,16},{16,0},{1,17},{17,1},{2,18},{18,2},{3,19},{19,3},{4,20},{20... | collective-permute-start | bytes 1572872 | tf_op jit(solution)/shard_map/ppermute | solution.py:62
  245.8 19.6 %all-to-all-start.2 = ((bf16[8,128,256]{2,1,0:T(8,128)(2,1)}), bf16[8,128,256]{2,1,0:T(8,128)(2,1)}, u32[]{:S(2)}, u32[]{:S(2)}) async-start(bf16[8,128,256]{2,1,0:T(8,128)(2,1)} %bitcast.312), calls=%async_computation.2 | async-start | bytes 1048576 | tf_op jit(solution)/shard_map/all_to_all | solution.py:138
  250.0 130.5 %reduce-scatter.2.cloned.1.call-start = ((), (), s32[]{:S(2)}) async-start(), calls=%async_computation.5 | async-start | bytes 5898240 | tf_op jit(solution)/shard_map/reduce_scatter | solution.py:781
  308.0 31.7 %all-to-all-start.3 = ((bf16[8,128,512]{2,1,0:T(8,128)(2,1)}), bf16[8,128,512]{2,1,0:T(8,128)(2,1)}, u32[]{:S(2)}, u32[]{:S(2)}) async-start(bf16[8,128,512]{2,1,0:T(8,128)(2,1)} %bitcast.326), calls=%async_computation.3 | async-start | bytes 2097152 | tf_op jit(solution)/shard_map/all_to_all | solution.py:138
  325.1 21.1 %collective-permute-start.20 = (f32[256,1024]{1,0:T(8,128)}, f32[256,1024]{1,0:T(8,128)S(1)}, u32[]{:S(2)}, u32[]{:S(2)}) collective-permute-start(f32[256,1024]{1,0:T(8,128)} %slice.252), channel_id=1, source_target_pairs={{0,8},{8,0},{1,9},{9,1},{2,10},{10,2},{3,11},{11,3},{4,12},{12,4},... | collective-permute-start | bytes 3145736 | tf_op jit(solution)/shard_map/ppermute | solution.py:53
  328.2 18.0 %collective-permute-start.24 = (bf16[256,1024]{1,0:T(8,128)(2,1)}, bf16[256,1024]{1,0:T(8,128)(2,1)}, u32[]{:S(2)}, u32[]{:S(2)}) collective-permute-start(bf16[256,1024]{1,0:T(8,128)(2,1)} %fusion.46), channel_id=1, source_target_pairs={{0,16},{16,0},{1,17},{17,1},{2,18},{18,2},{3,19},{19,3},{4,20},{20... | collective-permute-start | bytes 1572872 | tf_op jit(solution)/shard_map/ppermute | solution.py:62
  343.1 22.3 %collective-permute-start.32 = (f32[256,1024]{1,0:T(8,128)S(1)}, f32[256,1024]{1,0:T(8,128)S(1)}, u32[]{:S(2)}, u32[]{:S(2)}) collective-permute-start(f32[256,1024]{1,0:T(8,128)S(1)} %slice.265), channel_id=1, source_target_pairs={{0,8},{8,0},{1,9},{9,1},{2,10},{10,2},{3,11},{11,3},{4,12},{12,4},... | collective-permute-start | bytes 3145736 | tf_op jit(solution)/shard_map/ppermute | solution.py:53
  343.9 19.2 %collective-permute-start.34 = (bf16[2,2,2,2,32,512]{5,4,1,2,3,0:T(8,128)(2,1)S(1)}, bf16[2,2,2,2,32,512]{5,4,1,2,3,0:T(8,128)(2,1)S(1)}, u32[]{:S(2)}, u32[]{:S(2)}) collective-permute-start(bf16[2,2,2,2,32,512]{5,4,1,2,3,0:T(8,128)(2,1)S(1)} %fusion.72), channel_id=1, source_target_pairs={{0,2},{1,3},{2,0},{3,1},{4,6},{5,7},{6,4},{7,5},{8,10},{9,11},{10,... | collective-permute-start | bytes 1572872 | tf_op jit(solution)/shard_map/ppermute | solution.py:62
  344.8 19.4 %collective-permute-start.33 = (bf16[2,2,2,2,32,512]{5,4,3,2,1,0:T(8,128)(2,1)S(1)}, bf16[2,2,2,2,32,512]{5,4,3,2,1,0:T(8,128)(2,1)S(1)}, u32[]{:S(2)}, u32[]{:S(2)}) collective-permute-start(bf16[2,2,2,2,32,512]{5,4,3,2,1,0:T(8,128)(2,1)S(1)} %fusion.71), channel_id=1, source_target_pairs={{0,16},{16,0},{1,17},{17,1},{2,18},{18,2},{3,19},{19,3},{4,20},{20... | collective-permute-start | bytes 1572872 | tf_op jit(solution)/shard_map/ppermute | solution.py:62
  387.3 9.1 %collective-permute-start.36 = (bf16[2,2,2,32,512]{4,3,0,1,2:T(8,128)(2,1)S(1)}, bf16[2,2,2,32,512]{4,3,0,1,2:T(8,128)(2,1)S(1)}, u32[]{:S(2)}, u32[]{:S(2)}) collective-permute-start(bf16[2,2,2,32,512]{4,3,0,1,2:T(8,128)(2,1)S(1)} %fusion.75), channel_id=1, source_target_pairs={{0,16},{16,0},{1,17},{17,1},{2,18},{18,2},{3,19},{19,3},{4,20},{20... | collective-permute-start | bytes 786440 | tf_op jit(solution)/shard_map/ppermute | solution.py:62
  393.4 20.1 %collective-permute-start.49 = (bf16[2,32,1024]{2,1,0:T(8,128)(2,1)S(1)}, bf16[2,32,1024]{2,1,0:T(8,128)(2,1)S(1)}, u32[]{:S(2)}, u32[]{:S(2)}) collective-permute-start(bf16[2,32,1024]{2,1,0:T(8,128)(2,1)S(1)} %bitcast.353), channel_id=1, source_target_pairs={{0,8},{8,0},{1,9},{9,1},{2,10},{10,2},{3,11},{11,3},{4,12},{12,4},... | collective-permute-start | bytes 393224 | tf_op jit(solution)/shard_map/ppermute | solution.py:53
  (69 other events, 448.5 us)
Sparse Core Ops, SparseCore 0:
  60.8 110.9 all-gather.2
  265.6 114.8 reduce-scatter.1

commit v3 on v2

--- a/solution.py
+++ b/solution.py
@@ -12,8 +12,10 @@
 SPAN = 64
 PAIR = 2 * SPAN
 WINDOW = PAIR + SPAN
-FORWARD_PAIRS = 4
-BACKWARD_PAIRS = 4
+FORWARD_PAIRS = 12
+BACKWARD_PAIRS = 12
+HEADS_AT_CALL = 2
+TIE = 0
 F32 = jnp.float32
 BF16 = jnp.bfloat16
 CORE_SWAP = [(0, 1), (1, 0)]
@@ -98,18 +100,16 @@
         self.starts[dim], self.sizes[dim] = 0, 2
 
 
-class Stack:
-    def __init__(self, block):
-        self.held = block
-
-    def step(self, step):
-        self.held = ordered(self.held, exchange(self.held, *step), *step)
+class Held:
+    def __init__(self, held):
+        self.held = held
 
 
 class Scatter:
-    def __init__(self, total):
-        self.dims = half_steps("chip") + [None] + half_steps("seq")
-        self.held = total.reshape([2] * len(self.dims) + list(total.shape[3:]))
+    def __init__(self, total, whole_core=True):
+        self.dims = half_steps("chip") + [None] * whole_core + half_steps("seq")
+        shape = total.shape[3:] if whole_core else (-1,) + total.shape[1:]
+        self.held = total.reshape([2] * len(self.dims) + list(shape))
 
     def step(self, step):
         dim = self.dims.index(step)
@@ -120,13 +120,14 @@
 
 
 class Halve:
-    def __init__(self, total):
-        self.held = total
+    def __init__(self, total, sent_as):
+        self.held, self.sent_as = total, sent_as
 
     def step(self, step):
         half = self.held.reshape((2, self.held.shape[0] // 2) + self.held.shape[1:])
         mine = side(*step)
-        self.held = pick(half, mine, 0) + exchange(pick(half, 1 - mine, 0), *step)
+        sent = exchange(pick(half, 1 - mine, 0).astype(self.sent_as), *step)
+        self.held = pick(half, mine, 0) + sent.astype(F32)
 
 
 def together(chains):
@@ -250,7 +251,7 @@
             placed_ref[0, where, first : first + HEAD_DIM] = (query * (scale * (1.0 / HEAD_DIM))).astype(BF16)
         return carry
 
-    lax.fori_loop(0, slots // place_rows, place, 0)
+    lax.fori_loop(0, slots // place_rows, place, 0, unroll=2)
 
     pairs = slots // PAIR
     batch = at_once(pairs, FORWARD_PAIRS)
@@ -292,7 +293,7 @@
         spread_ref[this_round, where, :] = sum_three(rows[:, width:], heads)
         return carry
 
-    lax.fori_loop(0, tokens // token_rows, read_back, 0)
+    lax.fori_loop(0, tokens // token_rows, read_back, 0, unroll=2)
 
     if mixing:
 
@@ -319,7 +320,7 @@
                     mixed_ref[where, lanes] = total.astype(BF16)
                 return carry
 
-            lax.fori_loop(0, tokens // 128, mix, 0)
+            lax.fori_loop(0, tokens // 128, mix, 0, unroll=4)
 
 
 def backward_kernel(
@@ -363,7 +364,7 @@
                 d_spread_ref[r, where, :] = weight_ref[r, where, :] * (inner[r] - every)
             return carry
 
-        lax.fori_loop(0, tokens // 128, dots, 0)
+        lax.fori_loop(0, tokens // 128, dots, 0, unroll=4)
 
 
     def weigh(step, carry):
@@ -376,7 +377,7 @@
         )
         return carry
 
-    lax.fori_loop(0, tokens // 128, weigh, 0)
+    lax.fori_loop(0, tokens // 128, weigh, 0, unroll=4)
 
     def place(step, carry):
         base = pl.multiple_of(step * place_rows, place_rows)
@@ -386,7 +387,7 @@
         ).astype(BF16)
         return carry
 
-    lax.fori_loop(0, slots // place_rows, place, 0)
+    lax.fori_loop(0, slots // place_rows, place, 0, unroll=2)
 
     pairs = slots // PAIR
     batch = at_once(pairs, BACKWARD_PAIRS)
@@ -461,7 +462,7 @@
         sum_ref[where, :] += matmul(hot, d_place_ref[SPAN:, :])
         return carry
 
-    lax.fori_loop(0, tokens // token_rows, read_back, 0)
+    lax.fori_loop(0, tokens // token_rows, read_back, 0, unroll=2)
 
     if mixing:
 
@@ -571,6 +572,7 @@
     own_rows = batch * tok
     width = features // (2 * chips)
     heads = width // HEAD_DIM
+    at_call = min(heads, HEADS_AT_CALL)
     hidden_units = w_inner.shape[1]
     quarter = hidden_units // (2 * chips)
     units = sequences * chips
@@ -608,49 +610,70 @@
 
     base = 64
     meta = jnp.stack([slot_place // base, slot_place % base, bucket_ids + 1], 1).astype(BF16)
-    small = [norm1_gain, norm1_bias, norm2_gain, norm2_bias, outer_bias]
-    small = jnp.concatenate([jnp.concatenate(small), inner_bias, meta.reshape(-1)])
-
-    key_split = w_query_key.reshape(shard, chips, 2, width)
-    value_split = w_value.reshape(shard, chips, 2, width)
-    joined_split = jnp.concatenate([key_split, value_split], 3)
-    joined_own, joined_sent = pick(joined_split, core, 2), pick(joined_split, 1 - core, 2)
-    streams, joined_got, small_other = lax.optimization_barrier(
-        (stream_two.reshape(own_rows, features), swap(joined_sent), swap(small))
-    )
-    joined_both = by_core(joined_own, joined_got)
-    chains = [Gather(joined_both[:, :, pair]) for pair in range(chips)]
-    small = Stack(by_core(small, small_other))
-    small_steps = mid_steps + seq_steps[:1] + seq_steps[-1:]
+    vectors = jnp.stack([norm1_gain, norm1_bias, norm2_gain, norm2_bias, outer_bias])
+    small_rows = [meta.reshape(-1, tok)] + [
+        jnp.pad(part, ((0, 0), (0, tok - part.shape[1]))) for part in (vectors, inner_bias[None])
+    ]
+    taken = [part.shape[0] for part in small_rows]
+    fold = 2 * width // tok
+    extra = 8 * (-(-sum(taken) // (8 * fold)))
+    small = jnp.concatenate(
+        small_rows + [jnp.zeros((extra * fold - sum(taken), tok), BF16)], 0
+    )
+    small = jnp.concatenate([small[k * extra : (k + 1) * extra] for k in range(fold)], 1)
+
+    key_split = w_query_key.reshape(shard, chips, 2, heads, HEAD_DIM)
+    value_split = w_value.reshape(shard, chips, 2, heads, HEAD_DIM)
+
+    def pair_blocks(which):
+        keys, values = pick(key_split, which, 2), pick(value_split, which, 2)
+        blocks = [
+            jnp.concatenate(
+                [
+                    part[:, pair, head]
+                    for first in range(0, heads, at_call)
+                    for part in (keys, values)
+                    for head in range(first, first + at_call)
+                ],
+                1,
+            )
+            for pair in range(chips)
+        ]
+        return [jnp.concatenate([blocks[0], small], 0)] + blocks[1:]
+
+    sent = jnp.concatenate(pair_blocks(1 - core), 0)
+    streams, got = lax.optimization_barrier((stream_two.reshape(own_rows, features), swap(sent)))
+    got = [got[: shard + extra]] + [
+        got[extra + pair * shard : extra + (pair + 1) * shard] for pair in range(1, chips)
+    ]
+    chains = [Gather(by_core(own, other)) for own, other in zip(pair_blocks(core), got)]
     for k in range(len(seq_steps) + len(chip_steps)):
         for pair, chain in enumerate(chains):
             chain.step(gather_orders[pair % 2][k])
-        if k < len(small_steps):
-            small.step(small_steps[k])
-            together(chains + [small])
-            if k == len(small_steps) - 1:
-                split = small.held.reshape([2] * len(small_steps) + list(small.held.shape[-2:]))
-                taken = small_steps[::-1]
-                split = jnp.transpose(
-                    split,
-                    [taken.index(step) for step in seq_steps] + [split.ndim - 2, split.ndim - 1],
-                ).reshape(devices, 2, -1)
-                vectors = Stack(jnp.swapaxes(split[:, :, : 5 * shard], 0, 1))
-                cut = 5 * shard + inner_bias.shape[0]
-                quarter_bias = pick(split[:, :, 5 * shard : cut], core, 1).reshape(-1).astype(F32)
-                meta = split[:, :, cut:].reshape(devices, 2, batch, 3, rounds, tok)
-                for step in chip_steps:
-                    vectors.step(step)
-    joined = [chain.held.reshape(features, 2 * width) for chain in chains]
-    vectors = jnp.moveaxis(vectors.held.reshape(-1, 5, shard), 1, 0).reshape(5, features).astype(F32)
+        together(chains)
+    small = chains[0].held.reshape(-1, shard + extra, 2 * width)[:, shard:]
+    small = jnp.concatenate([small[:, :, k * tok : (k + 1) * tok] for k in range(fold)], 1)
+    joined = [chains[0].held.reshape(-1, shard + extra, 2 * width)[:, :shard]]
+    joined = [part.reshape(features, 2 * width) for part in joined + [c.held for c in chains[1:]]]
+    cuts = [taken[0], taken[0] + taken[1]]
+    vectors = jnp.moveaxis(small[:, cuts[0] : cuts[1], :shard], 1, 0).reshape(taken[1], features)
+    vectors = vectors.astype(F32)
     gain_one, bias_one, gain_two, bias_two, full_outer_bias = [vectors[k] for k in range(5)]
+    by_place = small.reshape(chips, 2, devices, -1, tok)
+    quarter_bias = lax.dynamic_slice(
+        by_place, (chip, core, 0, cuts[1], 0), (1, 1, devices, 1, inner_bias.shape[0])
+    )
+    quarter_bias = quarter_bias.reshape(-1).astype(F32)
+    meta = pick(by_place, chip, 0)[:, :, : cuts[0]]
+    meta = jnp.swapaxes(meta, 0, 1).reshape(devices, 2, batch, 3, rounds, tok)
 
     inner_pieces = jnp.moveaxis(w_inner.reshape(shard, chips, 2, quarter), 0, 2)
     inner_pieces = trade_quarters(inner_pieces).reshape(-1, features)
     output_pieces = both_chips(w_output).reshape(-1, features)
     bundle = jnp.concatenate([w_outer, inner_pieces, output_pieces], 0)
     bundle, *joined = lax.optimization_barrier([bundle] + joined)
-    cuts = [w_outer.shape[0], w_outer.shape[0] + inner_pieces.shape[0]]
+    grad_rows = w_outer.shape[0]
+    cuts = [grad_rows, grad_rows + inner_pieces.shape[0]]
     gathered = lax.all_gather(bundle, "seq", axis=0, tiled=False)
     full_outer = gathered[:, : cuts[0]].reshape(quarter, features)
     full_inner = gathered[:, cuts[0] : cuts[1]].reshape(devices, 2 * chips, shard, quarter)
@@ -712,17 +735,36 @@
         value = value.reshape(sequences, chips, sharing, tok, -1)
         return [value[:, pair, 0].reshape(sequences * tok, -1) for pair in range(chips)]
 
-    round_out, weights, mixed, placed, slot_spread = attention_forward(
-        to_attention(projected), places, key_bias, mixing
-    )
-    if not mixing:
-        top = group_max(jnp.max(weights, 0), sharing)
-        weights = jnp.exp(weights - top)
-        weights = weights / group_sum(jnp.sum(weights, 0), sharing)
-        by_head = round_out.reshape(own_rounds, tokens, heads, HEAD_DIM)
-        mixed = group_sum(jnp.sum(weights[:, :, :heads, None] * by_head, 0), sharing)
-        mixed = mixed.reshape(tokens, width).astype(BF16)
-    mixed = jnp.concatenate(from_attention(mixed), 1)
+    def by_heads(pairs, size):
+        arrived = []
+        for call in range(heads // at_call):
+            parts = [pair[:, call * size : (call + 1) * size] for pair in pairs]
+            if arrived:
+                parts, arrived[-1] = lax.optimization_barrier((parts, arrived[-1]))
+            arrived.append(to_attention(parts))
+        return arrived
+
+    def join_heads(parts):
+        return [jnp.concatenate([part[pair] for part in parts], 1) for pair in range(chips)]
+
+    kept, mixed = [], []
+    for qv in by_heads(projected, 2 * at_call * HEAD_DIM):
+        round_out, weights, head_mixed, placed, slot_spread = attention_forward(
+            qv, places, key_bias, mixing
+        )
+        if not mixing:
+            top = group_max(jnp.max(weights, 0), sharing)
+            weights = jnp.exp(weights - top)
+            weights = weights / group_sum(jnp.sum(weights, 0), sharing)
+            by_head = round_out.reshape(own_rounds, tokens, at_call, HEAD_DIM)
+            head_mixed = group_sum(jnp.sum(weights[:, :, :at_call, None] * by_head, 0), sharing)
+            head_mixed = head_mixed.reshape(tokens, -1).astype(BF16)
+        kept.append((round_out, weights, placed, slot_spread))
+        mixed.append(from_attention(head_mixed))
+    mixed = jnp.concatenate(join_heads(mixed), 1)
+    cot_own = grad_two.reshape(own_rows, features)
+    parts_cot = [near(cot_own)] + ([far(cot_own)] if chips == 2 else [])
+    mixed, parts_cot = lax.optimization_barrier((mixed, parts_cot))
 
     def core_sum(value):
         return value[:own_rows] + swap(value[own_rows:])
@@ -730,7 +772,6 @@
     out_one = stream_a + core_sum(matmul(mixed, full_output))
     normed_two, unit_two, scale_two = norm_parts(out_one, gain_two, bias_two)
     inner_low = normed_two.astype(BF16)
-    cot_own = grad_two.reshape(own_rows, features)
 
     def feed_forward(value, cotangent):
         pre_act = matmul(value, full_inner) + quarter_bias
@@ -740,12 +781,21 @@
         d_pre = gelu_pull(d_act)[0].astype(BF16)
         return act_low, d_pre, matmul(act_low, full_outer), matmul_right(d_pre, full_inner)
 
-    parts = [(near(inner_low), near(cot_own))]
+    parts = [(near(inner_low), parts_cot[0])]
+    done = [feed_forward(*parts[0])]
     if chips == 2:
-        parts.append((far(inner_low), far(cot_own)))
-    done = [feed_forward(*part) for part in parts]
+        crossed, done[0] = lax.optimization_barrier((flip(inner_low), done[0]))
+        parts.append((near(crossed), parts_cot[1]))
+        done.append(feed_forward(*parts[1]))
     rows_in, rows_cot = [jnp.concatenate([part[k] for part in parts], 0) for k in range(2)]
     act_low, d_pre = [jnp.concatenate([part[k] for part in done], 0) for k in range(2)]
+
+    grad_outer = matmul_left(act_low, rows_cot).astype(BF16)
+    grad_inner = matmul_left(rows_in, d_pre).astype(BF16)
+    grad_inner = jnp.swapaxes(grad_inner.reshape(2 * chips, devices, shard, quarter), 0, 1)
+    summed = jnp.concatenate(
+        [grad_outer.reshape(devices, -1, features), grad_inner.reshape(devices, -1, features)], 1
+    )
 
     def quarter_sum(values):
         total = core_sum(values[0])
@@ -753,7 +803,10 @@
             total = total + flip(core_sum(values[1]).astype(BF16)).astype(F32)
         return total
 
-    d_normed_two = quarter_sum([part[3] for part in done])
+    d_normed_two = core_sum(done[0][3])
+    if chips == 2:
+        crossed, summed = lax.optimization_barrier((flip(core_sum(done[1][3]).astype(BF16)), summed))
+        d_normed_two = d_normed_two + crossed.astype(F32)
     d_from_two, grad_gain_two, grad_bias_two = norm_back(
         d_normed_two, unit_two, scale_two, gain_two
     )
@@ -762,36 +815,38 @@
 
     d_attended = near(back_one.astype(BF16))
     d_mixed = matmul_right(d_attended, full_output).astype(BF16)
-    d_mixed = to_attention([d_mixed[:, p * width : (p + 1) * width] for p in range(chips)])
-
-    grad_outer = matmul_left(act_low, rows_cot).astype(BF16)
-    grad_inner = matmul_left(rows_in, d_pre).astype(BF16)
-    grad_output = matmul_left(mixed, d_attended).astype(BF16)
-    grad_inner = jnp.swapaxes(grad_inner.reshape(2 * chips, devices, shard, quarter), 0, 1)
-    grad_output = jnp.swapaxes(grad_output.reshape(chips, devices, shard, features), 0, 1)
-    summed = jnp.concatenate(
-        [
-            grad_outer.reshape(devices, -1, features),
-            grad_inner.reshape(devices, -1, features),
-            grad_output.reshape(devices, -1, features),
-        ],
-        1,
-    )
-    summed, d_mixed = lax.optimization_barrier((summed, d_mixed))
-    summed = lax.psum_scatter(summed, "seq", scatter_dimension=0, tiled=True)[0]
+    d_mixed = by_heads([d_mixed[:, p * width : (p + 1) * width] for p in range(chips)], at_call * HEAD_DIM)
+
+    reduced = Held(lax.psum_scatter(summed, "seq", scatter_dimension=0, tiled=True)[0])
+
+    grad_output = Scatter(matmul_left(mixed, d_attended), whole_core=False)
+    output_steps = scatter_orders[0][:]
+
+    def beside(value, count):
+        for _ in range(count):
+            grad_output.step(output_steps.pop(0))
+        grad_output.held, value = lax.optimization_barrier((grad_output.held, value))
+        return value
+
+    d_mixed[0] = beside(d_mixed[0], len(chip_steps))
     quarter_bias_grad = jnp.sum(d_pre.astype(F32), 0).reshape(devices, -1)
 
-    all_dot = None
-    if not mixing:
-        inner = d_mixed.reshape(1, tokens, heads, HEAD_DIM).astype(F32) * by_head
-        inner = jnp.sum(weights[:, :, :heads] * jnp.sum(inner, -1), 0)
-        all_dot = jnp.pad(group_sum(inner, sharing), ((0, 0), (0, 128 - heads)))
-    d_total = attention_backward(
-        d_mixed, round_out, weights, all_dot, placed, slot_spread, places, key_bias
-    )
-    if not mixing:
-        d_total = group_sum(d_total, sharing).astype(BF16)
-    d_projected = from_attention(d_total)
+    d_projected = []
+    for call, (round_out, weights, placed, slot_spread) in enumerate(kept):
+        all_dot = None
+        if not mixing:
+            inner = d_mixed[call].astype(F32) * round_out.astype(F32)
+            inner = jnp.sum(inner.reshape(own_rounds, tokens, at_call, HEAD_DIM), -1)
+            inner = group_sum(jnp.sum(weights[:, :, :at_call] * inner, 0), sharing)
+            all_dot = jnp.pad(inner, ((0, 0), (0, 128 - at_call)))
+        d_total = attention_backward(
+            d_mixed[call], round_out, weights, all_dot, placed, slot_spread, places, key_bias
+        )
+        d_total = beside(d_total, 1)
+        if not mixing:
+            d_total = group_sum(d_total, sharing).astype(BF16)
+        d_projected.append(beside(from_attention(d_total), len(mid_steps)))
+    d_projected = join_heads(d_projected)
 
     chains = []
     for pair in range(chips):
@@ -809,11 +864,12 @@
         [grad_gain_one, grad_bias_one, grad_gain_two, grad_bias_two, jnp.sum(cot_own.astype(F32), 0)]
     )
     small_grads = jnp.swapaxes(small_grads.reshape(5, 2 * chips * devices, shard), 0, 1)
-    small_grads = Halve(small_grads.reshape(-1, 5 * shard))
+    small_grads = Halve(small_grads.reshape(-1, 5 * shard), F32)
     small_steps = chip_steps + [("core", 1)] + seq_steps
-    reduced = Stack(summed)
+    while output_steps:
+        grad_output.step(output_steps.pop(0))
     for k in range(max(len(orders) - 1, len(small_steps))):
-        together(chains + [small_grads] + [reduced] * (k == 0))
+        together(chains + [small_grads] + [grad_output, reduced] * (k == TIE))
         if k + 1 < len(orders):
             for chain, step in zip(chains, orders[k + 1]):
                 chain.step(step)
@@ -824,20 +880,14 @@
             small_grads.held = jnp.concatenate([small_grads.held, quarter_bias_grad], 1)
         small_grads.step(small_steps[k])
     summed = reduced.held
-    grad_outer = summed[: cuts[0]].astype(F32)
-    grad_inner = trade_quarters(summed[cuts[0] : cuts[1]].reshape(chips, 2, shard, quarter))
+    grad_outer = summed[: grad_rows].astype(F32)
+    grad_inner = trade_quarters(summed[grad_rows:].reshape(chips, 2, shard, quarter))
     grad_inner = jnp.moveaxis(grad_inner, 2, 0).reshape(shard, hidden_units).astype(F32)
-    grad_output = summed[cuts[1] :].reshape(chips, shard, features)
-    if chips == 2:
-        other = flip(pick(grad_output, 1 - chip, 0)).astype(F32)
-        grad_output = pick(grad_output, chip, 0).astype(F32) + other
-    else:
-        grad_output = grad_output[0].astype(F32)
     small_grads, grad_inner_bias = (
         small_grads.held[0, : 5 * shard].reshape(5, shard), small_grads.held[0, 5 * shard :]
     )
-    grad_joined = grad_joined.reshape(2, chips, shard, 2, width)
-    grad_joined = jnp.transpose(grad_joined, (3, 2, 1, 0, 4)).reshape(2, shard, features)
+    grad_joined = grad_joined.reshape(2, chips, shard, heads // at_call, 2, at_call * HEAD_DIM)
+    grad_joined = jnp.transpose(grad_joined, (4, 2, 1, 0, 3, 5)).reshape(2, shard, features)
     out_shape = (batch, tok, features)
     return (
         out_one.reshape(out_shape),
@@ -848,7 +898,7 @@
         small_grads[1],
         grad_joined[0],
         grad_joined[1],
-        grad_output,
+        grad_output.held,
         small_grads[2],
         small_grads[3],
         grad_inner,

time: 438 us -> 430 us (0.982)
  blocking collectives: 24.8 us -> 0 us
  other arithmetic: 33.5 us -> 51.7 us
  Pallas kernels: 76.8 us -> 61 us
  starting transfers between devices: 53.1 us -> 64.6 us
  waiting for transfers between devices: 145 us -> 152 us
  matrix products: 34.4 us -> 29.2 us
    all_to_all x1 -> x0, blocking collectives: 24.8 us -> none  [all_to_all(): return lax.all_to_all(block, 'seq', split_axis=0, concat_axis=0, tiled=True)]
    all_to_all x3 -> x4, waiting for transfers between devices: 43 us -> 67.6 us  [all_to_all(): return lax.all_to_all(block, 'seq', split_axis=0, concat_axis=0, tiled=True)]
    ppermute x33 -> x32, waiting for transfers between devices: 87.9 us -> 73.7 us  [exchange(): return lax.ppermute(block, axis, [(i, i ^ bit) for i in range(size)])]
    reduce_scatter x1, waiting for transfers between devices: 11.9 us -> 0.01 us  [local(): lax.psum_scatter(summed, 'seq', scatter_dimension=0, tiled=True)[0]]
    pallas_call x1, Pallas kernels: 41.9 us -> 33.5 us  [attention_backward(): pl.pallas_call(functools.partial(backward_kernel, heads, mixing), grid=(r...]
    pallas_call x1, Pallas kernels: 34.9 us -> 27.5 us  [attention_forward(): pl.pallas_call(functools.partial(forward_kernel, heads, mixing), grid=(ro...]
    ppermute x17 -> x16, waiting for transfers between devices: 2.12 us -> 9.11 us  [swap(): return lax.ppermute(block, 'core', CORE_SWAP)]
    add x8 -> x12, other arithmetic: 2.54 us -> 9.23 us  [step(): self.held = pick(self.held, mine, dim) + sent.astype(F32)]
  transfers between devices with their start and end apart: 55 -> 54, of which waited for: 29 -> 30; matrix products, arithmetic and copies ran while one was open for 22% -> 23% of each run, Pallas kernels for 18% -> 14%
where the time goes in v3:
time: 430 us; the launch traced here: 423 us
  waiting for transfers between devices  152 us (35%)
  starting transfers between devices  64.6 us (15%)
  Pallas kernels  61 us (14%)
  other arithmetic  51.7 us (12%)
  local copies, waits for them, and re-layouts  49.7 us (12%)
  matrix products  29.2 us (7%)
  between operations  15.8 us (4%)
    ppermute x32, waiting for transfers between devices, exchange(): return lax.ppermute(block, axis, [(i, i ^ bit) for i in range(size)])  73.7 us
    all_to_all x4, waiting for transfers between devices, all_to_all(): return lax.all_to_all(block, 'seq', split_axis=0, concat_axis=0, tiled=True)  67.6 us
    ppermute x32, starting transfers between devices, exchange(): return lax.ppermute(block, axis, [(i, i ^ bit) for i in range(size)])  42.6 us
    pallas_call x1, Pallas kernels, attention_backward(): pl.pallas_call(functools.partial(backward_kernel, heads, mixing), grid=(r...  33.5 us
    pallas_call x1, Pallas kernels, attention_forward(): pl.pallas_call(functools.partial(forward_kernel, heads, mixing), grid=(ro...  27.5 us
    all_to_all x4, starting transfers between devices, all_to_all(): return lax.all_to_all(block, 'seq', split_axis=0, concat_axis=0, tiled=True)  19.2 us
    dot_general x7, matrix products, matmul(): return jnp.dot(left, right, preferred_element_type=F32)  10.4 us
    dot_general x7, matrix products, matmul_right(): lax.dot_general(left, right, (((1,), (1,)), ((), ())), preferred_element_...  10.2 us
  transfers between devices with their start and end apart: 54, of which 30 were waited for; matrix products, arithmetic and copies ran while one was open for 23% of the time, Pallas kernels for 14%

profile of v3, /device:TPU:0, one launch (start us, length us, event | category | flops | bytes accessed | tf_op | source)
XLA Modules:
  0.0 423.4 jit_solution(5198683099232410056)
XLA Ops:
  13.0 2.9 collective-permute-start.3
  18.8 4.4 %collective-permute-done.2 = bf16[1,2,1,1,1,40,512]{6,5,4,3,2,1,0:T(8,128)(2,1)S(1)} collective-permute-done((bf16[1,2,1,1,1,40,512]{6,5,4,3,2,1,0:T(8,128)(2,1)S(1)}, bf16[1,2,1,1,1,40,512]{6,5,4,3,2,1,0:T(8,128)(2,1)S(1)}, u32[]{:S(2)}, u32[]{:S(2)}) %collective-permute-start.2) | collective-permute-done | bytes 81952 | tf_op jit(solution)/shard_map/ppermute | solution.py:64
  25.8 5.8 %collective-permute-done.5 = bf16[2,2,1,1,1,32,512]{6,5,4,3,2,1,0:T(8,128)(2,1)S(1)} collective-permute-done((bf16[2,2,1,1,1,32,512]{6,5,4,3,2,1,0:T(8,128)(2,1)S(1)}, bf16[2,2,1,1,1,32,512]{6,5,4,3,2,1,0:T(8,128)(2,1)S(1)}, u32[]{:S(2)}, u32[]{:S(2)}) %collective-permute-start.5) | collective-permute-done | bytes 131104 | tf_op jit(solution)/shard_map/ppermute | solution.py:64
  49.1 6.2 %collective-permute-done.9 = bf16[2,2,2,1,2,32,512]{6,5,4,3,2,1,0:T(8,128)(2,1)S(1)} collective-permute-done((bf16[2,2,2,1,2,32,512]{6,5,4,3,2,1,0:T(8,128)(2,1)}, bf16[2,2,2,1,2,32,512]{6,5,4,3,2,1,0:T(8,128)(2,1)S(1)}, u32[]{:S(2)}, u32[]{:S(2)}) %collective-permute-start.9) | collective-permute-done | bytes 524320 | tf_op jit(solution)/shard_map/ppermute | solution.py:64
  63.2 3.0 fusion
  69.4 6.6 %all-to-all-start = ((bf16[8,128,512]{2,1,0:T(8,128)(2,1)}), bf16[8,128,512]{2,1,0:T(8,128)(2,1)}, u32[]{:S(2)}, u32[]{:S(2)}) async-start(bf16[8,128,512]{2,1,0:T(8,128)(2,1)} %bitcast.54), calls=%async_computation | async-start | bytes 2097152 | tf_op jit(solution)/shard_map/all_to_all | solution.py:139
  77.0 3.9 select_reduce_fusion
  86.9 29.4 %all-to-all-done = bf16[8,128,512]{2,1,0:T(8,128)(2,1)} async-done(((bf16[8,128,512]{2,1,0:T(8,128)(2,1)}), bf16[8,128,512]{2,1,0:T(8,128)(2,1)}, u32[]{:S(2)}, u32[]{:S(2)}) %all-to-all-start) | async-done | bytes 1048608 | tf_op jit(solution)/shard_map/all_to_all | solution.py:139
  116.3 27.5 %shard_map.280 = (bf16[4,1024,256]{2,1,0:T(8,128)(2,1)}, f32[4,1024,128]{2,1,0:T(8,128)}, bf16[1024,256]{1,0:T(8,128)(2,1)}, bf16[4,1600,768]{2,1,0:T(8,128)(2,1)}, f32[4,12,8,128]{3,2,1,0:T(8,128)}) custom-call(bf16[1024,512]{1,0:T(8,128)(2,1)} %bitcast.55.qv_ref, s32[4,1,1024]{2,1,0:T(1,128)} %bitcast.385, s32[4,1024,1]{2,1,0:T(8,128)} %copy.224.column_ref, ...), custom_call_target="tpu_custom_call" | custom-call | flops 12482248704 | bytes 20971520 | tf_op jit(solution)/shard_map/pallas_call | solution.py:501
  143.8 3.7 all-to-all-start.1
  153.9 20.9 %all-to-all-done.1 = bf16[8,128,256]{2,1,0:T(8,128)(2,1)S(1)} async-done(((bf16[8,128,256]{2,1,0:T(8,128)(2,1)}), bf16[8,128,256]{2,1,0:T(8,128)(2,1)S(1)}, u32[]{:S(2)}, u32[]{:S(2)}) %all-to-all-start.1) | async-done | bytes 524320 | tf_op jit(solution)/shard_map/all_to_all | solution.py:139
  198.1 5.0 %collective-permute-done.17 = bf16[256,1024]{1,0:T(8,128)(2,1)S(1)} collective-permute-done((bf16[256,1024]{1,0:T(8,128)(2,1)S(1)}, bf16[256,1024]{1,0:T(8,128)(2,1)S(1)}, u32[]{:S(2)}, u32[]{:S(2)}) %collective-permute-start.17) | collective-permute-done | bytes 524320 | tf_op jit(solution)/shard_map/ppermute | solution.py:64
  222.3 7.9 %collective-permute-done.25 = bf16[256,1024]{1,0:T(8,128)(2,1)} collective-permute-done((bf16[256,1024]{1,0:T(8,128)(2,1)}, bf16[256,1024]{1,0:T(8,128)(2,1)}, u32[]{:S(2)}, u32[]{:S(2)}) %collective-permute-start.25) | collective-permute-done | bytes 524320 | tf_op jit(solution)/shard_map/ppermute | solution.py:64
  237.6 4.1 all-to-all-start.2
  246.3 12.8 %collective-permute-done.27 = bf16[2,2,2,32,1024]{4,3,0,1,2:T(8,128)(2,1)} collective-permute-done((bf16[2,2,2,32,1024]{4,3,0,1,2:T(8,128)(2,1)}, bf16[2,2,2,32,1024]{4,3,0,1,2:T(8,128)(2,1)}, u32[]{:S(2)}, u32[]{:S(2)}) %collective-permute-start.27) | collective-permute-done | bytes 524320 | tf_op jit(solution)/shard_map/ppermute | solution.py:64
  264.5 33.5 %shard_map.281 = bf16[1024,512]{1,0:T(8,128)(2,1)} custom-call(bf16[1024,256]{1,0:T(8,128)(2,1)} %bitcast.98.d_mixed_ref, bf16[4,1024,256]{2,1,0:T(8,128)(2,1)} %get-tuple-element.90.out_ref, f32[4,1024,128]{2,1,0:T(8,128)} %get-tuple-element.91.weight_ref, f32[8,128]{1,0:T(8,128)} %broadcast_in_dim.88.dot_ref, ...), custom_call_target="tpu_custom_call" | custom-call | flops 14294188032 | bytes 20971520 | tf_op jit(solution)/shard_map/pallas_call | solution.py:527
  298.9 4.8 %all-to-all-start.3 = ((bf16[8,128,512]{2,1,0:T(8,128)(2,1)}), bf16[8,128,512]{2,1,0:T(8,128)(2,1)S(1)}, u32[]{:S(2)}, u32[]{:S(2)}) async-start(bf16[8,128,512]{2,1,0:T(8,128)(2,1)} %bitcast.365), calls=%async_computation.3 | async-start | bytes 2097152 | tf_op jit(solution)/shard_map/all_to_all | solution.py:139
  303.7 3.2 fusion.114
  323.8 17.3 %all-to-all-done.3 = bf16[8,128,512]{2,1,0:T(8,128)(2,1)S(1)} async-done(((bf16[8,128,512]{2,1,0:T(8,128)(2,1)}), bf16[8,128,512]{2,1,0:T(8,128)(2,1)S(1)}, u32[]{:S(2)}, u32[]{:S(2)}) %all-to-all-start.3) | async-done | bytes 1048608 | tf_op jit(solution)/shard_map/all_to_all | solution.py:139
  353.5 10.5 %collective-permute-done.33 = bf16[32,1024]{1,0:T(8,128)(2,1)S(1)} collective-permute-done((bf16[32,1024]{1,0:T(8,128)(2,1)S(1)}, bf16[32,1024]{1,0:T(8,128)(2,1)S(1)}, u32[]{:S(2)}, u32[]{:S(2)}) %collective-permute-start.33) | collective-permute-done | bytes 65568 | tf_op jit(solution)/shard_map/ppermute | solution.py:64
  382.5 4.6 %collective-permute-done.36 = f32[16,160]{1,0:T(8,128)S(1)} collective-permute-done((f32[16,160]{1,0:T(8,128)S(1)}, f32[16,160]{1,0:T(8,128)S(1)}, u32[]{:S(2)}, u32[]{:S(2)}) %collective-permute-start.36) | collective-permute-done | bytes 10272 | tf_op jit(solution)/shard_map/ppermute | solution.py:64
  392.5 3.5 collective-permute-done.37
  396.4 3.3 collective-permute-start.40
  399.9 3.0 collective-permute-start.41
  (393 shorter events, 180.0 us)
Async XLA Ops:
  7.2 168.9 %all-gather.3.cloned.1.call-start = ((), (), s32[]{:S(2)}) async-start(), calls=%async_computation.6 | async-start | bytes 5898240 | tf_op jit(solution)/shard_map/all_gather | solution.py:677
  35.3 11.4 %collective-permute-start.12 = (bf16[32,1024]{1,0:T(8,128)(2,1)}, bf16[32,1024]{1,0:T(8,128)(2,1)}, u32[]{:S(2)}, u32[]{:S(2)}) collective-permute-start(bf16[32,1024]{1,0:T(8,128)(2,1)} %param.27), channel_id=1, source_target_pairs={{0,16},{16,0},{1,17},{17,1},{2,18},{18,2},{3,19},{19,3},{4,20},{20... | collective-permute-start | bytes 196616 | tf_op jit(solution)/shard_map/ppermute | solution.py:64
  42.6 14.2 %collective-permute-start.8 = (bf16[1,2,2,2,2,40,512]{6,5,4,3,2,1,0:T(8,128)(2,1)}, bf16[1,2,2,2,2,40,512]{6,5,4,3,2,1,0:T(8,128)(2,1)}, u32[]{:S(2)}, u32[]{:S(2)}) collective-permute-start(bf16[1,2,2,2,2,40,512]{6,5,4,3,2,1,0:T(8,128)(2,1)} %constant_dynamic-slice_fusion.26), channel_id=1, source_target_pairs={{0,16},{16,0},{1,17},{17,1},{2,18},{18,2},{3,19},{19,3},{4,20},{20... | collective-permute-start | bytes 1966088 | tf_op jit(solution)/shard_map/ppermute | solution.py:64
  43.9 11.4 %collective-permute-start.9 = (bf16[2,2,2,1,2,32,512]{6,5,4,3,2,1,0:T(8,128)(2,1)}, bf16[2,2,2,1,2,32,512]{6,5,4,3,2,1,0:T(8,128)(2,1)S(1)}, u32[]{:S(2)}, u32[]{:S(2)}) collective-permute-start(bf16[2,2,2,1,2,32,512]{6,5,4,3,2,1,0:T(8,128)(2,1)} %constant_dynamic-slice_fusion.25), channel_id=1, source_target_pairs={{0,2},{1,3},{2,0},{3,1},{4,6},{5,7},{6,4},{7,5},{8,10},{9,11},{10,... | collective-permute-start | bytes 1572872 | tf_op jit(solution)/shard_map/ppermute | solution.py:64
  59.1 88.5 %collective-permute-start.14 = (bf16[256,1024]{1,0:T(8,128)(2,1)}, bf16[256,1024]{1,0:T(8,128)(2,1)}, u32[]{:S(2)}, u32[]{:S(2)}) collective-permute-start(bf16[256,1024]{1,0:T(8,128)(2,1)} %bitcast.74), channel_id=1, source_target_pairs={{0,16},{16,0},{1,17},{17,1},{2,18},{18,2},{3,19},{19,3},{4,20},{20... | collective-permute-start | bytes 1572872 | tf_op jit(solution)/shard_map/ppermute | solution.py:64
  69.4 46.9 %all-to-all-start = ((bf16[8,128,512]{2,1,0:T(8,128)(2,1)}), bf16[8,128,512]{2,1,0:T(8,128)(2,1)}, u32[]{:S(2)}, u32[]{:S(2)}) async-start(bf16[8,128,512]{2,1,0:T(8,128)(2,1)} %bitcast.54), calls=%async_computation | async-start | bytes 2097152 | tf_op jit(solution)/shard_map/all_to_all | solution.py:139
  143.8 30.9 %all-to-all-start.1 = ((bf16[8,128,256]{2,1,0:T(8,128)(2,1)}), bf16[8,128,256]{2,1,0:T(8,128)(2,1)S(1)}, u32[]{:S(2)}, u32[]{:S(2)}) async-start(bf16[8,128,256]{2,1,0:T(8,128)(2,1)} %bitcast.376), calls=%async_computation.1 | async-start | bytes 1048576 | tf_op jit(solution)/shard_map/all_to_all | solution.py:139
  188.8 14.3 %collective-permute-start.17 = (bf16[256,1024]{1,0:T(8,128)(2,1)S(1)}, bf16[256,1024]{1,0:T(8,128)(2,1)S(1)}, u32[]{:S(2)}, u32[]{:S(2)}) collective-permute-start(bf16[256,1024]{1,0:T(8,128)(2,1)S(1)} %add_convert_fusion.1), channel_id=1, source_target_pairs={{0,16},{16,0},{1,17},{17,1},{2,18},{18,2},{3,19},{19,3},{4,20},{20... | collective-permute-start | bytes 1572872 | tf_op jit(solution)/shard_map/ppermute | solution.py:64
  211.9 18.3 %collective-permute-start.23 = (f32[256,1024]{1,0:T(8,128)}, f32[256,1024]{1,0:T(8,128)}, u32[]{:S(2)}, u32[]{:S(2)}) collective-permute-start(f32[256,1024]{1,0:T(8,128)} %slice.305), channel_id=1, source_target_pairs={{0,8},{8,0},{1,9},{9,1},{2,10},{10,2},{3,11},{11,3},{4,12},{12,4},... | collective-permute-start | bytes 3145736 | tf_op jit(solution)/shard_map/ppermute | solution.py:55
  215.9 14.3 %collective-permute-start.25 = (bf16[256,1024]{1,0:T(8,128)(2,1)}, bf16[256,1024]{1,0:T(8,128)(2,1)}, u32[]{:S(2)}, u32[]{:S(2)}) collective-permute-start(bf16[256,1024]{1,0:T(8,128)(2,1)} %fusion.40), channel_id=1, source_target_pairs={{0,16},{16,0},{1,17},{17,1},{2,18},{18,2},{3,19},{19,3},{4,20},{20... | collective-permute-start | bytes 1572872 | tf_op jit(solution)/shard_map/ppermute | solution.py:64
  237.6 23.6 %all-to-all-start.2 = ((bf16[8,128,256]{2,1,0:T(8,128)(2,1)}), bf16[8,128,256]{2,1,0:T(8,128)(2,1)}, u32[]{:S(2)}, u32[]{:S(2)}) async-start(bf16[8,128,256]{2,1,0:T(8,128)(2,1)} %bitcast.97), calls=%async_computation.2 | async-start | bytes 1048576 | tf_op jit(solution)/shard_map/all_to_all | solution.py:139
  241.8 133.5 %reduce-scatter.2.cloned.1.call-start = ((), (), s32[]{:S(2)}) async-start(), calls=%async_computation.5 | async-start | bytes 4718592 | tf_op jit(solution)/shard_map/reduce_scatter | solution.py:820
  244.8 14.3 %collective-permute-start.27 = (bf16[2,2,2,32,1024]{4,3,0,1,2:T(8,128)(2,1)}, bf16[2,2,2,32,1024]{4,3,0,1,2:T(8,128)(2,1)}, u32[]{:S(2)}, u32[]{:S(2)}) collective-permute-start(bf16[2,2,2,32,1024]{4,3,0,1,2:T(8,128)(2,1)} %fusion.52), channel_id=1, source_target_pairs={{0,16},{16,0},{1,17},{17,1},{2,18},{18,2},{3,19},{19,3},{4,20},{20... | collective-permute-start | bytes 1572872 | tf_op jit(solution)/shard_map/ppermute | solution.py:64
  262.3 35.7 %collective-permute-start.28 = (bf16[2,2,32,1024]{3,2,0,1:T(8,128)(2,1)S(1)}, bf16[2,2,32,1024]{3,2,0,1:T(8,128)(2,1)S(1)}, u32[]{:S(2)}, u32[]{:S(2)}) collective-permute-start(bf16[2,2,32,1024]{3,2,0,1:T(8,128)(2,1)S(1)} %fusion.55), channel_id=1, source_target_pairs={{0,1},{1,0},{2,3},{3,2},{4,5},{5,4},{6,7},{7,6},{8,9},{9,8},{10,11... | collective-permute-start | bytes 786440 | tf_op jit(solution)/shard_map/ppermute | solution.py:64
  298.9 42.1 %all-to-all-start.3 = ((bf16[8,128,512]{2,1,0:T(8,128)(2,1)}), bf16[8,128,512]{2,1,0:T(8,128)(2,1)S(1)}, u32[]{:S(2)}, u32[]{:S(2)}) async-start(bf16[8,128,512]{2,1,0:T(8,128)(2,1)} %bitcast.365), calls=%async_computation.3 | async-start | bytes 2097152 | tf_op jit(solution)/shard_map/all_to_all | solution.py:139
  313.0 37.5 %collective-permute-start.19 = (f32[256,1024]{1,0:T(8,128)}, f32[256,1024]{1,0:T(8,128)}, u32[]{:S(2)}, u32[]{:S(2)}) collective-permute-start(f32[256,1024]{1,0:T(8,128)} %slice.300), channel_id=1, source_target_pairs={{0,8},{8,0},{1,9},{9,1},{2,10},{10,2},{3,11},{11,3},{4,12},{12,4},... | collective-permute-start | bytes 3145736 | tf_op jit(solution)/shard_map/ppermute | solution.py:55
  319.4 31.2 %collective-permute-start.22 = (bf16[256,1024]{1,0:T(8,128)(2,1)}, bf16[256,1024]{1,0:T(8,128)(2,1)}, u32[]{:S(2)}, u32[]{:S(2)}) collective-permute-start(bf16[256,1024]{1,0:T(8,128)(2,1)} %fusion.41), channel_id=1, source_target_pairs={{0,16},{16,0},{1,17},{17,1},{2,18},{18,2},{3,19},{19,3},{4,20},{20... | collective-permute-start | bytes 1572872 | tf_op jit(solution)/shard_map/ppermute | solution.py:64
  344.3 25.7 %collective-permute-start.30 = (f32[256,1024]{1,0:T(8,128)}, f32[256,1024]{1,0:T(8,128)S(1)}, u32[]{:S(2)}, u32[]{:S(2)}) collective-permute-start(f32[256,1024]{1,0:T(8,128)} %slice.376), channel_id=1, source_target_pairs={{0,8},{8,0},{1,9},{9,1},{2,10},{10,2},{3,11},{11,3},{4,12},{12,4},... | collective-permute-start | bytes 3145736 | tf_op jit(solution)/shard_map/ppermute | solution.py:55
  346.0 18.6 %collective-permute-start.31 = (bf16[2,2,2,2,32,512]{5,4,0,1,2,3:T(8,128)(2,1)}, bf16[2,2,2,2,32,512]{5,4,0,1,2,3:T(8,128)(2,1)}, u32[]{:S(2)}, u32[]{:S(2)}) collective-permute-start(bf16[2,2,2,2,32,512]{5,4,0,1,2,3:T(8,128)(2,1)} %fusion.53), channel_id=1, source_target_pairs={{0,16},{16,0},{1,17},{17,1},{2,18},{18,2},{3,19},{19,3},{4,20},{20... | collective-permute-start | bytes 1572872 | tf_op jit(solution)/shard_map/ppermute | solution.py:64
  350.5 16.9 %collective-permute-start.32 = (bf16[2,2,2,2,32,512]{5,4,1,2,3,0:T(8,128)(2,1)}, bf16[2,2,2,2,32,512]{5,4,1,2,3,0:T(8,128)(2,1)}, u32[]{:S(2)}, u32[]{:S(2)}) collective-permute-start(bf16[2,2,2,2,32,512]{5,4,1,2,3,0:T(8,128)(2,1)} %fusion.54), channel_id=1, source_target_pairs={{0,2},{1,3},{2,0},{3,1},{4,6},{5,7},{6,4},{7,5},{8,10},{9,11},{10,... | collective-permute-start | bytes 1572872 | tf_op jit(solution)/shard_map/ppermute | solution.py:64
  350.5 13.4 %collective-permute-start.33 = (bf16[32,1024]{1,0:T(8,128)(2,1)S(1)}, bf16[32,1024]{1,0:T(8,128)(2,1)S(1)}, u32[]{:S(2)}, u32[]{:S(2)}) collective-permute-start(bf16[32,1024]{1,0:T(8,128)(2,1)S(1)} %fusion.68), channel_id=1, source_target_pairs={{0,4},{1,5},{2,6},{3,7},{4,0},{5,1},{6,2},{7,3},{8,12},{9,13},{10,... | collective-permute-start | bytes 196616 | tf_op jit(solution)/shard_map/ppermute | solution.py:64
  376.3 13.5 %collective-permute-start.34 = (bf16[2,2,2,32,512]{4,3,0,1,2:T(8,128)(2,1)S(1)}, bf16[2,2,2,32,512]{4,3,0,1,2:T(8,128)(2,1)S(1)}, u32[]{:S(2)}, u32[]{:S(2)}) collective-permute-start(bf16[2,2,2,32,512]{4,3,0,1,2:T(8,128)(2,1)S(1)} %fusion.56), channel_id=1, source_target_pairs={{0,1},{1,0},{2,3},{3,2},{4,5},{5,4},{6,7},{7,6},{8,9},{9,8},{10,11... | collective-permute-start | bytes 786440 | tf_op jit(solution)/shard_map/ppermute | solution.py:64
  377.4 12.5 %collective-permute-start.35 = (bf16[2,2,2,32,512]{4,3,0,1,2:T(8,128)(2,1)S(1)}, bf16[2,2,2,32,512]{4,3,0,1,2:T(8,128)(2,1)S(1)}, u32[]{:S(2)}, u32[]{:S(2)}) collective-permute-start(bf16[2,2,2,32,512]{4,3,0,1,2:T(8,128)(2,1)S(1)} %fusion.57), channel_id=1, source_target_pairs={{0,16},{16,0},{1,17},{17,1},{2,18},{18,2},{3,19},{19,3},{4,20},{20... | collective-permute-start | bytes 786440 | tf_op jit(solution)/shard_map/ppermute | solution.py:64
  389.6 17.5 %collective-permute-start.47 = (bf16[2,32,1024]{2,1,0:T(8,128)(2,1)S(1)}, bf16[2,32,1024]{2,1,0:T(8,128)(2,1)S(1)}, u32[]{:S(2)}, u32[]{:S(2)}) collective-permute-start(bf16[2,32,1024]{2,1,0:T(8,128)(2,1)S(1)} %bitcast.387), channel_id=1, source_target_pairs={{0,8},{8,0},{1,9},{9,1},{2,10},{10,2},{3,11},{11,3},{4,12},{12,4},... | collective-permute-start | bytes 393224 | tf_op jit(solution)/shard_map/ppermute | solution.py:55
  (69 other events, 699.3 us)
Sparse Core Ops, SparseCore 0:
  59.2 116.8 all-gather.2
  246.4 100.0 reduce-scatter.1

commit v4 on v3

--- a/solution.py
+++ b/solution.py
@@ -605,7 +605,7 @@
     ]
     scatter_orders = [
         chip_steps + seq_steps[-1:] + mid_steps + seq_steps[:1],
-        mid_steps + chip_steps + seq_steps[-1:] + seq_steps[:1],
+        seq_steps[-1:] + chip_steps + mid_steps + seq_steps[:1],
     ]
 
     base = 64
@@ -869,7 +869,10 @@
     while output_steps:
         grad_output.step(output_steps.pop(0))
     for k in range(max(len(orders) - 1, len(small_steps))):
-        together(chains + [small_grads] + [grad_output, reduced] * (k == TIE))
+        held = [Held(d_from_one), reduced, small_grads] if k == 1 else []
+        together(chains + ([grad_output, reduced] if k == 0 else held))
+        if k == 1:
+            back_two = cot_own.astype(F32) + held[0].held
         if k + 1 < len(orders):
             for chain, step in zip(chains, orders[k + 1]):
                 chain.step(step)

time: 430 us -> 410 us (0.953)
  waiting for transfers between devices: 152 us -> 131 us
    ppermute x32, waiting for transfers between devices: 73.7 us -> 61.8 us  [exchange(): return lax.ppermute(block, axis, [(i, i ^ bit) for i in range(size)])]
    all_to_all x4, waiting for transfers between devices: 67.6 us -> 58.8 us  [all_to_all(): return lax.all_to_all(block, 'seq', split_axis=0, concat_axis=0, tiled=True)]
  transfers between devices with their start and end apart: 54 -> 54, of which waited for: 30 -> 30; matrix products, arithmetic and copies ran while one was open for 23% -> 24% of each run, Pallas kernels for 14% -> 15%
where the time goes in v4:
time: 410 us; the launch traced here: 403 us
  waiting for transfers between devices  131 us (32%)
  starting transfers between devices  62.8 us (15%)
  Pallas kernels  61 us (15%)
  other arithmetic  53.3 us (13%)
  local copies, waits for them, and re-layouts  49.6 us (12%)
  matrix products  29.1 us (7%)
  between operations  15.7 us (4%)
    ppermute x32, waiting for transfers between devices, exchange(): return lax.ppermute(block, axis, [(i, i ^ bit) for i in range(size)])  61.8 us
    all_to_all x4, waiting for transfers between devices, all_to_all(): return lax.all_to_all(block, 'seq', split_axis=0, concat_axis=0, tiled=True)  58.8 us
    ppermute x32, starting transfers between devices, exchange(): return lax.ppermute(block, axis, [(i, i ^ bit) for i in range(size)])  40.9 us
    pallas_call x1, Pallas kernels, attention_backward(): pl.pallas_call(functools.partial(backward_kernel, heads, mixing), grid=(r...  33.5 us
    pallas_call x1, Pallas kernels, attention_forward(): pl.pallas_call(functools.partial(forward_kernel, heads, mixing), grid=(ro...  27.5 us
    all_to_all x4, starting transfers between devices, all_to_all(): return lax.all_to_all(block, 'seq', split_axis=0, concat_axis=0, tiled=True)  19.2 us
    dot_general x7, matrix products, matmul(): return jnp.dot(left, right, preferred_element_type=F32)  10.4 us
    dot_general x7, matrix products, matmul_right(): lax.dot_general(left, right, (((1,), (1,)), ((), ())), preferred_element_...  10.3 us
  transfers between devices with their start and end apart: 54, of which 30 were waited for; matrix products, arithmetic and copies ran while one was open for 24% of the time, Pallas kernels for 15%

profile of v4, /device:TPU:0, one launch (start us, length us, event | category | flops | bytes accessed | tf_op | source)
XLA Modules:
  0.0 402.6 jit_solution(11928810119599454121)
XLA Ops:
  13.0 2.9 collective-permute-start.3
  18.8 4.4 %collective-permute-done.2 = bf16[1,2,1,1,1,40,512]{6,5,4,3,2,1,0:T(8,128)(2,1)S(1)} collective-permute-done((bf16[1,2,1,1,1,40,512]{6,5,4,3,2,1,0:T(8,128)(2,1)S(1)}, bf16[1,2,1,1,1,40,512]{6,5,4,3,2,1,0:T(8,128)(2,1)S(1)}, u32[]{:S(2)}, u32[]{:S(2)}) %collective-permute-start.2) | collective-permute-done | bytes 81952 | tf_op jit(solution)/shard_map/ppermute | solution.py:64
  25.8 5.8 %collective-permute-done.5 = bf16[2,2,1,1,1,32,512]{6,5,4,3,2,1,0:T(8,128)(2,1)S(1)} collective-permute-done((bf16[2,2,1,1,1,32,512]{6,5,4,3,2,1,0:T(8,128)(2,1)S(1)}, bf16[2,2,1,1,1,32,512]{6,5,4,3,2,1,0:T(8,128)(2,1)S(1)}, u32[]{:S(2)}, u32[]{:S(2)}) %collective-permute-start.5) | collective-permute-done | bytes 131104 | tf_op jit(solution)/shard_map/ppermute | solution.py:64
  49.1 6.2 %collective-permute-done.9 = bf16[2,2,2,1,2,32,512]{6,5,4,3,2,1,0:T(8,128)(2,1)S(1)} collective-permute-done((bf16[2,2,2,1,2,32,512]{6,5,4,3,2,1,0:T(8,128)(2,1)}, bf16[2,2,2,1,2,32,512]{6,5,4,3,2,1,0:T(8,128)(2,1)S(1)}, u32[]{:S(2)}, u32[]{:S(2)}) %collective-permute-start.9) | collective-permute-done | bytes 524320 | tf_op jit(solution)/shard_map/ppermute | solution.py:64
  63.2 3.0 fusion
  69.4 6.6 %all-to-all-start = ((bf16[8,128,512]{2,1,0:T(8,128)(2,1)}), bf16[8,128,512]{2,1,0:T(8,128)(2,1)}, u32[]{:S(2)}, u32[]{:S(2)}) async-start(bf16[8,128,512]{2,1,0:T(8,128)(2,1)} %bitcast.54), calls=%async_computation | async-start | bytes 2097152 | tf_op jit(solution)/shard_map/all_to_all | solution.py:139
  77.0 3.9 select_reduce_fusion
  86.9 29.4 %all-to-all-done = bf16[8,128,512]{2,1,0:T(8,128)(2,1)} async-done(((bf16[8,128,512]{2,1,0:T(8,128)(2,1)}), bf16[8,128,512]{2,1,0:T(8,128)(2,1)}, u32[]{:S(2)}, u32[]{:S(2)}) %all-to-all-start) | async-done | bytes 1048608 | tf_op jit(solution)/shard_map/all_to_all | solution.py:139
  116.3 27.5 %shard_map.280 = (bf16[4,1024,256]{2,1,0:T(8,128)(2,1)}, f32[4,1024,128]{2,1,0:T(8,128)}, bf16[1024,256]{1,0:T(8,128)(2,1)}, bf16[4,1600,768]{2,1,0:T(8,128)(2,1)}, f32[4,12,8,128]{3,2,1,0:T(8,128)}) custom-call(bf16[1024,512]{1,0:T(8,128)(2,1)} %bitcast.55.qv_ref, s32[4,1,1024]{2,1,0:T(1,128)} %bitcast.383, s32[4,1024,1]{2,1,0:T(8,128)} %copy.216.column_ref, ...), custom_call_target="tpu_custom_call" | custom-call | flops 12482248704 | bytes 20971520 | tf_op jit(solution)/shard_map/pallas_call | solution.py:501
  143.8 3.7 all-to-all-start.1
  153.9 20.9 %all-to-all-done.1 = bf16[8,128,256]{2,1,0:T(8,128)(2,1)S(1)} async-done(((bf16[8,128,256]{2,1,0:T(8,128)(2,1)}), bf16[8,128,256]{2,1,0:T(8,128)(2,1)S(1)}, u32[]{:S(2)}, u32[]{:S(2)}) %all-to-all-start.1) | async-done | bytes 524320 | tf_op jit(solution)/shard_map/all_to_all | solution.py:139
  185.9 2.7 fusion.104
  198.1 5.0 %collective-permute-done.17 = bf16[256,1024]{1,0:T(8,128)(2,1)S(1)} collective-permute-done((bf16[256,1024]{1,0:T(8,128)(2,1)S(1)}, bf16[256,1024]{1,0:T(8,128)(2,1)S(1)}, u32[]{:S(2)}, u32[]{:S(2)}) %collective-permute-start.17) | collective-permute-done | bytes 524320 | tf_op jit(solution)/shard_map/ppermute | solution.py:64
  222.3 7.9 %collective-permute-done.25 = bf16[256,1024]{1,0:T(8,128)(2,1)} collective-permute-done((bf16[256,1024]{1,0:T(8,128)(2,1)}, bf16[256,1024]{1,0:T(8,128)(2,1)}, u32[]{:S(2)}, u32[]{:S(2)}) %collective-permute-start.25) | collective-permute-done | bytes 524320 | tf_op jit(solution)/shard_map/ppermute | solution.py:64
  237.6 4.1 %all-to-all-start.2 = ((bf16[8,128,256]{2,1,0:T(8,128)(2,1)}), bf16[8,128,256]{2,1,0:T(8,128)(2,1)}, u32[]{:S(2)}, u32[]{:S(2)}) async-start(bf16[8,128,256]{2,1,0:T(8,128)(2,1)} %bitcast.97), calls=%async_computation.2 | async-start | bytes 1048576 | tf_op jit(solution)/shard_map/all_to_all | solution.py:139
  246.2 12.8 %collective-permute-done.27 = bf16[2,2,2,32,1024]{4,3,0,1,2:T(8,128)(2,1)} collective-permute-done((bf16[2,2,2,32,1024]{4,3,0,1,2:T(8,128)(2,1)}, bf16[2,2,2,32,1024]{4,3,0,1,2:T(8,128)(2,1)}, u32[]{:S(2)}, u32[]{:S(2)}) %collective-permute-start.27) | collective-permute-done | bytes 524320 | tf_op jit(solution)/shard_map/ppermute | solution.py:64
  264.5 33.5 %shard_map.281 = bf16[1024,512]{1,0:T(8,128)(2,1)} custom-call(bf16[1024,256]{1,0:T(8,128)(2,1)} %bitcast.98.d_mixed_ref, bf16[4,1024,256]{2,1,0:T(8,128)(2,1)} %get-tuple-element.88.out_ref, f32[4,1024,128]{2,1,0:T(8,128)} %get-tuple-element.89.weight_ref, f32[8,128]{1,0:T(8,128)} %broadcast_in_dim.88.dot_ref, ...), custom_call_target="tpu_custom_call" | custom-call | flops 14294188032 | bytes 20971520 | tf_op jit(solution)/shard_map/pallas_call | solution.py:527
  298.1 4.7 %all-to-all-start.3 = ((bf16[8,128,512]{2,1,0:T(8,128)(2,1)}), bf16[8,128,512]{2,1,0:T(8,128)(2,1)S(1)}, u32[]{:S(2)}, u32[]{:S(2)}) async-start(bf16[8,128,512]{2,1,0:T(8,128)(2,1)} %bitcast.363), calls=%async_computation.3 | async-start | bytes 2097152 | tf_op jit(solution)/shard_map/all_to_all | solution.py:139
  302.9 3.2 fusion.114
  321.8 8.5 %all-to-all-done.3 = bf16[8,128,512]{2,1,0:T(8,128)(2,1)S(1)} async-done(((bf16[8,128,512]{2,1,0:T(8,128)(2,1)}), bf16[8,128,512]{2,1,0:T(8,128)(2,1)S(1)}, u32[]{:S(2)}, u32[]{:S(2)}) %all-to-all-start.3) | async-done | bytes 1048608 | tf_op jit(solution)/shard_map/all_to_all | solution.py:139
  339.3 2.7 add_add_fusion
  342.2 4.0 collective-permute-done.32
  346.8 2.7 bitcast_add_fusion.1
  362.3 2.9 collective-permute-done.33
  (385 shorter events, 177.9 us)
Async XLA Ops:
  7.2 168.9 %all-gather.3.cloned.1.call-start = ((), (), s32[]{:S(2)}) async-start(), calls=%async_computation.6 | async-start | bytes 5898240 | tf_op jit(solution)/shard_map/all_gather | solution.py:677
  35.3 11.4 %collective-permute-start.12 = (bf16[32,1024]{1,0:T(8,128)(2,1)}, bf16[32,1024]{1,0:T(8,128)(2,1)}, u32[]{:S(2)}, u32[]{:S(2)}) collective-permute-start(bf16[32,1024]{1,0:T(8,128)(2,1)} %param.27), channel_id=1, source_target_pairs={{0,16},{16,0},{1,17},{17,1},{2,18},{18,2},{3,19},{19,3},{4,20},{20... | collective-permute-start | bytes 196616 | tf_op jit(solution)/shard_map/ppermute | solution.py:64
  37.2 8.5 %collective-permute-start.10 = (bf16[2,32,1024]{2,0,1:T(2,128)(2,1)S(1)}, bf16[2,32,1024]{2,0,1:T(2,128)(2,1)S(1)}, u32[]{:S(2)}, u32[]{:S(2)}) collective-permute-start(bf16[2,32,1024]{2,0,1:T(2,128)(2,1)S(1)} %get-tuple-element.160), channel_id=1, source_target_pairs={{0,16},{16,0},{1,17},{17,1},{2,18},{18,2},{3,19},{19,3},{4,20},{20... | collective-permute-start | bytes 393224 | tf_op jit(solution)/shard_map/ppermute | solution.py:64
  42.6 14.2 %collective-permute-start.8 = (bf16[1,2,2,2,2,40,512]{6,5,4,3,2,1,0:T(8,128)(2,1)}, bf16[1,2,2,2,2,40,512]{6,5,4,3,2,1,0:T(8,128)(2,1)}, u32[]{:S(2)}, u32[]{:S(2)}) collective-permute-start(bf16[1,2,2,2,2,40,512]{6,5,4,3,2,1,0:T(8,128)(2,1)} %constant_dynamic-slice_fusion.26), channel_id=1, source_target_pairs={{0,16},{16,0},{1,17},{17,1},{2,18},{18,2},{3,19},{19,3},{4,20},{20... | collective-permute-start | bytes 1966088 | tf_op jit(solution)/shard_map/ppermute | solution.py:64
  43.9 11.4 %collective-permute-start.9 = (bf16[2,2,2,1,2,32,512]{6,5,4,3,2,1,0:T(8,128)(2,1)}, bf16[2,2,2,1,2,32,512]{6,5,4,3,2,1,0:T(8,128)(2,1)S(1)}, u32[]{:S(2)}, u32[]{:S(2)}) collective-permute-start(bf16[2,2,2,1,2,32,512]{6,5,4,3,2,1,0:T(8,128)(2,1)} %constant_dynamic-slice_fusion.25), channel_id=1, source_target_pairs={{0,2},{1,3},{2,0},{3,1},{4,6},{5,7},{6,4},{7,5},{8,10},{9,11},{10,... | collective-permute-start | bytes 1572872 | tf_op jit(solution)/shard_map/ppermute | solution.py:64
  59.1 88.6 %collective-permute-start.14 = (bf16[256,1024]{1,0:T(8,128)(2,1)}, bf16[256,1024]{1,0:T(8,128)(2,1)}, u32[]{:S(2)}, u32[]{:S(2)}) collective-permute-start(bf16[256,1024]{1,0:T(8,128)(2,1)} %bitcast.74), channel_id=1, source_target_pairs={{0,16},{16,0},{1,17},{17,1},{2,18},{18,2},{3,19},{19,3},{4,20},{20... | collective-permute-start | bytes 1572872 | tf_op jit(solution)/shard_map/ppermute | solution.py:64
  69.4 46.9 %all-to-all-start = ((bf16[8,128,512]{2,1,0:T(8,128)(2,1)}), bf16[8,128,512]{2,1,0:T(8,128)(2,1)}, u32[]{:S(2)}, u32[]{:S(2)}) async-start(bf16[8,128,512]{2,1,0:T(8,128)(2,1)} %bitcast.54), calls=%async_computation | async-start | bytes 2097152 | tf_op jit(solution)/shard_map/all_to_all | solution.py:139
  143.8 30.9 %all-to-all-start.1 = ((bf16[8,128,256]{2,1,0:T(8,128)(2,1)}), bf16[8,128,256]{2,1,0:T(8,128)(2,1)S(1)}, u32[]{:S(2)}, u32[]{:S(2)}) async-start(bf16[8,128,256]{2,1,0:T(8,128)(2,1)} %bitcast.374), calls=%async_computation.1 | async-start | bytes 1048576 | tf_op jit(solution)/shard_map/all_to_all | solution.py:139
  188.8 14.3 %collective-permute-start.17 = (bf16[256,1024]{1,0:T(8,128)(2,1)S(1)}, bf16[256,1024]{1,0:T(8,128)(2,1)S(1)}, u32[]{:S(2)}, u32[]{:S(2)}) collective-permute-start(bf16[256,1024]{1,0:T(8,128)(2,1)S(1)} %add_convert_fusion.1), channel_id=1, source_target_pairs={{0,16},{16,0},{1,17},{17,1},{2,18},{18,2},{3,19},{19,3},{4,20},{20... | collective-permute-start | bytes 1572872 | tf_op jit(solution)/shard_map/ppermute | solution.py:64
  211.9 18.3 %collective-permute-start.23 = (f32[256,1024]{1,0:T(8,128)}, f32[256,1024]{1,0:T(8,128)}, u32[]{:S(2)}, u32[]{:S(2)}) collective-permute-start(f32[256,1024]{1,0:T(8,128)} %slice.305), channel_id=1, source_target_pairs={{0,8},{8,0},{1,9},{9,1},{2,10},{10,2},{3,11},{11,3},{4,12},{12,4},... | collective-permute-start | bytes 3145736 | tf_op jit(solution)/shard_map/ppermute | solution.py:55
  215.9 14.3 %collective-permute-start.25 = (bf16[256,1024]{1,0:T(8,128)(2,1)}, bf16[256,1024]{1,0:T(8,128)(2,1)}, u32[]{:S(2)}, u32[]{:S(2)}) collective-permute-start(bf16[256,1024]{1,0:T(8,128)(2,1)} %fusion.40), channel_id=1, source_target_pairs={{0,16},{16,0},{1,17},{17,1},{2,18},{18,2},{3,19},{19,3},{4,20},{20... | collective-permute-start | bytes 1572872 | tf_op jit(solution)/shard_map/ppermute | solution.py:64
  237.6 23.6 %all-to-all-start.2 = ((bf16[8,128,256]{2,1,0:T(8,128)(2,1)}), bf16[8,128,256]{2,1,0:T(8,128)(2,1)}, u32[]{:S(2)}, u32[]{:S(2)}) async-start(bf16[8,128,256]{2,1,0:T(8,128)(2,1)} %bitcast.97), calls=%async_computation.2 | async-start | bytes 1048576 | tf_op jit(solution)/shard_map/all_to_all | solution.py:139
  241.7 115.8 %reduce-scatter.2.cloned.1.call-start = ((), (), s32[]{:S(2)}) async-start(), calls=%async_computation.5 | async-start | bytes 4718592 | tf_op jit(solution)/shard_map/reduce_scatter | solution.py:820
  244.7 14.3 %collective-permute-start.27 = (bf16[2,2,2,32,1024]{4,3,0,1,2:T(8,128)(2,1)}, bf16[2,2,2,32,1024]{4,3,0,1,2:T(8,128)(2,1)}, u32[]{:S(2)}, u32[]{:S(2)}) collective-permute-start(bf16[2,2,2,32,1024]{4,3,0,1,2:T(8,128)(2,1)} %fusion.52), channel_id=1, source_target_pairs={{0,16},{16,0},{1,17},{17,1},{2,18},{18,2},{3,19},{19,3},{4,20},{20... | collective-permute-start | bytes 1572872 | tf_op jit(solution)/shard_map/ppermute | solution.py:64
  262.3 35.7 %collective-permute-start.28 = (bf16[2,2,32,1024]{3,2,0,1:T(8,128)(2,1)S(1)}, bf16[2,2,32,1024]{3,2,0,1:T(8,128)(2,1)S(1)}, u32[]{:S(2)}, u32[]{:S(2)}) collective-permute-start(bf16[2,2,32,1024]{3,2,0,1:T(8,128)(2,1)S(1)} %fusion.55), channel_id=1, source_target_pairs={{0,1},{1,0},{2,3},{3,2},{4,5},{5,4},{6,7},{7,6},{8,9},{9,8},{10,11... | collective-permute-start | bytes 786440 | tf_op jit(solution)/shard_map/ppermute | solution.py:64
  298.1 32.2 %all-to-all-start.3 = ((bf16[8,128,512]{2,1,0:T(8,128)(2,1)}), bf16[8,128,512]{2,1,0:T(8,128)(2,1)S(1)}, u32[]{:S(2)}, u32[]{:S(2)}) async-start(bf16[8,128,512]{2,1,0:T(8,128)(2,1)} %bitcast.363), calls=%async_computation.3 | async-start | bytes 2097152 | tf_op jit(solution)/shard_map/all_to_all | solution.py:139
  312.3 26.5 %collective-permute-start.19 = (f32[256,1024]{1,0:T(8,128)}, f32[256,1024]{1,0:T(8,128)}, u32[]{:S(2)}, u32[]{:S(2)}) collective-permute-start(f32[256,1024]{1,0:T(8,128)} %slice.300), channel_id=1, source_target_pairs={{0,8},{8,0},{1,9},{9,1},{2,10},{10,2},{3,11},{11,3},{4,12},{12,4},... | collective-permute-start | bytes 3145736 | tf_op jit(solution)/shard_map/ppermute | solution.py:55
  318.9 19.9 %collective-permute-start.22 = (bf16[256,1024]{1,0:T(8,128)(2,1)}, bf16[256,1024]{1,0:T(8,128)(2,1)}, u32[]{:S(2)}, u32[]{:S(2)}) collective-permute-start(bf16[256,1024]{1,0:T(8,128)(2,1)} %fusion.41), channel_id=1, source_target_pairs={{0,16},{16,0},{1,17},{17,1},{2,18},{18,2},{3,19},{19,3},{4,20},{20... | collective-permute-start | bytes 1572872 | tf_op jit(solution)/shard_map/ppermute | solution.py:64
  333.2 13.6 %collective-permute-start.30 = (bf16[2,2,2,2,32,512]{5,4,0,1,2,3:T(8,128)(2,1)}, bf16[2,2,2,2,32,512]{5,4,0,1,2,3:T(8,128)(2,1)}, u32[]{:S(2)}, u32[]{:S(2)}) collective-permute-start(bf16[2,2,2,2,32,512]{5,4,0,1,2,3:T(8,128)(2,1)} %fusion.53), channel_id=1, source_target_pairs={{0,16},{16,0},{1,17},{17,1},{2,18},{18,2},{3,19},{19,3},{4,20},{20... | collective-permute-start | bytes 1572872 | tf_op jit(solution)/shard_map/ppermute | solution.py:64
  336.4 13.2 %collective-permute-start.31 = (bf16[2,2,2,2,32,512]{5,4,1,2,3,0:T(8,128)(2,1)}, bf16[2,2,2,2,32,512]{5,4,1,2,3,0:T(8,128)(2,1)}, u32[]{:S(2)}, u32[]{:S(2)}) collective-permute-start(bf16[2,2,2,2,32,512]{5,4,1,2,3,0:T(8,128)(2,1)} %fusion.54), channel_id=1, source_target_pairs={{0,1},{1,0},{2,3},{3,2},{4,5},{5,4},{6,7},{7,6},{8,9},{9,8},{10,11... | collective-permute-start | bytes 1572872 | tf_op jit(solution)/shard_map/ppermute | solution.py:64
  337.0 9.2 %collective-permute-start.32 = (bf16[32,1024]{1,0:T(8,128)(2,1)S(1)}, bf16[32,1024]{1,0:T(8,128)(2,1)S(1)}, u32[]{:S(2)}, u32[]{:S(2)}) collective-permute-start(bf16[32,1024]{1,0:T(8,128)(2,1)S(1)} %fusion.68), channel_id=1, source_target_pairs={{0,4},{1,5},{2,6},{3,7},{4,0},{5,1},{6,2},{7,3},{8,12},{9,13},{10,... | collective-permute-start | bytes 196616 | tf_op jit(solution)/shard_map/ppermute | solution.py:64
  338.8 13.4 %collective-permute-start.35 = (f32[256,1024]{1,0:T(8,128)}, f32[256,1024]{1,0:T(8,128)S(1)}, u32[]{:S(2)}, u32[]{:S(2)}) collective-permute-start(f32[256,1024]{1,0:T(8,128)} %slice.376), channel_id=1, source_target_pairs={{0,8},{8,0},{1,9},{9,1},{2,10},{10,2},{3,11},{11,3},{4,12},{12,4},... | collective-permute-start | bytes 3145736 | tf_op jit(solution)/shard_map/ppermute | solution.py:55
  369.2 13.9 %collective-permute-start.41 = (bf16[2,2,32,512]{3,2,0,1:T(8,128)(2,1)S(1)}, bf16[2,2,32,512]{3,2,0,1:T(8,128)(2,1)S(1)}, u32[]{:S(2)}, u32[]{:S(2)}) collective-permute-start(bf16[2,2,32,512]{3,2,0,1:T(8,128)(2,1)S(1)} %fusion.61), channel_id=1, source_target_pairs={{0,2},{1,3},{2,0},{3,1},{4,6},{5,7},{6,4},{7,5},{8,10},{9,11},{10,... | collective-permute-start | bytes 393224 | tf_op jit(solution)/shard_map/ppermute | solution.py:64
  371.8 11.4 %collective-permute-start.42 = (bf16[2,2,32,512]{3,2,0,1:T(8,128)(2,1)S(1)}, bf16[2,2,32,512]{3,2,0,1:T(8,128)(2,1)S(1)}, u32[]{:S(2)}, u32[]{:S(2)}) collective-permute-start(bf16[2,2,32,512]{3,2,0,1:T(8,128)(2,1)S(1)} %fusion.62), channel_id=1, source_target_pairs={{0,2},{1,3},{2,0},{3,1},{4,6},{5,7},{6,4},{7,5},{8,10},{9,11},{10,... | collective-permute-start | bytes 393224 | tf_op jit(solution)/shard_map/ppermute | solution.py:64
  (67 other events, 649.8 us)
Sparse Core Ops, SparseCore 0:
  59.2 116.9 all-gather.2
  246.4 101.9 reduce-scatter.1

commit v5 on v4

--- a/solution.py
+++ b/solution.py
@@ -83,9 +83,9 @@
 
 
 class Gather:
-    def __init__(self, block):
-        self.dims = half_steps("chip") + [None] + half_steps("seq")
-        self.tail = list(block.shape[1:])
+    def __init__(self, block, whole_core=True):
+        self.dims = half_steps("chip") + [None] * whole_core + half_steps("seq")
+        self.tail = list(block.shape[1:] if whole_core else block.shape)
         self.sizes = [2 if dim is None else 1 for dim in self.dims] + self.tail
         self.starts = [0 if dim is None else side(*dim) for dim in self.dims] + [0] * len(self.tail)
         buffer = jnp.zeros([2] * len(self.dims) + self.tail, block.dtype)
@@ -650,7 +650,10 @@
     for k in range(len(seq_steps) + len(chip_steps)):
         for pair, chain in enumerate(chains):
             chain.step(gather_orders[pair % 2][k])
-        together(chains)
+        later = [Held(w_inner)] if k == 0 else []
+        together(chains + later)
+        if later:
+            w_inner = later[0].held
     small = chains[0].held.reshape(-1, shard + extra, 2 * width)[:, shard:]
     small = jnp.concatenate([small[:, :, k * tok : (k + 1) * tok] for k in range(fold)], 1)
     joined = [chains[0].held.reshape(-1, shard + extra, 2 * width)[:, :shard]]
@@ -669,8 +672,7 @@
 
     inner_pieces = jnp.moveaxis(w_inner.reshape(shard, chips, 2, quarter), 0, 2)
     inner_pieces = trade_quarters(inner_pieces).reshape(-1, features)
-    output_pieces = both_chips(w_output).reshape(-1, features)
-    bundle = jnp.concatenate([w_outer, inner_pieces, output_pieces], 0)
+    bundle = jnp.concatenate([w_outer, inner_pieces], 0)
     bundle, *joined = lax.optimization_barrier([bundle] + joined)
     grad_rows = w_outer.shape[0]
     cuts = [grad_rows, grad_rows + inner_pieces.shape[0]]
@@ -678,8 +680,6 @@
     full_outer = gathered[:, : cuts[0]].reshape(quarter, features)
     full_inner = gathered[:, cuts[0] : cuts[1]].reshape(devices, 2 * chips, shard, quarter)
     full_inner = jnp.swapaxes(full_inner, 0, 1).reshape(features, quarter)
-    full_output = gathered[:, cuts[1] :].reshape(devices, chips, shard, features)
-    full_output = jnp.swapaxes(full_output, 0, 1).reshape(chips * width, features)
 
     unit = lax.axis_index("seq") // sharing
     sequence = unit // chips
@@ -747,8 +747,17 @@
     def join_heads(parts):
         return [jnp.concatenate([part[pair] for part in parts], 1) for pair in range(chips)]
 
+    late_output, *projected = lax.optimization_barrier([w_output] + projected)
+    output_weights = Gather(late_output, whole_core=False)
+    arrived = by_heads(projected, 2 * at_call * HEAD_DIM)
+    for step in seq_steps[:1] + seq_steps[-1:] + mid_steps:
+        output_weights.step(step)
+    output_weights.held, arrived[0] = lax.optimization_barrier((output_weights.held, arrived[0]))
+    for step in chip_steps:
+        output_weights.step(step)
+    full_output = output_weights.held.reshape(chips * width, features)
     kept, mixed = [], []
-    for qv in by_heads(projected, 2 * at_call * HEAD_DIM):
+    for qv in arrived:
         round_out, weights, head_mixed, placed, slot_spread = attention_forward(
             qv, places, key_bias, mixing
         )
@@ -764,7 +773,9 @@
     mixed = jnp.concatenate(join_heads(mixed), 1)
     cot_own = grad_two.reshape(own_rows, features)
     parts_cot = [near(cot_own)] + ([far(cot_own)] if chips == 2 else [])
-    mixed, parts_cot = lax.optimization_barrier((mixed, parts_cot))
+    mixed, parts_cot, full_inner, full_outer = lax.optimization_barrier(
+        (mixed, parts_cot, full_inner, full_outer)
+    )
 
     def core_sum(value):
         return value[:own_rows] + swap(value[own_rows:])

time: 410 us -> 408 us (level)
  waiting for transfers between devices: 131 us -> 109 us
  local copies, waits for them, and re-layouts: 49.6 us -> 64.2 us
    all_to_all x4, waiting for transfers between devices: 58.8 us -> 11.1 us  [all_to_all(): return lax.all_to_all(block, 'seq', split_axis=0, concat_axis=0, tiled=True)]
    ppermute x32 -> x35, waiting for transfers between devices: 61.8 us -> 91.7 us  [exchange(): return lax.ppermute(block, axis, [(i, i ^ bit) for i in range(size)])]
    dynamic_slice x8 -> x12, local copies, waits for them, and re-layouts: 2.56 us -> 7.7 us  [step(): lax.dynamic_slice(self.held, self.starts, self.sizes)]
    dynamic_update_slice x8 -> x12, local copies, waits for them, and re-layouts: 2.24 us -> 7.04 us  [step(): self.held = lax.dynamic_update_slice(self.held, piece, opposite)]
    ppermute x32 -> x35, starting transfers between devices: 40.9 us -> 44.8 us  [exchange(): return lax.ppermute(block, axis, [(i, i ^ bit) for i in range(size)])]
  transfers between devices with their start and end apart: 54 -> 57, of which waited for: 30 -> 28; matrix products, arithmetic and copies ran while one was open for 24% -> 28% of each run, Pallas kernels for 15% -> 15%
where the time goes in v5:
time: 408 us; the launch traced here: 400 us
  waiting for transfers between devices  109 us (27%)
  starting transfers between devices  65.9 us (16%)
  local copies, waits for them, and re-layouts  64.2 us (16%)
  Pallas kernels  61 us (15%)
  other arithmetic  52.7 us (13%)
  matrix products  31.5 us (8%)
  between operations  15.8 us (4%)
    ppermute x35, waiting for transfers between devices, exchange(): return lax.ppermute(block, axis, [(i, i ^ bit) for i in range(size)])  91.7 us
    ppermute x35, starting transfers between devices, exchange(): return lax.ppermute(block, axis, [(i, i ^ bit) for i in range(size)])  44.8 us
    pallas_call x1, Pallas kernels, attention_backward(): pl.pallas_call(functools.partial(backward_kernel, heads, mixing), grid=(r...  33.5 us
    pallas_call x1, Pallas kernels, attention_forward(): pl.pallas_call(functools.partial(forward_kernel, heads, mixing), grid=(ro...  27.5 us
    all_to_all x4, starting transfers between devices, all_to_all(): return lax.all_to_all(block, 'seq', split_axis=0, concat_axis=0, tiled=True)  18.5 us
    dot_general x7, matrix products, matmul(): return jnp.dot(left, right, preferred_element_type=F32)  11.7 us
    dot_general x7, matrix products, matmul_right(): lax.dot_general(left, right, (((1,), (1,)), ((), ())), preferred_element_...  11.4 us
    all_to_all x4, waiting for transfers between devices, all_to_all(): return lax.all_to_all(block, 'seq', split_axis=0, concat_axis=0, tiled=True)  11.1 us
  transfers between devices with their start and end apart: 57, of which 28 were waited for; matrix products, arithmetic and copies ran while one was open for 28% of the time, Pallas kernels for 15%

profile of v5, /device:TPU:0, one launch (start us, length us, event | category | flops | bytes accessed | tf_op | source)
XLA Modules:
  0.0 400.3 jit_solution(5860741429922938366)
XLA Ops:
  19.7 4.6 %collective-permute-done.2 = bf16[1,2,1,1,1,40,512]{6,5,4,3,2,1,0:T(8,128)(2,1)S(1)} collective-permute-done((bf16[1,2,1,1,1,40,512]{6,5,4,3,2,1,0:T(8,128)(2,1)S(1)}, bf16[1,2,1,1,1,40,512]{6,5,4,3,2,1,0:T(8,128)(2,1)S(1)}, u32[]{:S(2)}, u32[]{:S(2)}) %collective-permute-start.2) | collective-permute-done | bytes 81952 | tf_op jit(solution)/shard_map/ppermute | solution.py:64
  29.0 4.7 %collective-permute-done.5 = bf16[2,2,1,1,1,32,512]{6,5,4,3,2,1,0:T(8,128)(2,1)S(1)} collective-permute-done((bf16[2,2,1,1,1,32,512]{6,5,4,3,2,1,0:T(8,128)(2,1)}, bf16[2,2,1,1,1,32,512]{6,5,4,3,2,1,0:T(8,128)(2,1)S(1)}, u32[]{:S(2)}, u32[]{:S(2)}) %collective-permute-start.5) | collective-permute-done | bytes 131104 | tf_op jit(solution)/shard_map/ppermute | solution.py:64
  41.2 3.7 collective-permute-done.6
  54.2 4.8 %collective-permute-done.9 = bf16[2,2,2,1,2,32,512]{6,5,4,3,2,1,0:T(8,128)(2,1)} collective-permute-done((bf16[2,2,2,1,2,32,512]{6,5,4,3,2,1,0:T(8,128)(2,1)}, bf16[2,2,2,1,2,32,512]{6,5,4,3,2,1,0:T(8,128)(2,1)}, u32[]{:S(2)}, u32[]{:S(2)}) %collective-permute-start.9) | collective-permute-done | bytes 524320 | tf_op jit(solution)/shard_map/ppermute | solution.py:64
  60.1 3.7 collective-permute-done.8
  67.0 3.1 fusion
  76.7 4.4 %all-to-all-start = ((bf16[8,128,512]{2,1,0:T(8,128)(2,1)}), bf16[8,128,512]{2,1,0:T(8,128)(2,1)}, u32[]{:S(2)}, u32[]{:S(2)}) async-start(bf16[8,128,512]{2,1,0:T(8,128)(2,1)} %bitcast.52), calls=%async_computation | async-start | bytes 2097152 | tf_op jit(solution)/shard_map/all_to_all | solution.py:139
  87.0 3.8 select_reduce_fusion
  100.2 13.5 %collective-permute-done.14 = bf16[1,2,1,2,32,1024]{5,4,3,2,1,0:T(8,128)(2,1)} collective-permute-done((bf16[1,2,1,2,32,1024]{5,4,3,2,1,0:T(8,128)(2,1)}, bf16[1,2,1,2,32,1024]{5,4,3,2,1,0:T(8,128)(2,1)}, u32[]{:S(2)}, u32[]{:S(2)}) %collective-permute-start.14) | collective-permute-done | bytes 262176 | tf_op jit(solution)/shard_map/ppermute | solution.py:64
  117.6 27.5 %shard_map.280 = (bf16[4,1024,256]{2,1,0:T(8,128)(2,1)}, f32[4,1024,128]{2,1,0:T(8,128)}, bf16[1024,256]{1,0:T(8,128)(2,1)}, bf16[4,1600,768]{2,1,0:T(8,128)(2,1)}, f32[4,12,8,128]{3,2,1,0:T(8,128)}) custom-call(bf16[1024,512]{1,0:T(8,128)(2,1)} %bitcast.53.qv_ref, s32[4,1,1024]{2,1,0:T(1,128)} %bitcast.377, s32[4,1024,1]{2,1,0:T(8,128)} %copy.212.column_ref, ...), custom_call_target="tpu_custom_call" | custom-call | flops 12482248704 | bytes 20971520 | tf_op jit(solution)/shard_map/pallas_call | solution.py:501
  145.1 5.1 %all-to-all-start.1 = ((bf16[8,128,256]{2,1,0:T(8,128)(2,1)}), bf16[8,128,256]{2,1,0:T(8,128)(2,1)S(1)}, u32[]{:S(2)}, u32[]{:S(2)}) async-start(bf16[8,128,256]{2,1,0:T(8,128)(2,1)} %bitcast.368), calls=%async_computation.1 | async-start | bytes 1048576 | tf_op jit(solution)/shard_map/all_to_all | solution.py:139
  156.1 9.6 %collective-permute-done.18 = bf16[1,2,2,2,32,1024]{5,4,3,2,1,0:T(8,128)(2,1)S(1)} collective-permute-done((bf16[1,2,2,2,32,1024]{5,4,3,2,1,0:T(8,128)(2,1)S(1)}, bf16[1,2,2,2,32,1024]{5,4,3,2,1,0:T(8,128)(2,1)S(1)}, u32[]{:S(2)}, u32[]{:S(2)}) %collective-permute-start.18) | collective-permute-done | bytes 524320 | tf_op jit(solution)/shard_map/ppermute | solution.py:64
  168.7 4.3 %fusion.104 = (bf16[8,128,1024]{2,1,0:T(8,128)(2,1)}, bf16[8,128,1024]{2,1,0:T(8,128)(2,1)S(1)}) fusion(bf16[8,256,1024]{2,1,0:T(8,128)(2,1)} %bitcast.341), kind=kLoop, calls=%fused_computation.318 | loop fusion | bytes 8388608 | tf_op jit(solution)/shard_map/slice | solution.py:680
  193.7 4.7 %collective-permute-done.20 = bf16[256,1024]{1,0:T(8,128)(2,1)S(1)} collective-permute-done((bf16[256,1024]{1,0:T(8,128)(2,1)S(1)}, bf16[256,1024]{1,0:T(8,128)(2,1)S(1)}, u32[]{:S(2)}, u32[]{:S(2)}) %collective-permute-start.20) | collective-permute-done | bytes 524320 | tf_op jit(solution)/shard_map/ppermute | solution.py:64
  217.4 7.9 %collective-permute-done.28 = bf16[256,1024]{1,0:T(8,128)(2,1)} collective-permute-done((bf16[256,1024]{1,0:T(8,128)(2,1)}, bf16[256,1024]{1,0:T(8,128)(2,1)}, u32[]{:S(2)}, u32[]{:S(2)}) %collective-permute-start.28) | collective-permute-done | bytes 524320 | tf_op jit(solution)/shard_map/ppermute | solution.py:64
  234.1 4.1 %all-to-all-start.2 = ((bf16[8,128,256]{2,1,0:T(8,128)(2,1)}), bf16[8,128,256]{2,1,0:T(8,128)(2,1)}, u32[]{:S(2)}, u32[]{:S(2)}) async-start(bf16[8,128,256]{2,1,0:T(8,128)(2,1)} %bitcast.93), calls=%async_computation.2 | async-start | bytes 1048576 | tf_op jit(solution)/shard_map/all_to_all | solution.py:139
  242.8 12.8 %collective-permute-done.30 = bf16[2,2,2,32,1024]{4,3,0,1,2:T(8,128)(2,1)} collective-permute-done((bf16[2,2,2,32,1024]{4,3,0,1,2:T(8,128)(2,1)}, bf16[2,2,2,32,1024]{4,3,0,1,2:T(8,128)(2,1)}, u32[]{:S(2)}, u32[]{:S(2)}) %collective-permute-start.30) | collective-permute-done | bytes 524320 | tf_op jit(solution)/shard_map/ppermute | solution.py:64
  261.0 33.5 %shard_map.281 = bf16[1024,512]{1,0:T(8,128)(2,1)} custom-call(bf16[1024,256]{1,0:T(8,128)(2,1)} %bitcast.94.d_mixed_ref, bf16[4,1024,256]{2,1,0:T(8,128)(2,1)} %get-tuple-element.104.out_ref, f32[4,1024,128]{2,1,0:T(8,128)} %get-tuple-element.105.weight_ref, f32[8,128]{1,0:T(8,128)} %broadcast_in_dim.92.dot_ref, ...), custom_call_target="tpu_custom_call" | custom-call | flops 14294188032 | bytes 20971520 | tf_op jit(solution)/shard_map/pallas_call | solution.py:527
  294.6 4.8 %all-to-all-start.3 = ((bf16[8,128,512]{2,1,0:T(8,128)(2,1)}), bf16[8,128,512]{2,1,0:T(8,128)(2,1)S(1)}, u32[]{:S(2)}, u32[]{:S(2)}) async-start(bf16[8,128,512]{2,1,0:T(8,128)(2,1)} %bitcast.357), calls=%async_computation.3 | async-start | bytes 2097152 | tf_op jit(solution)/shard_map/all_to_all | solution.py:139
  299.4 3.2 fusion.114
  318.0 6.7 %all-to-all-done.3 = bf16[8,128,512]{2,1,0:T(8,128)(2,1)S(1)} async-done(((bf16[8,128,512]{2,1,0:T(8,128)(2,1)}), bf16[8,128,512]{2,1,0:T(8,128)(2,1)S(1)}, u32[]{:S(2)}, u32[]{:S(2)}) %all-to-all-start.3) | async-done | bytes 1048608 | tf_op jit(solution)/shard_map/all_to_all | solution.py:139
  338.9 4.3 %collective-permute-done.35 = bf16[32,1024]{1,0:T(8,128)(2,1)S(1)} collective-permute-done((bf16[32,1024]{1,0:T(8,128)(2,1)S(1)}, bf16[32,1024]{1,0:T(8,128)(2,1)S(1)}, u32[]{:S(2)}, u32[]{:S(2)}) %collective-permute-start.35) | collective-permute-done | bytes 65568 | tf_op jit(solution)/shard_map/ppermute | solution.py:64
  360.2 3.4 collective-permute-done.36
  370.0 2.9 collective-permute-done.41
  (408 shorter events, 203.2 us)
Async XLA Ops:
  7.2 161.6 %all-gather.3.cloned.1.call-start = ((), (), s32[]{:S(2)}) async-start(), calls=%async_computation.6 | async-start | bytes 4718592 | tf_op jit(solution)/shard_map/all_gather | solution.py:679
  11.9 141.0 %collective-permute-start.15 = (bf16[256,1024]{1,0:T(8,128)(2,1)}, bf16[256,1024]{1,0:T(8,128)(2,1)}, u32[]{:S(2)}, u32[]{:S(2)}) collective-permute-start(bf16[256,1024]{1,0:T(8,128)(2,1)} %bitcast.334), channel_id=1, source_target_pairs={{0,8},{8,0},{1,9},{9,1},{2,10},{10,2},{3,11},{11,3},{4,12},{12,4},... | collective-permute-start | bytes 1572872 | tf_op jit(solution)/shard_map/ppermute | solution.py:55
  13.5 40.6 %collective-permute-start.1 = (bf16[256,1024]{1,0:T(8,128)(2,1)}, bf16[256,1024]{1,0:T(8,128)(2,1)S(1)}, u32[]{:S(2)}, u32[]{:S(2)}) collective-permute-start(bf16[256,1024]{1,0:T(8,128)(2,1)} %bitcast.321), channel_id=1, source_target_pairs={{0,8},{8,0},{1,9},{9,1},{2,10},{10,2},{3,11},{11,3},{4,12},{12,4},... | collective-permute-start | bytes 1572872 | tf_op jit(solution)/shard_map/ppermute | solution.py:55
  45.8 18.0 %collective-permute-start.8 = (bf16[1,2,2,2,2,40,512]{6,5,4,3,2,1,0:T(8,128)(2,1)}, bf16[1,2,2,2,2,40,512]{6,5,4,3,2,1,0:T(8,128)(2,1)}, u32[]{:S(2)}, u32[]{:S(2)}) collective-permute-start(bf16[1,2,2,2,2,40,512]{6,5,4,3,2,1,0:T(8,128)(2,1)} %constant_dynamic-slice_fusion.30), channel_id=1, source_target_pairs={{0,16},{16,0},{1,17},{17,1},{2,18},{18,2},{3,19},{19,3},{4,20},{20... | collective-permute-start | bytes 1966088 | tf_op jit(solution)/shard_map/ppermute | solution.py:64
  50.6 99.6 %collective-permute-start.16 = (bf16[256,1024]{1,0:T(8,128)(2,1)}, bf16[256,1024]{1,0:T(8,128)(2,1)}, u32[]{:S(2)}, u32[]{:S(2)}) collective-permute-start(bf16[256,1024]{1,0:T(8,128)(2,1)} %bitcast.335), channel_id=1, source_target_pairs={{0,16},{16,0},{1,17},{17,1},{2,18},{18,2},{3,19},{19,3},{4,20},{20... | collective-permute-start | bytes 1572872 | tf_op jit(solution)/shard_map/ppermute | solution.py:64
  76.7 40.9 %all-to-all-start = ((bf16[8,128,512]{2,1,0:T(8,128)(2,1)}), bf16[8,128,512]{2,1,0:T(8,128)(2,1)}, u32[]{:S(2)}, u32[]{:S(2)}) async-start(bf16[8,128,512]{2,1,0:T(8,128)(2,1)} %bitcast.52), calls=%async_computation | async-start | bytes 2097152 | tf_op jit(solution)/shard_map/all_to_all | solution.py:139
  93.7 19.9 %collective-permute-start.14 = (bf16[1,2,1,2,32,1024]{5,4,3,2,1,0:T(8,128)(2,1)}, bf16[1,2,1,2,32,1024]{5,4,3,2,1,0:T(8,128)(2,1)}, u32[]{:S(2)}, u32[]{:S(2)}) collective-permute-start(bf16[1,2,1,2,32,1024]{5,4,3,2,1,0:T(8,128)(2,1)} %constant_dynamic-slice_fusion.24), channel_id=1, source_target_pairs={{0,2},{1,3},{2,0},{3,1},{4,6},{5,7},{6,4},{7,5},{8,10},{9,11},{10,... | collective-permute-start | bytes 786440 | tf_op jit(solution)/shard_map/ppermute | solution.py:64
  145.1 23.6 %all-to-all-start.1 = ((bf16[8,128,256]{2,1,0:T(8,128)(2,1)}), bf16[8,128,256]{2,1,0:T(8,128)(2,1)S(1)}, u32[]{:S(2)}, u32[]{:S(2)}) async-start(bf16[8,128,256]{2,1,0:T(8,128)(2,1)} %bitcast.368), calls=%async_computation.1 | async-start | bytes 1048576 | tf_op jit(solution)/shard_map/all_to_all | solution.py:139
  151.4 14.4 %collective-permute-start.18 = (bf16[1,2,2,2,32,1024]{5,4,3,2,1,0:T(8,128)(2,1)S(1)}, bf16[1,2,2,2,32,1024]{5,4,3,2,1,0:T(8,128)(2,1)S(1)}, u32[]{:S(2)}, u32[]{:S(2)}) collective-permute-start(bf16[1,2,2,2,32,1024]{5,4,3,2,1,0:T(8,128)(2,1)S(1)} %constant_dynamic-slice_fusion.23), channel_id=1, source_target_pairs={{0,16},{16,0},{1,17},{17,1},{2,18},{18,2},{3,19},{19,3},{4,20},{20... | collective-permute-start | bytes 1572872 | tf_op jit(solution)/shard_map/ppermute | solution.py:64
  184.5 14.0 %collective-permute-start.20 = (bf16[256,1024]{1,0:T(8,128)(2,1)S(1)}, bf16[256,1024]{1,0:T(8,128)(2,1)S(1)}, u32[]{:S(2)}, u32[]{:S(2)}) collective-permute-start(bf16[256,1024]{1,0:T(8,128)(2,1)S(1)} %add_convert_fusion.1), channel_id=1, source_target_pairs={{0,16},{16,0},{1,17},{17,1},{2,18},{18,2},{3,19},{19,3},{4,20},{20... | collective-permute-start | bytes 1572872 | tf_op jit(solution)/shard_map/ppermute | solution.py:64
  207.0 18.3 %collective-permute-start.26 = (f32[256,1024]{1,0:T(8,128)}, f32[256,1024]{1,0:T(8,128)}, u32[]{:S(2)}, u32[]{:S(2)}) collective-permute-start(f32[256,1024]{1,0:T(8,128)} %slice.301), channel_id=1, source_target_pairs={{0,8},{8,0},{1,9},{9,1},{2,10},{10,2},{3,11},{11,3},{4,12},{12,4},... | collective-permute-start | bytes 3145736 | tf_op jit(solution)/shard_map/ppermute | solution.py:55
  211.0 14.3 %collective-permute-start.28 = (bf16[256,1024]{1,0:T(8,128)(2,1)}, bf16[256,1024]{1,0:T(8,128)(2,1)}, u32[]{:S(2)}, u32[]{:S(2)}) collective-permute-start(bf16[256,1024]{1,0:T(8,128)(2,1)} %fusion.40), channel_id=1, source_target_pairs={{0,16},{16,0},{1,17},{17,1},{2,18},{18,2},{3,19},{19,3},{4,20},{20... | collective-permute-start | bytes 1572872 | tf_op jit(solution)/shard_map/ppermute | solution.py:64
  234.1 23.6 %all-to-all-start.2 = ((bf16[8,128,256]{2,1,0:T(8,128)(2,1)}), bf16[8,128,256]{2,1,0:T(8,128)(2,1)}, u32[]{:S(2)}, u32[]{:S(2)}) async-start(bf16[8,128,256]{2,1,0:T(8,128)(2,1)} %bitcast.93), calls=%async_computation.2 | async-start | bytes 1048576 | tf_op jit(solution)/shard_map/all_to_all | solution.py:139
  238.3 117.4 %reduce-scatter.2.cloned.1.call-start = ((), (), s32[]{:S(2)}) async-start(), calls=%async_computation.5 | async-start | bytes 4718592 | tf_op jit(solution)/shard_map/reduce_scatter | solution.py:831
  241.3 14.3 %collective-permute-start.30 = (bf16[2,2,2,32,1024]{4,3,0,1,2:T(8,128)(2,1)}, bf16[2,2,2,32,1024]{4,3,0,1,2:T(8,128)(2,1)}, u32[]{:S(2)}, u32[]{:S(2)}) collective-permute-start(bf16[2,2,2,32,1024]{4,3,0,1,2:T(8,128)(2,1)} %fusion.52), channel_id=1, source_target_pairs={{0,16},{16,0},{1,17},{17,1},{2,18},{18,2},{3,19},{19,3},{4,20},{20... | collective-permute-start | bytes 1572872 | tf_op jit(solution)/shard_map/ppermute | solution.py:64
  258.8 35.8 %collective-permute-start.31 = (bf16[2,2,32,1024]{3,2,0,1:T(8,128)(2,1)S(1)}, bf16[2,2,32,1024]{3,2,0,1:T(8,128)(2,1)S(1)}, u32[]{:S(2)}, u32[]{:S(2)}) collective-permute-start(bf16[2,2,32,1024]{3,2,0,1:T(8,128)(2,1)S(1)} %fusion.55), channel_id=1, source_target_pairs={{0,1},{1,0},{2,3},{3,2},{4,5},{5,4},{6,7},{7,6},{8,9},{9,8},{10,11... | collective-permute-start | bytes 786440 | tf_op jit(solution)/shard_map/ppermute | solution.py:64
  294.6 30.2 %all-to-all-start.3 = ((bf16[8,128,512]{2,1,0:T(8,128)(2,1)}), bf16[8,128,512]{2,1,0:T(8,128)(2,1)S(1)}, u32[]{:S(2)}, u32[]{:S(2)}) async-start(bf16[8,128,512]{2,1,0:T(8,128)(2,1)} %bitcast.357), calls=%async_computation.3 | async-start | bytes 2097152 | tf_op jit(solution)/shard_map/all_to_all | solution.py:139
  307.9 27.6 %collective-permute-start.22 = (f32[256,1024]{1,0:T(8,128)}, f32[256,1024]{1,0:T(8,128)}, u32[]{:S(2)}, u32[]{:S(2)}) collective-permute-start(f32[256,1024]{1,0:T(8,128)} %slice.296), channel_id=1, source_target_pairs={{0,8},{8,0},{1,9},{9,1},{2,10},{10,2},{3,11},{11,3},{4,12},{12,4},... | collective-permute-start | bytes 3145736 | tf_op jit(solution)/shard_map/ppermute | solution.py:55
  314.4 21.1 %collective-permute-start.25 = (bf16[256,1024]{1,0:T(8,128)(2,1)}, bf16[256,1024]{1,0:T(8,128)(2,1)}, u32[]{:S(2)}, u32[]{:S(2)}) collective-permute-start(bf16[256,1024]{1,0:T(8,128)(2,1)} %fusion.41), channel_id=1, source_target_pairs={{0,16},{16,0},{1,17},{17,1},{2,18},{18,2},{3,19},{19,3},{4,20},{20... | collective-permute-start | bytes 1572872 | tf_op jit(solution)/shard_map/ppermute | solution.py:64
  329.6 14.2 %collective-permute-start.33 = (bf16[2,2,2,2,32,512]{5,4,0,1,2,3:T(8,128)(2,1)S(1)}, bf16[2,2,2,2,32,512]{5,4,0,1,2,3:T(8,128)(2,1)}, u32[]{:S(2)}, u32[]{:S(2)}) collective-permute-start(bf16[2,2,2,2,32,512]{5,4,0,1,2,3:T(8,128)(2,1)S(1)} %fusion.53), channel_id=1, source_target_pairs={{0,16},{16,0},{1,17},{17,1},{2,18},{18,2},{3,19},{19,3},{4,20},{20... | collective-permute-start | bytes 1572872 | tf_op jit(solution)/shard_map/ppermute | solution.py:64
  332.8 13.7 %collective-permute-start.34 = (bf16[2,2,2,2,32,512]{5,4,1,2,3,0:T(8,128)(2,1)}, bf16[2,2,2,2,32,512]{5,4,1,2,3,0:T(8,128)(2,1)}, u32[]{:S(2)}, u32[]{:S(2)}) collective-permute-start(bf16[2,2,2,2,32,512]{5,4,1,2,3,0:T(8,128)(2,1)} %fusion.54), channel_id=1, source_target_pairs={{0,1},{1,0},{2,3},{3,2},{4,5},{5,4},{6,7},{7,6},{8,9},{9,8},{10,11... | collective-permute-start | bytes 1572872 | tf_op jit(solution)/shard_map/ppermute | solution.py:64
  335.4 13.7 %collective-permute-start.38 = (f32[256,1024]{1,0:T(8,128)}, f32[256,1024]{1,0:T(8,128)}, u32[]{:S(2)}, u32[]{:S(2)}) collective-permute-start(f32[256,1024]{1,0:T(8,128)} %slice.371), channel_id=1, source_target_pairs={{0,8},{8,0},{1,9},{9,1},{2,10},{10,2},{3,11},{11,3},{4,12},{12,4},... | collective-permute-start | bytes 3145736 | tf_op jit(solution)/shard_map/ppermute | solution.py:55
  367.1 13.9 %collective-permute-start.44 = (bf16[2,2,32,512]{3,2,0,1:T(8,128)(2,1)S(1)}, bf16[2,2,32,512]{3,2,0,1:T(8,128)(2,1)S(1)}, u32[]{:S(2)}, u32[]{:S(2)}) collective-permute-start(bf16[2,2,32,512]{3,2,0,1:T(8,128)(2,1)S(1)} %fusion.61), channel_id=1, source_target_pairs={{0,2},{1,3},{2,0},{3,1},{4,6},{5,7},{6,4},{7,5},{8,10},{9,11},{10,... | collective-permute-start | bytes 393224 | tf_op jit(solution)/shard_map/ppermute | solution.py:64
  368.9 12.1 %collective-permute-start.45 = (bf16[2,2,32,512]{3,2,0,1:T(8,128)(2,1)S(1)}, bf16[2,2,32,512]{3,2,0,1:T(8,128)(2,1)S(1)}, u32[]{:S(2)}, u32[]{:S(2)}) collective-permute-start(bf16[2,2,32,512]{3,2,0,1:T(8,128)(2,1)S(1)} %fusion.62), channel_id=1, source_target_pairs={{0,2},{1,3},{2,0},{3,1},{4,6},{5,7},{6,4},{7,5},{8,10},{9,11},{10,... | collective-permute-start | bytes 393224 | tf_op jit(solution)/shard_map/ppermute | solution.py:64
  (75 other events, 743.3 us)
Sparse Core Ops, SparseCore 0:
  66.2 96.8 all-gather.2
  242.9 101.9 reduce-scatter.1

commit v6 on v5

--- a/solution.py
+++ b/solution.py
@@ -650,10 +650,7 @@
     for k in range(len(seq_steps) + len(chip_steps)):
         for pair, chain in enumerate(chains):
             chain.step(gather_orders[pair % 2][k])
-        later = [Held(w_inner)] if k == 0 else []
-        together(chains + later)
-        if later:
-            w_inner = later[0].held
+        together(chains)
     small = chains[0].held.reshape(-1, shard + extra, 2 * width)[:, shard:]
     small = jnp.concatenate([small[:, :, k * tok : (k + 1) * tok] for k in range(fold)], 1)
     joined = [chains[0].held.reshape(-1, shard + extra, 2 * width)[:, :shard]]

time: 408 us -> 410 us (level)
  transfers between devices with their start and end apart: 57 -> 57, of which waited for: 28 -> 27; matrix products, arithmetic and copies ran while one was open for 28% -> 28% of each run, Pallas kernels for 15% -> 15%
where the time goes in v6:
time: 410 us; the launch traced here: 402 us
  waiting for transfers between devices  109 us (27%)
  starting transfers between devices  66.3 us (16%)
  local copies, waits for them, and re-layouts  66.2 us (16%)
  Pallas kernels  61.1 us (15%)
  other arithmetic  53.2 us (13%)
  matrix products  31.5 us (8%)
  between operations  15.7 us (4%)
    ppermute x35, waiting for transfers between devices, exchange(): return lax.ppermute(block, axis, [(i, i ^ bit) for i in range(size)])  89.2 us
    ppermute x35, starting transfers between devices, exchange(): return lax.ppermute(block, axis, [(i, i ^ bit) for i in range(size)])  46.5 us
    pallas_call x1, Pallas kernels, attention_backward(): pl.pallas_call(functools.partial(backward_kernel, heads, mixing), grid=(r...  33.5 us
    pallas_call x1, Pallas kernels, attention_forward(): pl.pallas_call(functools.partial(forward_kernel, heads, mixing), grid=(ro...  27.6 us
    all_to_all x4, starting transfers between devices, all_to_all(): return lax.all_to_all(block, 'seq', split_axis=0, concat_axis=0, tiled=True)  17.5 us
    all_to_all x4, waiting for transfers between devices, all_to_all(): return lax.all_to_all(block, 'seq', split_axis=0, concat_axis=0, tiled=True)  12.8 us
    dot_general x7, matrix products, matmul(): return jnp.dot(left, right, preferred_element_type=F32)  11.7 us
    dot_general x7, matrix products, matmul_right(): lax.dot_general(left, right, (((1,), (1,)), ((), ())), preferred_element_...  11.4 us
  transfers between devices with their start and end apart: 57, of which 27 were waited for; matrix products, arithmetic and copies ran while one was open for 28% of the time, Pallas kernels for 15%

profile of v6, /device:TPU:0, one launch (start us, length us, event | category | flops | bytes accessed | tf_op | source)
XLA Modules:
  0.0 402.5 jit_solution(16627779343214023129)
XLA Ops:
  18.1 2.9 collective-permute-start.2
  22.2 3.2 collective-permute-done.2
  29.3 5.8 %collective-permute-done.5 = bf16[2,2,1,1,1,32,512]{6,5,4,3,2,1,0:T(8,128)(2,1)} collective-permute-done((bf16[2,2,1,1,1,32,512]{6,5,4,3,2,1,0:T(8,128)(2,1)}, bf16[2,2,1,1,1,32,512]{6,5,4,3,2,1,0:T(8,128)(2,1)}, u32[]{:S(2)}, u32[]{:S(2)}) %collective-permute-start.5) | collective-permute-done | bytes 131104 | tf_op jit(solution)/shard_map/ppermute | solution.py:64
  55.4 5.5 %collective-permute-done.9 = bf16[2,2,2,1,2,32,512]{6,5,4,3,2,1,0:T(8,128)(2,1)} collective-permute-done((bf16[2,2,2,1,2,32,512]{6,5,4,3,2,1,0:T(8,128)(2,1)}, bf16[2,2,2,1,2,32,512]{6,5,4,3,2,1,0:T(8,128)(2,1)}, u32[]{:S(2)}, u32[]{:S(2)}) %collective-permute-start.9) | collective-permute-done | bytes 524320 | tf_op jit(solution)/shard_map/ppermute | solution.py:64
  62.0 3.0 collective-permute-done.8
  68.2 3.1 fusion
  78.9 4.4 %all-to-all-start = ((bf16[8,128,512]{2,1,0:T(8,128)(2,1)}), bf16[8,128,512]{2,1,0:T(8,128)(2,1)}, u32[]{:S(2)}, u32[]{:S(2)}) async-start(bf16[8,128,512]{2,1,0:T(8,128)(2,1)} %bitcast.52), calls=%async_computation | async-start | bytes 2097152 | tf_op jit(solution)/shard_map/all_to_all | solution.py:139
  87.9 3.8 select_reduce_fusion
  102.2 14.6 %collective-permute-done.14 = bf16[1,2,1,2,32,1024]{5,4,3,2,1,0:T(8,128)(2,1)} collective-permute-done((bf16[1,2,1,2,32,1024]{5,4,3,2,1,0:T(8,128)(2,1)}, bf16[1,2,1,2,32,1024]{5,4,3,2,1,0:T(8,128)(2,1)}, u32[]{:S(2)}, u32[]{:S(2)}) %collective-permute-start.14) | collective-permute-done | bytes 262176 | tf_op jit(solution)/shard_map/ppermute | solution.py:64
  120.6 27.6 %shard_map.280 = (bf16[4,1024,256]{2,1,0:T(8,128)(2,1)}, f32[4,1024,128]{2,1,0:T(8,128)}, bf16[1024,256]{1,0:T(8,128)(2,1)}, bf16[4,1600,768]{2,1,0:T(8,128)(2,1)}, f32[4,12,8,128]{3,2,1,0:T(8,128)}) custom-call(bf16[1024,512]{1,0:T(8,128)(2,1)} %bitcast.53.qv_ref, s32[4,1,1024]{2,1,0:T(1,128)} %bitcast.374, s32[4,1024,1]{2,1,0:T(8,128)} %copy.212.column_ref, ...), custom_call_target="tpu_custom_call" | custom-call | flops 12482248704 | bytes 20971520 | tf_op jit(solution)/shard_map/pallas_call | solution.py:501
  148.2 4.1 %all-to-all-start.1 = ((bf16[8,128,256]{2,1,0:T(8,128)(2,1)}), bf16[8,128,256]{2,1,0:T(8,128)(2,1)S(1)}, u32[]{:S(2)}, u32[]{:S(2)}) async-start(bf16[8,128,256]{2,1,0:T(8,128)(2,1)} %bitcast.365), calls=%async_computation.1 | async-start | bytes 1048576 | tf_op jit(solution)/shard_map/all_to_all | solution.py:139
  158.4 9.5 %collective-permute-done.18 = bf16[1,2,2,2,32,1024]{5,4,3,2,1,0:T(8,128)(2,1)S(1)} collective-permute-done((bf16[1,2,2,2,32,1024]{5,4,3,2,1,0:T(8,128)(2,1)S(1)}, bf16[1,2,2,2,32,1024]{5,4,3,2,1,0:T(8,128)(2,1)S(1)}, u32[]{:S(2)}, u32[]{:S(2)}) %collective-permute-start.18) | collective-permute-done | bytes 524320 | tf_op jit(solution)/shard_map/ppermute | solution.py:64
  168.7 3.3 all-to-all-done.1
  172.2 4.3 %fusion.104 = (bf16[8,128,1024]{2,1,0:T(8,128)(2,1)}, bf16[8,128,1024]{2,1,0:T(8,128)(2,1)S(1)}) fusion(bf16[8,256,1024]{2,1,0:T(8,128)(2,1)} %bitcast.338), kind=kLoop, calls=%fused_computation.318 | loop fusion | bytes 8388608 | tf_op jit(solution)/shard_map/slice | solution.py:677
  197.0 4.8 %collective-permute-done.20 = bf16[256,1024]{1,0:T(8,128)(2,1)S(1)} collective-permute-done((bf16[256,1024]{1,0:T(8,128)(2,1)S(1)}, bf16[256,1024]{1,0:T(8,128)(2,1)S(1)}, u32[]{:S(2)}, u32[]{:S(2)}) %collective-permute-start.20) | collective-permute-done | bytes 524320 | tf_op jit(solution)/shard_map/ppermute | solution.py:64
  220.7 8.0 %collective-permute-done.28 = bf16[256,1024]{1,0:T(8,128)(2,1)} collective-permute-done((bf16[256,1024]{1,0:T(8,128)(2,1)}, bf16[256,1024]{1,0:T(8,128)(2,1)}, u32[]{:S(2)}, u32[]{:S(2)}) %collective-permute-start.28) | collective-permute-done | bytes 524320 | tf_op jit(solution)/shard_map/ppermute | solution.py:64
  237.5 4.1 %all-to-all-start.2 = ((bf16[8,128,256]{2,1,0:T(8,128)(2,1)}), bf16[8,128,256]{2,1,0:T(8,128)(2,1)}, u32[]{:S(2)}, u32[]{:S(2)}) async-start(bf16[8,128,256]{2,1,0:T(8,128)(2,1)} %bitcast.93), calls=%async_computation.2 | async-start | bytes 1048576 | tf_op jit(solution)/shard_map/all_to_all | solution.py:139
  246.1 12.9 %collective-permute-done.30 = bf16[2,2,2,32,1024]{4,3,0,1,2:T(8,128)(2,1)} collective-permute-done((bf16[2,2,2,32,1024]{4,3,0,1,2:T(8,128)(2,1)}, bf16[2,2,2,32,1024]{4,3,0,1,2:T(8,128)(2,1)}, u32[]{:S(2)}, u32[]{:S(2)}) %collective-permute-start.30) | collective-permute-done | bytes 524320 | tf_op jit(solution)/shard_map/ppermute | solution.py:64
  264.4 33.5 %shard_map.281 = bf16[1024,512]{1,0:T(8,128)(2,1)} custom-call(bf16[1024,256]{1,0:T(8,128)(2,1)} %bitcast.94.d_mixed_ref, bf16[4,1024,256]{2,1,0:T(8,128)(2,1)} %get-tuple-element.102.out_ref, f32[4,1024,128]{2,1,0:T(8,128)} %get-tuple-element.103.weight_ref, f32[8,128]{1,0:T(8,128)} %broadcast_in_dim.92.dot_ref, ...), custom_call_target="tpu_custom_call" | custom-call | flops 14294188032 | bytes 20971520 | tf_op jit(solution)/shard_map/pallas_call | solution.py:527
  298.0 4.8 %all-to-all-start.3 = ((bf16[8,128,512]{2,1,0:T(8,128)(2,1)}), bf16[8,128,512]{2,1,0:T(8,128)(2,1)S(1)}, u32[]{:S(2)}, u32[]{:S(2)}) async-start(bf16[8,128,512]{2,1,0:T(8,128)(2,1)} %bitcast.354), calls=%async_computation.3 | async-start | bytes 2097152 | tf_op jit(solution)/shard_map/all_to_all | solution.py:139
  302.8 3.2 fusion.114
  321.7 7.4 %all-to-all-done.3 = bf16[8,128,512]{2,1,0:T(8,128)(2,1)S(1)} async-done(((bf16[8,128,512]{2,1,0:T(8,128)(2,1)}), bf16[8,128,512]{2,1,0:T(8,128)(2,1)S(1)}, u32[]{:S(2)}, u32[]{:S(2)}) %all-to-all-start.3) | async-done | bytes 1048608 | tf_op jit(solution)/shard_map/all_to_all | solution.py:139
  340.8 5.0 %collective-permute-done.35 = bf16[32,1024]{1,0:T(8,128)(2,1)S(1)} collective-permute-done((bf16[32,1024]{1,0:T(8,128)(2,1)S(1)}, bf16[32,1024]{1,0:T(8,128)(2,1)S(1)}, u32[]{:S(2)}, u32[]{:S(2)}) %collective-permute-start.35) | collective-permute-done | bytes 65568 | tf_op jit(solution)/shard_map/ppermute | solution.py:64
  346.4 2.7 bitcast_add_fusion.1
  (400 shorter events, 205.2 us)
Async XLA Ops:
  7.2 165.0 %all-gather.3.cloned.1.call-start = ((), (), s32[]{:S(2)}) async-start(), calls=%async_computation.6 | async-start | bytes 4718592 | tf_op jit(solution)/shard_map/all_gather | solution.py:676
  13.9 25.8 %collective-permute-start.10 = (bf16[2,32,1024]{2,0,1:T(2,128)(2,1)}, bf16[2,32,1024]{2,0,1:T(2,128)(2,1)}, u32[]{:S(2)}, u32[]{:S(2)}) collective-permute-start(bf16[2,32,1024]{2,0,1:T(2,128)(2,1)} %get-tuple-element.174), channel_id=1, source_target_pairs={{0,16},{16,0},{1,17},{17,1},{2,18},{18,2},{3,19},{19,3},{4,20},{20... | collective-permute-start | bytes 393224 | tf_op jit(solution)/shard_map/ppermute | solution.py:64
  16.4 138.6 %collective-permute-start.15 = (bf16[256,1024]{1,0:T(8,128)(2,1)}, bf16[256,1024]{1,0:T(8,128)(2,1)}, u32[]{:S(2)}, u32[]{:S(2)}) collective-permute-start(bf16[256,1024]{1,0:T(8,128)(2,1)} %bitcast.72), channel_id=1, source_target_pairs={{0,8},{8,0},{1,9},{9,1},{2,10},{10,2},{3,11},{11,3},{4,12},{12,4},... | collective-permute-start | bytes 1572872 | tf_op jit(solution)/shard_map/ppermute | solution.py:55
  29.3 26.0 %collective-permute-start.1 = (bf16[256,1024]{1,0:T(8,128)(2,1)S(1)}, bf16[256,1024]{1,0:T(8,128)(2,1)S(1)}, u32[]{:S(2)}, u32[]{:S(2)}) collective-permute-start(bf16[256,1024]{1,0:T(8,128)(2,1)S(1)} %bitcast.322), channel_id=1, source_target_pairs={{0,8},{8,0},{1,9},{9,1},{2,10},{10,2},{3,11},{11,3},{4,12},{12,4},... | collective-permute-start | bytes 1572872 | tf_op jit(solution)/shard_map/ppermute | solution.py:55
  47.0 18.0 %collective-permute-start.8 = (bf16[1,2,2,2,2,40,512]{6,5,4,3,2,1,0:T(8,128)(2,1)}, bf16[1,2,2,2,2,40,512]{6,5,4,3,2,1,0:T(8,128)(2,1)}, u32[]{:S(2)}, u32[]{:S(2)}) collective-permute-start(bf16[1,2,2,2,2,40,512]{6,5,4,3,2,1,0:T(8,128)(2,1)} %constant_dynamic-slice_fusion.30), channel_id=1, source_target_pairs={{0,16},{16,0},{1,17},{17,1},{2,18},{18,2},{3,19},{19,3},{4,20},{20... | collective-permute-start | bytes 1966088 | tf_op jit(solution)/shard_map/ppermute | solution.py:64
  52.8 99.5 %collective-permute-start.16 = (bf16[256,1024]{1,0:T(8,128)(2,1)}, bf16[256,1024]{1,0:T(8,128)(2,1)}, u32[]{:S(2)}, u32[]{:S(2)}) collective-permute-start(bf16[256,1024]{1,0:T(8,128)(2,1)} %bitcast.72), channel_id=1, source_target_pairs={{0,16},{16,0},{1,17},{17,1},{2,18},{18,2},{3,19},{19,3},{4,20},{20... | collective-permute-start | bytes 1572872 | tf_op jit(solution)/shard_map/ppermute | solution.py:64
  78.9 41.7 %all-to-all-start = ((bf16[8,128,512]{2,1,0:T(8,128)(2,1)}), bf16[8,128,512]{2,1,0:T(8,128)(2,1)}, u32[]{:S(2)}, u32[]{:S(2)}) async-start(bf16[8,128,512]{2,1,0:T(8,128)(2,1)} %bitcast.52), calls=%async_computation | async-start | bytes 2097152 | tf_op jit(solution)/shard_map/all_to_all | solution.py:139
  94.6 22.2 %collective-permute-start.14 = (bf16[1,2,1,2,32,1024]{5,4,3,2,1,0:T(8,128)(2,1)}, bf16[1,2,1,2,32,1024]{5,4,3,2,1,0:T(8,128)(2,1)}, u32[]{:S(2)}, u32[]{:S(2)}) collective-permute-start(bf16[1,2,1,2,32,1024]{5,4,3,2,1,0:T(8,128)(2,1)} %constant_dynamic-slice_fusion.24), channel_id=1, source_target_pairs={{0,2},{1,3},{2,0},{3,1},{4,6},{5,7},{6,4},{7,5},{8,10},{9,11},{10,... | collective-permute-start | bytes 786440 | tf_op jit(solution)/shard_map/ppermute | solution.py:64
  148.2 23.8 %all-to-all-start.1 = ((bf16[8,128,256]{2,1,0:T(8,128)(2,1)}), bf16[8,128,256]{2,1,0:T(8,128)(2,1)S(1)}, u32[]{:S(2)}, u32[]{:S(2)}) async-start(bf16[8,128,256]{2,1,0:T(8,128)(2,1)} %bitcast.365), calls=%async_computation.1 | async-start | bytes 1048576 | tf_op jit(solution)/shard_map/all_to_all | solution.py:139
  153.5 14.4 %collective-permute-start.18 = (bf16[1,2,2,2,32,1024]{5,4,3,2,1,0:T(8,128)(2,1)S(1)}, bf16[1,2,2,2,32,1024]{5,4,3,2,1,0:T(8,128)(2,1)S(1)}, u32[]{:S(2)}, u32[]{:S(2)}) collective-permute-start(bf16[1,2,2,2,32,1024]{5,4,3,2,1,0:T(8,128)(2,1)S(1)} %constant_dynamic-slice_fusion.23), channel_id=1, source_target_pairs={{0,16},{16,0},{1,17},{17,1},{2,18},{18,2},{3,19},{19,3},{4,20},{20... | collective-permute-start | bytes 1572872 | tf_op jit(solution)/shard_map/ppermute | solution.py:64
  187.9 14.0 %collective-permute-start.20 = (bf16[256,1024]{1,0:T(8,128)(2,1)S(1)}, bf16[256,1024]{1,0:T(8,128)(2,1)S(1)}, u32[]{:S(2)}, u32[]{:S(2)}) collective-permute-start(bf16[256,1024]{1,0:T(8,128)(2,1)S(1)} %add_convert_fusion.1), channel_id=1, source_target_pairs={{0,16},{16,0},{1,17},{17,1},{2,18},{18,2},{3,19},{19,3},{4,20},{20... | collective-permute-start | bytes 1572872 | tf_op jit(solution)/shard_map/ppermute | solution.py:64
  210.4 18.3 %collective-permute-start.26 = (f32[256,1024]{1,0:T(8,128)}, f32[256,1024]{1,0:T(8,128)}, u32[]{:S(2)}, u32[]{:S(2)}) collective-permute-start(f32[256,1024]{1,0:T(8,128)} %slice.301), channel_id=1, source_target_pairs={{0,8},{8,0},{1,9},{9,1},{2,10},{10,2},{3,11},{11,3},{4,12},{12,4},... | collective-permute-start | bytes 3145736 | tf_op jit(solution)/shard_map/ppermute | solution.py:55
  214.4 14.3 %collective-permute-start.28 = (bf16[256,1024]{1,0:T(8,128)(2,1)}, bf16[256,1024]{1,0:T(8,128)(2,1)}, u32[]{:S(2)}, u32[]{:S(2)}) collective-permute-start(bf16[256,1024]{1,0:T(8,128)(2,1)} %fusion.40), channel_id=1, source_target_pairs={{0,16},{16,0},{1,17},{17,1},{2,18},{18,2},{3,19},{19,3},{4,20},{20... | collective-permute-start | bytes 1572872 | tf_op jit(solution)/shard_map/ppermute | solution.py:64
  237.5 23.6 %all-to-all-start.2 = ((bf16[8,128,256]{2,1,0:T(8,128)(2,1)}), bf16[8,128,256]{2,1,0:T(8,128)(2,1)}, u32[]{:S(2)}, u32[]{:S(2)}) async-start(bf16[8,128,256]{2,1,0:T(8,128)(2,1)} %bitcast.93), calls=%async_computation.2 | async-start | bytes 1048576 | tf_op jit(solution)/shard_map/all_to_all | solution.py:139
  241.6 114.8 %reduce-scatter.2.cloned.1.call-start = ((), (), s32[]{:S(2)}) async-start(), calls=%async_computation.5 | async-start | bytes 4718592 | tf_op jit(solution)/shard_map/reduce_scatter | solution.py:828
  244.7 14.3 %collective-permute-start.30 = (bf16[2,2,2,32,1024]{4,3,0,1,2:T(8,128)(2,1)}, bf16[2,2,2,32,1024]{4,3,0,1,2:T(8,128)(2,1)}, u32[]{:S(2)}, u32[]{:S(2)}) collective-permute-start(bf16[2,2,2,32,1024]{4,3,0,1,2:T(8,128)(2,1)} %fusion.52), channel_id=1, source_target_pairs={{0,16},{16,0},{1,17},{17,1},{2,18},{18,2},{3,19},{19,3},{4,20},{20... | collective-permute-start | bytes 1572872 | tf_op jit(solution)/shard_map/ppermute | solution.py:64
  262.2 35.8 %collective-permute-start.31 = (bf16[2,2,32,1024]{3,2,0,1:T(8,128)(2,1)S(1)}, bf16[2,2,32,1024]{3,2,0,1:T(8,128)(2,1)S(1)}, u32[]{:S(2)}, u32[]{:S(2)}) collective-permute-start(bf16[2,2,32,1024]{3,2,0,1:T(8,128)(2,1)S(1)} %fusion.55), channel_id=1, source_target_pairs={{0,1},{1,0},{2,3},{3,2},{4,5},{5,4},{6,7},{7,6},{8,9},{9,8},{10,11... | collective-permute-start | bytes 786440 | tf_op jit(solution)/shard_map/ppermute | solution.py:64
  298.0 31.1 %all-to-all-start.3 = ((bf16[8,128,512]{2,1,0:T(8,128)(2,1)}), bf16[8,128,512]{2,1,0:T(8,128)(2,1)S(1)}, u32[]{:S(2)}, u32[]{:S(2)}) async-start(bf16[8,128,512]{2,1,0:T(8,128)(2,1)} %bitcast.354), calls=%async_computation.3 | async-start | bytes 2097152 | tf_op jit(solution)/shard_map/all_to_all | solution.py:139
  312.2 25.1 %collective-permute-start.22 = (f32[256,1024]{1,0:T(8,128)}, f32[256,1024]{1,0:T(8,128)}, u32[]{:S(2)}, u32[]{:S(2)}) collective-permute-start(f32[256,1024]{1,0:T(8,128)} %slice.296), channel_id=1, source_target_pairs={{0,8},{8,0},{1,9},{9,1},{2,10},{10,2},{3,11},{11,3},{4,12},{12,4},... | collective-permute-start | bytes 3145736 | tf_op jit(solution)/shard_map/ppermute | solution.py:55
  318.8 18.5 %collective-permute-start.25 = (bf16[256,1024]{1,0:T(8,128)(2,1)}, bf16[256,1024]{1,0:T(8,128)(2,1)}, u32[]{:S(2)}, u32[]{:S(2)}) collective-permute-start(bf16[256,1024]{1,0:T(8,128)(2,1)} %fusion.41), channel_id=1, source_target_pairs={{0,16},{16,0},{1,17},{17,1},{2,18},{18,2},{3,19},{19,3},{4,20},{20... | collective-permute-start | bytes 1572872 | tf_op jit(solution)/shard_map/ppermute | solution.py:64
  332.0 14.4 %collective-permute-start.33 = (bf16[2,2,2,2,32,512]{5,4,0,1,2,3:T(8,128)(2,1)}, bf16[2,2,2,2,32,512]{5,4,0,1,2,3:T(8,128)(2,1)}, u32[]{:S(2)}, u32[]{:S(2)}) collective-permute-start(bf16[2,2,2,2,32,512]{5,4,0,1,2,3:T(8,128)(2,1)} %fusion.53), channel_id=1, source_target_pairs={{0,16},{16,0},{1,17},{17,1},{2,18},{18,2},{3,19},{19,3},{4,20},{20... | collective-permute-start | bytes 1572872 | tf_op jit(solution)/shard_map/ppermute | solution.py:64
  334.9 14.2 %collective-permute-start.34 = (bf16[2,2,2,2,32,512]{5,4,1,2,3,0:T(8,128)(2,1)}, bf16[2,2,2,2,32,512]{5,4,1,2,3,0:T(8,128)(2,1)}, u32[]{:S(2)}, u32[]{:S(2)}) collective-permute-start(bf16[2,2,2,2,32,512]{5,4,1,2,3,0:T(8,128)(2,1)} %fusion.54), channel_id=1, source_target_pairs={{0,1},{1,0},{2,3},{3,2},{4,5},{5,4},{6,7},{7,6},{8,9},{9,8},{10,11... | collective-permute-start | bytes 1572872 | tf_op jit(solution)/shard_map/ppermute | solution.py:64
  337.3 14.4 %collective-permute-start.38 = (f32[256,1024]{1,0:T(8,128)}, f32[256,1024]{1,0:T(8,128)S(1)}, u32[]{:S(2)}, u32[]{:S(2)}) collective-permute-start(f32[256,1024]{1,0:T(8,128)} %slice.371), channel_id=1, source_target_pairs={{0,8},{8,0},{1,9},{9,1},{2,10},{10,2},{3,11},{11,3},{4,12},{12,4},... | collective-permute-start | bytes 3145736 | tf_op jit(solution)/shard_map/ppermute | solution.py:55
  368.8 13.9 %collective-permute-start.44 = (bf16[2,2,32,512]{3,2,0,1:T(8,128)(2,1)S(1)}, bf16[2,2,32,512]{3,2,0,1:T(8,128)(2,1)S(1)}, u32[]{:S(2)}, u32[]{:S(2)}) collective-permute-start(bf16[2,2,32,512]{3,2,0,1:T(8,128)(2,1)S(1)} %fusion.61), channel_id=1, source_target_pairs={{0,2},{1,3},{2,0},{3,1},{4,6},{5,7},{6,4},{7,5},{8,10},{9,11},{10,... | collective-permute-start | bytes 393224 | tf_op jit(solution)/shard_map/ppermute | solution.py:64
  (71 other events, 722.4 us)
Sparse Core Ops, SparseCore 0:
  67.4 99.9 all-gather.2
  246.2 101.9 reduce-scatter.1
